TPU v7x, 32 devices: a whole 2x2x4 slice. The times are simulated.
32 devices in a mesh: seq: 8 (over z, x), ch: 4 (over y, core).
Axes of the slice: x: 2, y: 2, z: 4, core: 2. Of those that a mesh axis runs over, the one named last changes fastest.
Arguments:
- value_proj: bfloat16 [3072, 512], P('seq', 'ch'), may hold values from -6 to 6
- gate_in: bfloat16 [3072, 512], P('seq', 'ch'), may hold values from -6 to 6
- gate_out: bfloat16 [3072, 512], P('seq', 'ch'), may hold values from -6 to 6
- skip_gain: float32 [512], P('ch'), may hold values from -3 to 3
- filter_taps: float32 [1536], replicated, may hold values from -0.15625 to 0.15625
- doc_lengths: int32 [3], replicated, may hold values from 1 to 4, 8 in all
- cotangent: bfloat16 [3072, 512], P('seq', 'ch'), may hold values from -6 to 6
Outputs:
- layer_out: bfloat16 [3072, 512], P('seq', 'ch')
- grad_value: bfloat16 [3072, 512], P('seq', 'ch')
- grad_gate: bfloat16 [3072, 512], P('seq', 'ch')
- filter_grad: float32 [1536], P('seq')
Inputs may be any that keep to these rules, and one draw needn't show every extreme that they name: doc_lengths lists, in order, the lengths in shards of 384 tokens of the 3 documents that fill the sequence; they add up to the number of shards, and the longest is exactly 4.
All inputs are finite; a program needn't handle non-finite values.
Results may differ from a plain program's by a relative error of at most 0.0055.
Values may be sent and summed in bfloat16 or wider, within the bound.
No kernel may reach another device: no remote copies, remote signals or barrier semaphores. Data moves between devices by JAX's collectives and lax.ppermute only.
A program may use at most 64 MiB of HBM per device.

v0:
```python
import math

import jax
import jax.numpy as jnp
from jax import lax
from jax.sharding import PartitionSpec as P


def shifted(value, axis, by):
    length = lax.axis_size(axis)
    pairs = [(i, i + by) for i in range(length) if 0 <= i + by < length]
    return lax.ppermute(value, axis, pairs)


def toeplitz_block(padded_taps, offset, block_rows):
    window = lax.dynamic_slice_in_dim(padded_taps, offset * block_rows + 1, 2 * block_rows - 1)
    tiled_taps = jnp.tile(window, block_rows + 1)
    skewed = tiled_taps[block_rows - 1 : block_rows - 1 + block_rows * (2 * block_rows - 2)]
    return skewed.reshape(block_rows, 2 * block_rows - 2)[:, :block_rows]


def diagonal_sums(product):
    block_rows = product.shape[0]
    widened = jnp.pad(product, ((0, 0), (0, block_rows)))
    skewed = widened.reshape(-1)[: block_rows * (2 * block_rows - 1)]
    return jnp.sum(skewed.reshape(block_rows, 2 * block_rows - 1), axis=0)


def add_lags(lag_sums, offset, diag_sums, block_rows):
    first_lag = offset * block_rows + 1
    current = lax.dynamic_slice_in_dim(lag_sums, first_lag, 2 * block_rows - 1)
    return lax.dynamic_update_slice_in_dim(lag_sums, current + diag_sums, first_lag, 0)


def body(value_proj, gate_in, gate_out, skip_gain, filter_taps, doc_lengths, cotangent):
    block_rows = value_proj.shape[0]
    longest = filter_taps.shape[0] // block_rows
    position = lax.axis_index("seq")
    doc_ends = jnp.cumsum(doc_lengths)
    passed = doc_ends <= position
    doc_start = jnp.sum(jnp.where(passed, doc_lengths, 0))
    doc_end = jnp.min(jnp.where(passed, doc_ends[-1], doc_ends))
    gated = (gate_in.astype(jnp.float32) * value_proj.astype(jnp.float32)).astype(jnp.bfloat16)
    cot_gated = (cotangent.astype(jnp.float32) * gate_out.astype(jnp.float32)).astype(jnp.bfloat16)
    zero_rim = jnp.zeros((block_rows,), jnp.bfloat16)
    padded_taps = jnp.concatenate([zero_rim, filter_taps.astype(jnp.bfloat16), zero_rim])
    contract_rows = (((0,), (0,)), ((), ()))
    contract_cols = (((1,), (1,)), ((), ()))
    diagonal = toeplitz_block(padded_taps, 0, block_rows)
    convolved = lax.dot_general(diagonal, gated, contract_rows, preferred_element_type=jnp.float32)
    transposed = jnp.dot(diagonal, cot_gated, preferred_element_type=jnp.float32)
    lag_sums = jnp.zeros((filter_taps.shape[0] + 2 * block_rows,), jnp.float32)
    own_product = lax.dot_general(
        cot_gated, gated[::-1], contract_cols, preferred_element_type=jnp.float32
    )
    lag_sums = add_lags(lag_sums, 0, diagonal_sums(own_product), block_rows)
    carried = (convolved, lag_sums, transposed)
    moving_up = gated
    moving_down = cot_gated
    for offset in range(1, longest):
        moving_up = shifted(moving_up, "seq", 1)
        moving_down = shifted(moving_down, "seq", -1)
        source_block = moving_up
        later_block = moving_down
        forward_ok = position - offset >= doc_start
        backward_ok = position + offset < doc_end

        def work(carried_state):
            convolved, lag_sums, transposed = carried_state
            toeplitz = toeplitz_block(padded_taps, offset, block_rows)

            def ahead(carried_pair):
                conv_now, lags_now = carried_pair
                conv_now = conv_now + lax.dot_general(
                    toeplitz, source_block, contract_rows, preferred_element_type=jnp.float32
                )
                product = lax.dot_general(
                    cot_gated, source_block[::-1], contract_cols, preferred_element_type=jnp.float32
                )
                lags_now = add_lags(lags_now, offset, diagonal_sums(product), block_rows)
                return (conv_now, lags_now)

            def behind(back_now):
                return back_now + jnp.dot(toeplitz, later_block, preferred_element_type=jnp.float32)

            convolved, lag_sums = lax.cond(
                forward_ok, ahead, lambda carried_pair: carried_pair, (convolved, lag_sums)
            )
            transposed = lax.cond(backward_ok, behind, lambda back_now: back_now, transposed)
            return (convolved, lag_sums, transposed)

        carried = lax.cond(
            jnp.logical_or(forward_ok, backward_ok),
            work,
            lambda carried_state: carried_state,
            carried,
        )
    convolved, lag_sums, transposed = carried
    lag_part = lag_sums[block_rows : block_rows + filter_taps.shape[0]]
    owned_lags = lax.psum_scatter(lag_part, "seq", scatter_dimension=0, tiled=True)
    lag_total = lax.psum(owned_lags, "ch")
    grad_scale = 1.0 / math.sqrt(
        lax.axis_size("seq") * block_rows * value_proj.shape[1] * lax.axis_size("ch")
    )
    skip_row = skip_gain[None, :]
    layer_out = (
        gate_out.astype(jnp.float32) * (convolved + skip_row * gated.astype(jnp.float32))
    ).astype(jnp.bfloat16)
    through = transposed + skip_row * cot_gated.astype(jnp.float32)
    grad_value = (through * gate_in.astype(jnp.float32)).astype(jnp.bfloat16)
    grad_gate = (through * value_proj.astype(jnp.float32)).astype(jnp.bfloat16)
    return (layer_out, grad_value, grad_gate, lag_total * grad_scale)


def solution(mesh):
    placed = (P("seq", "ch"), P("seq", "ch"), P("seq", "ch"), P("ch"), P(), P(), P("seq", "ch"))
    return jax.shard_map(
        body,
        mesh=mesh,
        in_specs=placed,
        out_specs=(P("seq", "ch"), P("seq", "ch"), P("seq", "ch"), P("seq")),
        check_vma=False,
    )
```

profile of v0, /device:TPU:0, one launch (start us, length us, event | category | flops | bytes accessed | tf_op | source)
XLA Modules:
  0.0 83.0 jit_solution(15980257422983567027)
XLA Ops:
  0.6 1.0 %fusion.4 = bf16[384,128]{1,0:T(8,128)(2,1)S(1)} fusion(bf16[384,128]{1,0:T(8,128)(2,1)} %param.27, bf16[384,128]{1,0:T(8,128)(2,1)} %param.31), kind=kLoop, calls=%fused_computation.18 | loop fusion | flops 196608 | bytes 294912 | tf_op jit(solution)/shard_map/convert_element_type | solution.py:44
  1.6 1.3 %collective-permute-start.1 = (bf16[384,128]{1,0:T(8,128)(2,1)S(1)}, bf16[384,128]{1,0:T(8,128)(2,1)S(1)}, u32[]{:S(2)}, u32[]{:S(2)}) collective-permute-start(bf16[384,128]{1,0:T(8,128)(2,1)S(1)} %fusion.4), channel_id=1, source_target_pairs={{4,0},{8,4},{12,8},{16,12},{20,16},{24,20},{28,24},{5,1},{9,5},{13... | collective-permute-start | bytes 294920 | tf_op jit(solution)/shard_map/ppermute | solution.py:12
  2.9 1.0 %fusion.7 = bf16[384,128]{1,0:T(8,128)(2,1)S(1)} fusion(bf16[384,128]{1,0:T(8,128)(2,1)} %param.25, bf16[384,128]{1,0:T(8,128)(2,1)} %param.26), kind=kLoop, calls=%fused_computation.21 | loop fusion | flops 196608 | bytes 294912 | tf_op jit(solution)/shard_map/convert_element_type | solution.py:43
  3.9 5.5 %collective-permute-start = (bf16[384,128]{1,0:T(8,128)(2,1)S(1)}, bf16[384,128]{1,0:T(8,128)(2,1)S(1)}, u32[]{:S(2)}, u32[]{:S(2)}) collective-permute-start(bf16[384,128]{1,0:T(8,128)(2,1)S(1)} %fusion.7), channel_id=1, source_target_pairs={{0,4},{4,8},{8,12},{12,16},{16,20},{20,24},{24,28},{1,5},{5,9},{9,... | collective-permute-start | bytes 294920 | tf_op jit(solution)/shard_map/ppermute | solution.py:12
  9.4 0.1 rev.12
  9.5 0.7 convert_element_type.75
  10.2 0.1 pad_slice_fusion
  10.3 1.1 %tile.27 = bf16[295295]{0:T(1024)(128)(2,1)S(1)} reshape(bf16[385,767]{1,0:T(8,128)(2,1)S(1)} %tile.26) | data formatting | bytes 1181180 | tf_op jit(solution)/shard_map/tile | solution.py:17
  11.4 0.4 slice.57
  11.7 1.4 %reshape.59 = bf16[384,766]{1,0:T(8,128)(2,1)S(1)} reshape(bf16[294144]{0:T(1024)(128)(2,1)S(1)} %slice.57) | data formatting | bytes 1176576 | tf_op jit(solution)/shard_map/reshape | solution.py:19
  13.1 0.0 copy-start.7
  13.1 0.3 fusion.14
  13.4 0.2 fusion
  13.6 1.3 %collective-permute-start.3 = (bf16[384,128]{1,0:T(8,128)(2,1)S(1)}, bf16[384,128]{1,0:T(8,128)(2,1)}, u32[]{:S(2)}, u32[]{:S(2)}) collective-permute-start(bf16[384,128]{1,0:T(8,128)(2,1)S(1)} %collective-permute-done.1), channel_id=1, source_target_pairs={{4,0},{8,4},{12,8},{16,12},{20,16},{24,20},{28,24},{5,1},{9,5},{13... | collective-permute-start | bytes 294920 | tf_op jit(solution)/shard_map/ppermute | solution.py:12
  15.0 6.1 %collective-permute-start.2 = (bf16[384,128]{1,0:T(8,128)(2,1)S(1)}, bf16[384,128]{1,0:T(8,128)(2,1)}, u32[]{:S(2)}, u32[]{:S(2)}) collective-permute-start(bf16[384,128]{1,0:T(8,128)(2,1)S(1)} %collective-permute-done), channel_id=1, source_target_pairs={{0,4},{4,8},{8,12},{12,16},{16,20},{20,24},{24,28},{1,5},{5,9},{9,... | collective-permute-start | bytes 294920 | tf_op jit(solution)/shard_map/ppermute | solution.py:12
  21.0 0.3 fusion.2
  21.3 0.2 reduce-window.4
  21.5 0.6 slice.43
  22.1 0.1 pad.15
  22.2 0.1 reshape.60
  22.3 1.2 %reshape.61 = f32[384,767]{1,0:T(8,128)S(1)} reshape(f32[294528]{0:T(1024)S(1)} %bitcast.32) | data formatting | bytes 2356224 | tf_op jit(solution)/shard_map/reshape | solution.py:26
  23.5 0.0 copy-start.8
  23.5 0.1 reduce_sum.46
  23.6 0.1 dynamic_update_slice.12
  23.7 1.3 %collective-permute-start.5 = (bf16[384,128]{1,0:T(8,128)(2,1)}, bf16[384,128]{1,0:T(8,128)(2,1)S(1)}, u32[]{:S(2)}, u32[]{:S(2)}) collective-permute-start(bf16[384,128]{1,0:T(8,128)(2,1)} %collective-permute-done.3), channel_id=1, source_target_pairs={{4,0},{8,4},{12,8},{16,12},{20,16},{24,20},{28,24},{5,1},{9,5},{13... | collective-permute-start | bytes 294920 | tf_op jit(solution)/shard_map/ppermute | solution.py:12
  25.0 4.8 %collective-permute-start.4 = (bf16[384,128]{1,0:T(8,128)(2,1)}, bf16[384,128]{1,0:T(8,128)(2,1)S(1)}, u32[]{:S(2)}, u32[]{:S(2)}) collective-permute-start(bf16[384,128]{1,0:T(8,128)(2,1)} %collective-permute-done.2), channel_id=1, source_target_pairs={{0,4},{4,8},{8,12},{12,16},{16,20},{20,24},{24,28},{1,5},{5,9},{9,... | collective-permute-start | bytes 294920 | tf_op jit(solution)/shard_map/ppermute | solution.py:12
  29.8 1.3 %fusion.10 = (s32[]{:T(128)}, s32[]{:T(128)}) fusion(s32[3,1]{0,1:T(1,128)S(1)} %reduce-window.4, s32[]{:T(128)} %bitcast.2, s32[]{:T(128)S(6)} %axis_index.15, s32[3]{0:T(128)S(1)} %copy-done.7), kind=kLoop, calls=%fused_computation.28 | loop fusion | flops 13 | bytes 40 | tf_op jit(solution)/shard_map/reduce_min | solution.py:42
  35.0 0.6 dynamic-slice
  36.2 4.2 %conditional.9 = ((f32[384,128]{1,0:T(8,128)S(1)}, f32[2304]{0:T(1024)S(1)}, f32[384,128]{1,0:T(8,128)S(1)})) conditional(s32[]{:T(128)} %convert_element_type.74, (f32[384,128]{1,0:T(8,128)S(1)}, f32[2304]{0:T(1024)S(1)}, f32[384,128]{1,0:T(8,128)S(1)}) %tuple.66, (pred[]{:T(512)}, bf16[1536]{0:T(1024)(128)(2,1)S(1)}, f32[384,128]{1,0:T(8,128)S(1)}, ...), branch_computations={%region_4.5_spmd, %region_5.11_spmd} | conditional | flops 113639040 | bytes 15347118 | solution.py:92
  36.2 0.0 copy-start.6
  36.3 0.1 dynamic_slice.15
  36.4 1.1 %tile.6 = bf16[295295]{0:T(1024)(128)(2,1)S(1)} reshape(bf16[385,767]{1,0:T(8,128)(2,1)S(1)} %tile.3) | data formatting | bytes 1181180 | tf_op jit(solution)/shard_map/cond/branch_1_fun/tile | solution.py:17
  37.4 0.4 slice.49
  37.8 1.4 %reshape.45 = bf16[384,766]{1,0:T(8,128)(2,1)S(1)} reshape(bf16[294144]{0:T(1024)(128)(2,1)S(1)} %slice.49) | data formatting | bytes 1176576 | tf_op jit(solution)/shard_map/cond/branch_1_fun/reshape | solution.py:19
  39.2 1.1 %conditional.1 = (f32[384,128]{1,0:T(8,128)S(1)}) conditional(s32[]{:T(128)} %convert_element_type.51, f32[384,128]{1,0:T(8,128)S(1)} %get-tuple-element.161, (bf16[384,384]{1,0:T(8,128)(2,1)S(1)}, bf16[384,128]{1,0:T(8,128)(2,1)}, f32[384,128]{1,0:T(8,128)S(1)}) %tuple.105), branch_computations={%region_9.9_spmd, %region_10.10_spmd} | conditional | flops 37797888 | bytes 786440 | solution.py:89
  39.3 1.1 %convolution_add_fusion.1 = f32[384,128]{1,0:T(8,128)S(1)} fusion(f32[384,128]{1,0:T(8,128)S(1)} %get-tuple-element.149, bf16[384,384]{1,0:T(8,128)(2,1)S(1)} %get-tuple-element.150, bf16[384,128]{1,0:T(8,128)(2,1)} %get-tuple-element.151), kind=kOutput, calls=%fused_computation.2 | convolution fusion | flops 37797888 | bytes 786432 | tf_op jit(solution)/shard_map/cond/branch_1_fun/cond/branch_1_fun/dot_general | solution.py:84
  40.4 4.5 %conditional.10 = ((f32[384,128]{1,0:T(8,128)S(1)}, f32[2304]{0:T(1024)S(1)}, f32[384,128]{1,0:T(8,128)S(1)})) conditional(s32[]{:T(128)} %convert_element_type.73, (f32[384,128]{1,0:T(8,128)S(1)}, f32[2304]{0:T(1024)S(1)}, f32[384,128]{1,0:T(8,128)S(1)}) %get-tuple-element.264, (pred[]{:T(512)}, bf16[1536]{0:T(1024)(128)(2,1)S(1)}, ...), branch_computations={%region_11.12_spmd, %region_12.18_spmd} | conditional | flops 113639040 | bytes 14953874 | solution.py:92
  40.6 0.1 dynamic_slice.17
  40.7 1.1 %tile.16 = bf16[295295]{0:T(1024)(128)(2,1)S(1)} reshape(bf16[385,767]{1,0:T(8,128)(2,1)S(1)} %tile.7) | data formatting | bytes 1181180 | tf_op jit(solution)/shard_map/cond/branch_1_fun/tile | solution.py:17
  41.8 0.4 slice.52
  42.1 1.4 %reshape.48 = bf16[384,766]{1,0:T(8,128)(2,1)S(1)} reshape(bf16[294144]{0:T(1024)(128)(2,1)S(1)} %slice.52) | data formatting | bytes 1176576 | tf_op jit(solution)/shard_map/cond/branch_1_fun/reshape | solution.py:19
  43.6 1.1 %conditional.3 = (f32[384,128]{1,0:T(8,128)S(1)}) conditional(s32[]{:T(128)} %convert_element_type.53, f32[384,128]{1,0:T(8,128)S(1)} %get-tuple-element.180, (bf16[384,384]{1,0:T(8,128)(2,1)S(1)}, bf16[384,128]{1,0:T(8,128)(2,1)}, f32[384,128]{1,0:T(8,128)S(1)}) %tuple.53), branch_computations={%region_16.16_spmd, %region_17.17_spmd} | conditional | flops 37797888 | bytes 786440 | solution.py:89
  43.6 1.1 %convolution_add_fusion.3 = f32[384,128]{1,0:T(8,128)S(1)} fusion(f32[384,128]{1,0:T(8,128)S(1)} %get-tuple-element.168, bf16[384,384]{1,0:T(8,128)(2,1)S(1)} %get-tuple-element.169, bf16[384,128]{1,0:T(8,128)(2,1)} %get-tuple-element.170), kind=kOutput, calls=%fused_computation.5 | convolution fusion | flops 37797888 | bytes 786432 | tf_op jit(solution)/shard_map/cond/branch_1_fun/cond/branch_1_fun/dot_general | solution.py:84
  45.0 30.2 %all-reduce.6 = f32[1536]{0:T(1024)S(1)} all-reduce(f32[1536]{0:T(1024)S(1)} %slice.47), channel_id=2, replica_groups=mesh['seq'=8,'ch'=4] {'seq'}, use_global_device_ids=true, to_apply=%region_25.26.clone | all-reduce | flops 1536 | bytes 12288
  75.3 0.1 dynamic-slice.1
  75.4 5.6 %psum.7 = f32[192]{0:T(256)S(1)} all-reduce(f32[192]{0:T(256)S(1)} %dynamic-slice.1), channel_id=1, replica_groups=mesh['seq'=8,'ch'=4] {'ch'}, use_global_device_ids=true, to_apply=%region_26.27 | all-reduce | flops 192 | bytes 1536 | tf_op jit(solution)/shard_map/psum | solution.py:101
  81.0 0.6 broadcast_multiply_fusion
  81.6 1.4 %fusion.8 = (bf16[384,128]{1,0:T(8,128)(2,1)}, bf16[384,128]{1,0:T(8,128)(2,1)}, bf16[384,128]{1,0:T(8,128)(2,1)}) fusion(bf16[384,128]{1,0:T(8,128)(2,1)S(1)} %copy-done, f32[384,128]{1,0:T(8,128)S(1)} %get-tuple-element.221, bf16[384,128]{1,0:T(8,128)(2,1)S(1)} %fusion.4, f32[128]{0:T(128)} %param.28, bf16[384,128]{1,0:T(8,128)(2,1)S(1)} %copy-done.1, ...), kind=kLoop, calls=%fused_computation.22 | loop fusion | flops 737280 | bytes 1180160 | tf_op jit(solution)/shard_map/convert_element_type | solution.py:111
  (24 shorter events, 0.3 us)
Async XLA Ops:
  1.6 12.0 %collective-permute-start.1 = (bf16[384,128]{1,0:T(8,128)(2,1)S(1)}, bf16[384,128]{1,0:T(8,128)(2,1)S(1)}, u32[]{:S(2)}, u32[]{:S(2)}) collective-permute-start(bf16[384,128]{1,0:T(8,128)(2,1)S(1)} %fusion.4), channel_id=1, source_target_pairs={{4,0},{8,4},{12,8},{16,12},{20,16},{24,20},{28,24},{5,1},{9,5},{13... | collective-permute-start | bytes 294920 | tf_op jit(solution)/shard_map/ppermute | solution.py:12
  3.9 11.1 %collective-permute-start = (bf16[384,128]{1,0:T(8,128)(2,1)S(1)}, bf16[384,128]{1,0:T(8,128)(2,1)S(1)}, u32[]{:S(2)}, u32[]{:S(2)}) collective-permute-start(bf16[384,128]{1,0:T(8,128)(2,1)S(1)} %fusion.7), channel_id=1, source_target_pairs={{0,4},{4,8},{8,12},{12,16},{16,20},{20,24},{24,28},{1,5},{5,9},{9,... | collective-permute-start | bytes 294920 | tf_op jit(solution)/shard_map/ppermute | solution.py:12
  13.1 8.2 %copy-start.7 = (s32[3]{0:T(128)S(1)}, s32[3]{0:T(128)}, u32[]{:S(2)}) copy-start(s32[3]{0:T(128)} %param.30) | copy-start | bytes 40
  13.6 10.0 %collective-permute-start.3 = (bf16[384,128]{1,0:T(8,128)(2,1)S(1)}, bf16[384,128]{1,0:T(8,128)(2,1)}, u32[]{:S(2)}, u32[]{:S(2)}) collective-permute-start(bf16[384,128]{1,0:T(8,128)(2,1)S(1)} %collective-permute-done.1), channel_id=1, source_target_pairs={{4,0},{8,4},{12,8},{16,12},{20,16},{24,20},{28,24},{5,1},{9,5},{13... | collective-permute-start | bytes 294920 | tf_op jit(solution)/shard_map/ppermute | solution.py:12
  15.0 10.0 %collective-permute-start.2 = (bf16[384,128]{1,0:T(8,128)(2,1)S(1)}, bf16[384,128]{1,0:T(8,128)(2,1)}, u32[]{:S(2)}, u32[]{:S(2)}) collective-permute-start(bf16[384,128]{1,0:T(8,128)(2,1)S(1)} %collective-permute-done), channel_id=1, source_target_pairs={{0,4},{4,8},{8,12},{12,16},{16,20},{20,24},{24,28},{1,5},{5,9},{9,... | collective-permute-start | bytes 294920 | tf_op jit(solution)/shard_map/ppermute | solution.py:12
  23.5 11.5 %copy-start.8 = (u32[32]{0:T(128)S(1)}, u32[32]{0:T(128)}, u32[]{:S(2)}) copy-start(u32[32]{0:T(128)} %constant.65) | copy-start | bytes 388
  23.7 21.3 %collective-permute-start.5 = (bf16[384,128]{1,0:T(8,128)(2,1)}, bf16[384,128]{1,0:T(8,128)(2,1)S(1)}, u32[]{:S(2)}, u32[]{:S(2)}) collective-permute-start(bf16[384,128]{1,0:T(8,128)(2,1)} %collective-permute-done.3), channel_id=1, source_target_pairs={{4,0},{8,4},{12,8},{16,12},{20,16},{24,20},{28,24},{5,1},{9,5},{13... | collective-permute-start | bytes 294920 | tf_op jit(solution)/shard_map/ppermute | solution.py:12
  25.0 20.0 %collective-permute-start.4 = (bf16[384,128]{1,0:T(8,128)(2,1)}, bf16[384,128]{1,0:T(8,128)(2,1)S(1)}, u32[]{:S(2)}, u32[]{:S(2)}) collective-permute-start(bf16[384,128]{1,0:T(8,128)(2,1)} %collective-permute-done.2), channel_id=1, source_target_pairs={{0,4},{4,8},{8,12},{12,16},{16,20},{20,24},{24,28},{1,5},{5,9},{9,... | collective-permute-start | bytes 294920 | tf_op jit(solution)/shard_map/ppermute | solution.py:12
  36.2 3.0 %copy-start.6 = (bf16[384,128]{1,0:T(8,128)(2,1)}, bf16[384,128]{1,0:T(8,128)(2,1)S(1)}, u32[]{:S(2)}) copy-start(bf16[384,128]{1,0:T(8,128)(2,1)S(1)} %get-tuple-element.162) | copy-start | bytes 294916 | tf_op jit(solution)/shard_map/cond
  45.0 36.6 %copy-start = (bf16[384,128]{1,0:T(8,128)(2,1)S(1)}, bf16[384,128]{1,0:T(8,128)(2,1)}, u32[]{:S(2)}) copy-start(bf16[384,128]{1,0:T(8,128)(2,1)} %param.25) | copy-start | bytes 294916
  45.0 36.6 %copy-start.1 = (bf16[384,128]{1,0:T(8,128)(2,1)S(1)}, bf16[384,128]{1,0:T(8,128)(2,1)}, u32[]{:S(2)}) copy-start(bf16[384,128]{1,0:T(8,128)(2,1)} %param.26) | copy-start | bytes 294916
  45.0 36.6 %copy-start.2 = (bf16[384,128]{1,0:T(8,128)(2,1)S(1)}, bf16[384,128]{1,0:T(8,128)(2,1)}, u32[]{:S(2)}) copy-start(bf16[384,128]{1,0:T(8,128)(2,1)} %param.27) | copy-start | bytes 294916
where the time goes:
time: 83.7 us; the launch traced here: 83 us
  blocking collectives  35.9 us (43%)
  starting transfers between devices  20.3 us (24%)
  local copies, waits for them, and re-layouts  11.6 us (14%)
  other arithmetic  6.2 us (7%)
  between operations  5.45 us (7%)
  matrix products  3.03 us (4%)
    unnamed x1, blocking collectives  30.2 us
    ppermute x6, starting transfers between devices, shifted(): return lax.ppermute(value, axis, pairs)  20.3 us
    psum x1, blocking collectives, body(): lag_total = lax.psum(owned_lags, 'ch')  5.63 us
    reshape x3, local copies, waits for them, and re-layouts, toeplitz_block(): return skewed.reshape(block_rows, 2 * block_rows - 2)[:, :block_rows]  4.11 us
    another operation x6, local copies, waits for them, and re-layouts, toeplitz_block(): tiled_taps = jnp.tile(window, block_rows + 1)  3.3 us
    dot_general x2, matrix products, behind(): jnp.dot(toeplitz, later_block, preferred_element_type=jnp.float32)  2.27 us
  transfers between devices with their start and end apart: 6, of which 0 were waited for; matrix products, arithmetic and copies ran while one was open for 21% of the time, Pallas kernels for 0%

commit v1 on v0

v1 whole, which is shorter than its diff:
```python
import functools
import math

import jax
import jax.numpy as jnp
from jax import lax
from jax.experimental import pallas as pl
from jax.experimental.pallas import tpu as pltpu
from jax.sharding import PartitionSpec as P

TILE = 128
LIMIT = 8 * 1024 * 1024
LAGF = 10**10
CONVF = 10**10
F32 = jnp.float32
BF16 = jnp.bfloat16


def shifted(value, axis, by):
    length = lax.axis_size(axis)
    pairs = [(i, i + by) for i in range(length) if 0 <= i + by < length]
    return lax.ppermute(value, axis, pairs)


def doc_bounds(lengths_ref, position):
    start, stop, end = 0, 0, 0
    for k in range(lengths_ref.shape[0]):
        begin, end = end, end + lengths_ref[k]
        inside = jnp.logical_and(begin <= position, position < end)
        start = jnp.where(inside, begin, start)
        stop = jnp.where(inside, end, stop)
    return start, stop


def flip_matrix():
    row = lax.broadcasted_iota(jnp.int32, (TILE, TILE), 0)
    col = lax.broadcasted_iota(jnp.int32, (TILE, TILE), 1)
    return (row + col == TILE - 1).astype(F32).astype(BF16)


def masks_kernel(lengths_ref, gate_out_ref, skip_ref, masks_ref, gate_ref, skip_out_ref):
    longest = masks_ref.shape[0] // 2
    gate_ref[...] = gate_out_ref[...]
    skip_out_ref[...] = skip_ref[...]
    position = lax.axis_index("seq")
    start, stop = doc_bounds(lengths_ref, position)
    for k in range(longest):
        for n, ok in ((k, position - k >= start), (longest + k, position + k < stop)):
            masks_ref[n] = jnp.full(masks_ref.shape[1:], ok.astype(F32)).astype(BF16)


def lag_kernel(masks_ref, flipped_ref, before_ref, cots_ref, parts_ref, sources_ref, *, owned, copies, scale):
    evens, rows, chans = cots_ref.shape
    blocks = rows // TILE
    longest = masks_ref.shape[0] // 2
    count = 2 * evens * blocks
    before = before_ref[...] * masks_ref[1, 0:1, :]
    sources = [block[at : at + TILE] for block in (before, flipped_ref[...]) for at in range(0, rows, TILE)]
    for n, tile in enumerate(sources[::-1]):
        sources_ref[n * TILE : (n + 1) * TILE, :] = tile
    zero = jnp.zeros((TILE, chans), BF16)
    wide = []
    for e in range(evens):
        cots = cots_ref[e] if e == 0 else cots_ref[e] * masks_ref[longest + 2 * e, 0:1, :]
        tiles = [zero] + [cots[at : at + TILE] for at in range(0, rows, TILE)] + [zero]
        wide += [jnp.concatenate(tiles[n : n + 2], axis=1) for n in range(blocks + 1)]
    wide = jnp.concatenate(wide, axis=0)
    sums = [None] * count
    for x in range(0, 2 * blocks, 2):
        source = jnp.concatenate(sources[x : x + 2], axis=1)
        product = lax.dot_general(source, wide, (((1,), (1,)), ((), ())), preferred_element_type=F32)
        for e in range(evens):
            for n in range(blocks + 1):
                d = 2 * blocks * e + n - 1 + blocks - x
                if d >= 0:
                    at = (e * (blocks + 1) + n) * TILE
                    piece = product[:, at : at + TILE]
                    sums[d] = piece if sums[d] is None else sums[d] + piece
    row = lax.broadcasted_iota(jnp.int32, (TILE, TILE), 0)
    col = lax.broadcasted_iota(jnp.int32, (TILE, TILE), 1)
    sums[0] = jnp.where(row + col >= TILE - 1, sums[0], 0.0)
    width = count * TILE
    skewed = pltpu.roll(jnp.concatenate(sums, axis=1), width - TILE + 1, 1, stride=1, stride_axis=0)
    lags = jnp.sum(skewed, axis=0, keepdims=True) * scale
    for p in range(width // owned):
        piece = lags[:, p * owned : (p + 1) * owned]
        for q in range(copies):
            parts_ref[p * copies + q, :, :owned] = piece


def ahead_kernel(masks_ref, taps_ref, sources_ref, later_ref, earlier_ref, ahead_ref):
    width = taps_ref.shape[1]
    count = sources_ref.shape[0] // TILE
    longest = masks_ref.shape[0] // 2
    rounded = taps_ref[...].astype(BF16).astype(F32)
    skewed = pltpu.roll(jnp.broadcast_to(rounded, (TILE, width)), 0, 1, stride=1, stride_axis=0)
    flip = flip_matrix()
    for d in range(width // TILE):
        block = skewed[:, d * TILE : (d + 1) * TILE]
        if d == 0:
            row = lax.broadcasted_iota(jnp.int32, block.shape, 0)
            col = lax.broadcasted_iota(jnp.int32, block.shape, 1)
            block = jnp.where(col >= row, block, 0.0)
        block = block.astype(BF16)
        later_ref[:, d * TILE : (d + 1) * TILE] = block
        earlier_ref[:, d * TILE : (d + 1) * TILE] = lax.dot_general(
            block, flip, (((0,), (0,)), ((), ())), preferred_element_type=F32
        ).astype(BF16)
    for m in range(1, longest // 2):
        mask = masks_ref[longest + 2 * m, 0:1, :]
        for b in range(count // 2):
            first = m * count + b + 1 - count // 2
            part = jnp.dot(
                earlier_ref[:, first * TILE : (first + count) * TILE], sources_ref[...], preferred_element_type=F32
            )
            ahead_ref[m - 1, b * TILE : (b + 1) * TILE, :] = part.astype(BF16) * mask


def near_kernel(
    masks_ref, value_ref, gate_in_ref, skip_ref, later_ref, earlier_ref, sources_ref, cots_ref,
    near_ref, grad_value_ref, grad_gate_ref, future_ref,
):
    longest, rows, _ = cots_ref.shape
    blocks = rows // TILE
    for k in range(longest):
        block = cots_ref[k] if k == 0 else cots_ref[k] * masks_ref[longest + k, 0:1, :]
        future_ref[k * rows : (k + 1) * rows, :] = block
    skip = skip_ref[...]
    for b in range(blocks):
        here = slice(b * TILE, (b + 1) * TILE)
        transposed = jnp.dot(
            later_ref[:, : (longest * blocks - b) * TILE], future_ref[b * TILE :, :], preferred_element_type=F32
        )
        through = transposed + skip * cots_ref[0, here, :].astype(F32)
        gate_in, value = gate_in_ref[here, :].astype(F32), value_ref[here, :].astype(F32)
        grad_value_ref[here, :] = (through * gate_in).astype(BF16)
        grad_gate_ref[here, :] = (through * value).astype(BF16)
        newer = blocks - 1 - b
        convolved = jnp.dot(
            earlier_ref[:, : (2 * blocks - newer) * TILE], sources_ref[newer * TILE :, :], preferred_element_type=F32
        )
        near_ref[here, :] = convolved + skip * (gate_in * value).astype(BF16).astype(F32)


def sum_kernel(gathered_ref, layer_out_ref, total_ref):
    del layer_out_ref
    owned = total_ref.shape[1]
    total_ref[...] = jnp.sum(gathered_ref[:, 0, :], axis=0, keepdims=True)[:, :owned]


PARAMS = pltpu.CompilerParams(vmem_limit_bytes=LIMIT)
VMEM = pl.BlockSpec(memory_space=pltpu.VMEM)
SMEM = pl.BlockSpec(memory_space=pltpu.SMEM)


def body(value_proj, gate_in, gate_out, skip_gain, filter_taps, doc_lengths, cotangent):
    rows, chans = value_proj.shape
    maxlag = filter_taps.shape[0]
    longest = maxlag // rows
    shards, groups = lax.axis_size("seq"), lax.axis_size("ch")
    block = jax.ShapeDtypeStruct((rows, chans), BF16)
    cot_gated = (cotangent.astype(F32) * gate_out.astype(F32)).astype(BF16)
    gated = (gate_in.astype(F32) * value_proj.astype(F32)).astype(BF16)
    flipped = gated.reshape(rows // TILE, TILE, chans)[:, ::-1].reshape(rows, chans)

    future = cot_gated[None]
    span = longest
    while span > 2:
        span //= 2
        future = jnp.concatenate([future, shifted(future, "seq", -span)], axis=0)
    before = shifted(flipped, "seq", 1)
    bits = max(future.shape[0].bit_length() - 1, 1)
    order = sorted(range(future.shape[0]), key=lambda n: int(format(n, f"0{bits}b")[::-1], 2))
    evens = future if len(order) <= 2 else jnp.stack([future[n] for n in order])
    odds = shifted(evens, "seq", -1)
    future = jnp.stack([evens, odds], axis=1).reshape(longest, rows, chans)

    masks, gate, skip = pl.pallas_call(
        masks_kernel,
        out_shape=(
            jax.ShapeDtypeStruct((2 * longest, 16, chans), BF16), block, jax.ShapeDtypeStruct((1, chans), F32)
        ),
        in_specs=[SMEM, VMEM, VMEM],
        out_specs=(VMEM,) * 3,
        compiler_params=PARAMS,
        name="masks",
    )(doc_lengths, gate_out, skip_gain.reshape(1, chans))

    owned = maxlag // shards
    grad_scale = 1.0 / math.sqrt(shards * rows * chans * groups)
    parts, sources = pl.pallas_call(
        functools.partial(lag_kernel, owned=owned, copies=groups, scale=grad_scale),
        out_shape=(
            jax.ShapeDtypeStruct((shards * groups, 1, -(-owned // TILE) * TILE), F32),
            jax.ShapeDtypeStruct((2 * rows, chans), BF16),
        ),
        in_specs=[VMEM] * 4,
        out_specs=(VMEM,) * 2,
        compiler_params=PARAMS,
        cost_estimate=pl.CostEstimate(flops=LAGF, bytes_accessed=2**20, transcendentals=0),
        name="lags",
    )(masks, flipped, before, evens)
    gathered = lax.all_to_all(parts, ("seq", "ch"), 0, 0, tiled=True)

    band = jax.ShapeDtypeStruct((TILE, maxlag), BF16)
    further = longest // 2 - 1
    later, earlier, ahead = pl.pallas_call(
        ahead_kernel,
        out_shape=(band, band, jax.ShapeDtypeStruct((further, rows, chans), BF16)),
        in_specs=[VMEM] * 3,
        out_specs=(VMEM,) * 3,
        compiler_params=PARAMS,
        name="ahead",
    )(masks, filter_taps.reshape(1, maxlag), sources)
    far = sum(shifted(ahead[m], "seq", 2 * m + 2).astype(F32) for m in range(further))

    near, grad_value, grad_gate = pl.pallas_call(
        near_kernel,
        out_shape=(jax.ShapeDtypeStruct((rows, chans), F32), block, block),
        in_specs=[VMEM] * 8,
        out_specs=(VMEM,) * 3,
        scratch_shapes=[pltpu.VMEM((maxlag, chans), BF16)],
        compiler_params=PARAMS,
        cost_estimate=pl.CostEstimate(flops=CONVF, bytes_accessed=2**20, transcendentals=0),
        name="near",
    )(masks, value_proj, gate_in, skip, later, earlier, sources, future)
    layer_out = (gate.astype(F32) * (near + far)).astype(BF16)
    filter_grad = pl.pallas_call(
        sum_kernel,
        out_shape=jax.ShapeDtypeStruct((1, owned), F32),
        in_specs=[VMEM, pl.BlockSpec(memory_space=pl.ANY)],
        out_specs=VMEM,
        compiler_params=PARAMS,
        name="sum",
    )(gathered, layer_out)[0]
    return (layer_out, grad_value, grad_gate, filter_grad)


def solution(mesh):
    placed = (P("seq", "ch"), P("seq", "ch"), P("seq", "ch"), P("ch"), P(), P(), P("seq", "ch"))
    return jax.shard_map(
        body,
        mesh=mesh,
        in_specs=placed,
        out_specs=(P("seq", "ch"), P("seq", "ch"), P("seq", "ch"), P("seq")),
        check_vma=False,
    )
```

time: 83.7 us -> 28.3 us (0.34)
  blocking collectives: 35.9 us -> 0 us
  local copies, waits for them, and re-layouts: 11.6 us -> 0.83 us
  other arithmetic: 6.2 us -> 1.15 us
  between operations: 5.45 us -> 0.84 us
  Pallas kernels: 0 us -> 4.58 us
  matrix products: 3.03 us -> 0 us
  waiting for transfers between devices: 0.02 us -> 1.45 us
  starting transfers between devices: 20.3 us -> 19.1 us
    unnamed x1 -> x0, blocking collectives: 30.2 us -> none
    ppermute x6 -> x4, starting transfers between devices: 20.3 us -> 11.1 us  [shifted(): return lax.ppermute(value, axis, pairs)]
    all_to_all x0 -> x1, starting transfers between devices: none -> 8.03 us  [body(): gathered = lax.all_to_all(parts, ('seq', 'ch'), 0, 0, tiled=True)]
    psum x1 -> x0, blocking collectives: 5.63 us -> none  [body(): lag_total = lax.psum(owned_lags, 'ch')]
    reshape x5 -> x1, local copies, waits for them, and re-layouts: 5.37 us -> 0.01 us  [body(): filter_taps.reshape(1, maxlag)]
    pallas_call x0 -> x5, Pallas kernels: none -> 4.58 us  [the longest x1 1.39 us: body(): pl.pallas_call(functools.partial(lag_kernel, owned=owned, copies=groups,...]
    convert_element_type x4 -> x2, other arithmetic: 4.07 us -> 0.07 us  [the longest x1 0.04 us: body(): layer_out = (gate.astype(F32) * (near + far)).astype(BF16)]
    another operation x6 -> x1, local copies, waits for them, and re-layouts: 3.3 us -> 0.03 us  [body(): future = jnp.stack([evens, odds], axis=1).reshape(longest, rows, chans)]
  transfers between devices with their start and end apart: 6 -> 5, of which waited for: 0 -> 3; matrix products, arithmetic and copies ran while one was open for 21% -> 1% of each run, Pallas kernels for 0% -> 14%
where the time goes in v1:
time: 28.3 us; the launch traced here: 28 us
  starting transfers between devices  19.1 us (67%)
  Pallas kernels  4.58 us (16%)
  waiting for transfers between devices  1.45 us (5%)
  other arithmetic  1.15 us (4%)
  between operations  0.84 us (3%)
  local copies, waits for them, and re-layouts  0.83 us (3%)
    ppermute x4, starting transfers between devices, shifted(): return lax.ppermute(value, axis, pairs)  11.1 us
    all_to_all x1, starting transfers between devices, body(): gathered = lax.all_to_all(parts, ('seq', 'ch'), 0, 0, tiled=True)  8.03 us
    pallas_call x1, Pallas kernels, body(): pl.pallas_call(functools.partial(lag_kernel, owned=owned, copies=groups,...  1.39 us
    pallas_call x1, Pallas kernels, body(): pl.pallas_call(near_kernel, out_shape=(jax.ShapeDtypeStruct((rows, chans)...  1.28 us
    ppermute x4, waiting for transfers between devices, shifted(): return lax.ppermute(value, axis, pairs)  1.06 us
    broadcast_in_dim x1, other arithmetic, body(): future = cot_gated[None]  1.01 us
    pallas_call x1, Pallas kernels, body(): pl.pallas_call(ahead_kernel, out_shape=(band, band, jax.ShapeDtypeStruct(...  0.76 us
    unnamed x14, local copies, waits for them, and re-layouts  0.68 us
  transfers between devices with their start and end apart: 5, of which 3 were waited for; matrix products, arithmetic and copies ran while one was open for 1% of the time, Pallas kernels for 14%

profile of v1, /device:TPU:0, one launch (start us, length us, event | category | flops | bytes accessed | tf_op | source)
XLA Modules:
  0.0 28.0 jit_solution(15054038691802296738)
XLA Ops:
  0.6 0.0 copy-start.3
  0.6 0.0 copy-start.2
  0.7 1.0 %fusion = bf16[1,384,128]{2,1,0:T(8,128)(2,1)S(1)} fusion(bf16[384,128]{1,0:T(8,128)(2,1)} %gate_out_ref.1, bf16[384,128]{1,0:T(8,128)(2,1)} %param.13), kind=kLoop, calls=%fused_computation.5 | loop fusion | flops 196608 | bytes 294912 | tf_op jit(solution)/shard_map/broadcast_in_dim | solution.py:166
  1.7 1.3 %collective-permute-start.1 = (bf16[1,384,128]{2,1,0:T(8,128)(2,1)S(1)}, bf16[1,384,128]{2,1,0:T(8,128)(2,1)S(1)}, u32[]{:S(2)}, u32[]{:S(2)}) collective-permute-start(bf16[1,384,128]{2,1,0:T(8,128)(2,1)S(1)} %fusion), channel_id=1, source_target_pairs={{8,0},{12,4},{16,8},{20,12},{24,16},{28,20},{9,1},{13,5},{17,9},{2... | collective-permute-start | bytes 294920 | tf_op jit(solution)/shard_map/ppermute | solution.py:22
  3.0 0.0 copy-done.3
  3.0 0.0 copy-done.2
  3.0 0.0 copy-start.6
  3.0 0.0 copy-start
  3.0 0.1 rev.3
  3.2 4.8 %collective-permute-start = (bf16[384,128]{1,0:T(8,128)(2,1)S(1)}, bf16[384,128]{1,0:T(8,128)(2,1)S(1)}, u32[]{:S(2)}, u32[]{:S(2)}) collective-permute-start(bf16[384,128]{1,0:T(8,128)(2,1)S(1)} %bitcast.12), channel_id=1, source_target_pairs={{0,4},{4,8},{8,12},{12,16},{16,20},{20,24},{24,28},{1,5},{5,9},{9,... | collective-permute-start | bytes 294920 | tf_op jit(solution)/shard_map/ppermute | solution.py:22
  8.0 0.0 copy-done.6
  8.1 0.0 copy-start.4
  8.1 0.0 copy-start.5
  8.1 0.0 copy-done
  8.1 0.6 %copy-done.4 = s32[3]{0:T(128)S(1)} copy-done((s32[3]{0:T(128)S(1)}, s32[3]{0:T(128)}, u32[]{:S(2)}) %copy-start.4) | copy-done | bytes 36
  8.7 0.0 copy-done.5
  8.7 0.6 %masks.1 = (bf16[8,16,128]{2,1,0:T(8,128)(2,1)S(1)}, bf16[384,128]{1,0:T(8,128)(2,1)S(1)}, f32[1,128]{1,0:T(1,128)S(1)}) custom-call(s32[3]{0:T(128)S(1)} %copy-done.4, bf16[384,128]{1,0:T(8,128)(2,1)S(1)} %copy-done, f32[1,128]{1,0:T(1,128)S(1)} %bitcast.14), custom_call_target="tpu_custom_call" | custom-call | tf_op jit(solution)/shard_map/masks/pallas_call | solution.py:178
  9.3 0.1 collective-permute-done.1
  9.4 1.3 %collective-permute-start.2 = (bf16[2,384,128]{2,1,0:T(8,128)(2,1)S(1)}, bf16[2,384,128]{2,1,0:T(8,128)(2,1)S(1)}, u32[]{:S(2)}, u32[]{:S(2)}) collective-permute-start(bf16[2,384,128]{2,1,0:T(8,128)(2,1)S(1)} %get-tuple-element.27.cots_ref), channel_id=1, source_target_pairs={{4,0},{8,4},{12,8},{16,12},{20,16},{24,20},{28,24},{5,1},{9,5},{13... | collective-permute-start | bytes 589832 | tf_op jit(solution)/shard_map/ppermute | solution.py:22
  10.7 0.0 collective-permute-done.before_ref
  10.7 1.4 %lags.1 = (f32[32,1,256]{2,1,0:T(1,128)}, bf16[768,128]{1,0:T(8,128)(2,1)S(1)}) custom-call(bf16[8,16,128]{2,1,0:T(8,128)(2,1)S(1)} %get-tuple-element.16.masks_ref, bf16[384,128]{1,0:T(8,128)(2,1)S(1)} %bitcast.13, bf16[384,128]{1,0:T(8,128)(2,1)S(1)} %collective-permute-done.before_ref, bf16[2,384,128]{2,1,0:T(8,128)(2,1)S(1)} %get-tuple-element.27.cots_ref), custom_call_target="tpu_custom_call" | custom-call | flops 10000000000 | bytes 1048576 | tf_op jit(solution)/shard_map/lags/pallas_call | solution.py:191
  12.1 8.0 %all-to-all-start = ((f32[32,1,256]{2,1,0:T(1,128)}), f32[32,1,256]{2,1,0:T(1,128)S(1)}, u32[]{:S(2)}, u32[]{:S(2)}) async-start(f32[32,1,256]{2,1,0:T(1,128)} %get-tuple-element.25), calls=%async_computation | async-start | bytes 65536 | tf_op jit(solution)/shard_map/all_to_all | solution.py:203
  20.1 0.8 %ahead.1 = (bf16[128,1536]{1,0:T(8,128)(2,1)S(1)}, bf16[128,1536]{1,0:T(8,128)(2,1)S(1)}, bf16[1,384,128]{2,1,0:T(8,128)(2,1)S(1)}) custom-call(bf16[8,16,128]{2,1,0:T(8,128)(2,1)S(1)} %get-tuple-element.16.masks_ref, f32[1,1536]{1,0:T(1,128)S(1)} %reshape.24.taps_ref, bf16[768,128]{1,0:T(8,128)(2,1)S(1)} %get-tuple-element.18.sources_ref), custom_call_target="tpu_custom_call" | custom-call | tf_op jit(solution)/shard_map/ahead/pallas_call | solution.py:207
  20.9 3.7 %collective-permute-start.3 = (bf16[384,128]{1,0:T(8,128)(2,1)S(1)}, bf16[384,128]{1,0:T(8,128)(2,1)S(1)}, u32[]{:S(2)}, u32[]{:S(2)}) collective-permute-start(bf16[384,128]{1,0:T(8,128)(2,1)S(1)} %bitcast.15), channel_id=1, source_target_pairs={{0,8},{4,12},{8,16},{12,20},{16,24},{20,28},{1,9},{5,13},{9,17},{1... | collective-permute-start | bytes 294920 | tf_op jit(solution)/shard_map/ppermute | solution.py:22
  24.6 0.0 collective-permute-done.2
  24.7 1.3 %near.1 = (f32[384,128]{1,0:T(8,128)S(1)}, bf16[384,128]{1,0:T(8,128)(2,1)}, bf16[384,128]{1,0:T(8,128)(2,1)}) custom-call(bf16[8,16,128]{2,1,0:T(8,128)(2,1)S(1)} %get-tuple-element.16.masks_ref, bf16[384,128]{1,0:T(8,128)(2,1)S(1)} %copy-done.2, bf16[384,128]{1,0:T(8,128)(2,1)S(1)} %copy-done.3, f32[1,128]{1,0:T(1,128)S(1)} %get-tuple-element.17.skip_ref, ...), custom_call_target="tpu_custom_call" | custom-call | flops 10000000000 | bytes 1048576 | tf_op jit(solution)/shard_map/near/pallas_call | solution.py:217
  26.0 1.0 %collective-permute-done.3 = bf16[384,128]{1,0:T(8,128)(2,1)S(1)} collective-permute-done((bf16[384,128]{1,0:T(8,128)(2,1)S(1)}, bf16[384,128]{1,0:T(8,128)(2,1)S(1)}, u32[]{:S(2)}, u32[]{:S(2)}) %collective-permute-start.3) | collective-permute-done | bytes 98336 | tf_op jit(solution)/shard_map/ppermute | solution.py:22
  27.0 0.0 copy-start.1
  27.0 0.4 %all-to-all-done.gathered_ref = f32[32,1,256]{2,1,0:T(1,128)S(1)} async-done(((f32[32,1,256]{2,1,0:T(1,128)}), f32[32,1,256]{2,1,0:T(1,128)S(1)}, u32[]{:S(2)}, u32[]{:S(2)}) %all-to-all-start) | async-done | bytes 32800 | tf_op jit(solution)/shard_map/all_to_all | solution.py:203
  27.4 0.6 %sum.1 = f32[1,192]{1,0:T(1,128)} custom-call(f32[32,1,256]{2,1,0:T(1,128)S(1)} %all-to-all-done.gathered_ref, bf16[384,128]{1,0:T(8,128)(2,1)S(1)} %multiply_convert_fusion.layer_out_ref), custom_call_target="tpu_custom_call" | custom-call | tf_op jit(solution)/shard_map/sum/pallas_call | solution.py:228
  28.0 0.0 copy-done.1
  (6 shorter events, 0.2 us)
Async XLA Ops:
  0.6 2.3 %copy-start.3 = (bf16[384,128]{1,0:T(8,128)(2,1)S(1)}, bf16[384,128]{1,0:T(8,128)(2,1)}, u32[]{:S(2)}) copy-start(bf16[384,128]{1,0:T(8,128)(2,1)} %gate_in_ref.1) | copy-start | bytes 294916
  0.6 2.3 %copy-start.2 = (bf16[384,128]{1,0:T(8,128)(2,1)S(1)}, bf16[384,128]{1,0:T(8,128)(2,1)}, u32[]{:S(2)}) copy-start(bf16[384,128]{1,0:T(8,128)(2,1)} %value_ref.1) | copy-start | bytes 294916
  1.7 7.7 %collective-permute-start.1 = (bf16[1,384,128]{2,1,0:T(8,128)(2,1)S(1)}, bf16[1,384,128]{2,1,0:T(8,128)(2,1)S(1)}, u32[]{:S(2)}, u32[]{:S(2)}) collective-permute-start(bf16[1,384,128]{2,1,0:T(8,128)(2,1)S(1)} %fusion), channel_id=1, source_target_pairs={{8,0},{12,4},{16,8},{20,12},{24,16},{28,20},{9,1},{13,5},{17,9},{2... | collective-permute-start | bytes 294920 | tf_op jit(solution)/shard_map/ppermute | solution.py:22
  3.0 5.0 %copy-start.6 = (f32[1536]{0:T(1024)S(1)}, f32[1536]{0:T(1024)}, u32[]{:S(2)}) copy-start(f32[1536]{0:T(1024)} %param.11) | copy-start | bytes 18436
  3.0 5.1 %copy-start = (bf16[384,128]{1,0:T(8,128)(2,1)S(1)}, bf16[384,128]{1,0:T(8,128)(2,1)}, u32[]{:S(2)}) copy-start(bf16[384,128]{1,0:T(8,128)(2,1)} %gate_out_ref.1) | copy-start | bytes 294916
  3.2 7.5 %collective-permute-start = (bf16[384,128]{1,0:T(8,128)(2,1)S(1)}, bf16[384,128]{1,0:T(8,128)(2,1)S(1)}, u32[]{:S(2)}, u32[]{:S(2)}) collective-permute-start(bf16[384,128]{1,0:T(8,128)(2,1)S(1)} %bitcast.12), channel_id=1, source_target_pairs={{0,4},{4,8},{8,12},{12,16},{16,20},{20,24},{24,28},{1,5},{5,9},{9,... | collective-permute-start | bytes 294920 | tf_op jit(solution)/shard_map/ppermute | solution.py:22
  8.1 0.7 %copy-start.4 = (s32[3]{0:T(128)S(1)}, s32[3]{0:T(128)}, u32[]{:S(2)}) copy-start(s32[3]{0:T(128)} %lengths_ref.1) | copy-start | bytes 40
  8.1 0.7 %copy-start.5 = (f32[128]{0:T(128)S(1)}, f32[128]{0:T(128)}, u32[]{:S(2)}) copy-start(f32[128]{0:T(128)} %param.10) | copy-start | bytes 1540
  9.4 15.2 %collective-permute-start.2 = (bf16[2,384,128]{2,1,0:T(8,128)(2,1)S(1)}, bf16[2,384,128]{2,1,0:T(8,128)(2,1)S(1)}, u32[]{:S(2)}, u32[]{:S(2)}) collective-permute-start(bf16[2,384,128]{2,1,0:T(8,128)(2,1)S(1)} %get-tuple-element.27.cots_ref), channel_id=1, source_target_pairs={{4,0},{8,4},{12,8},{16,12},{20,16},{24,20},{28,24},{5,1},{9,5},{13... | collective-permute-start | bytes 589832 | tf_op jit(solution)/shard_map/ppermute | solution.py:22
  12.1 15.3 %all-to-all-start = ((f32[32,1,256]{2,1,0:T(1,128)}), f32[32,1,256]{2,1,0:T(1,128)S(1)}, u32[]{:S(2)}, u32[]{:S(2)}) async-start(f32[32,1,256]{2,1,0:T(1,128)} %get-tuple-element.25), calls=%async_computation | async-start | bytes 65536 | tf_op jit(solution)/shard_map/all_to_all | solution.py:203
  20.9 6.0 %collective-permute-start.3 = (bf16[384,128]{1,0:T(8,128)(2,1)S(1)}, bf16[384,128]{1,0:T(8,128)(2,1)S(1)}, u32[]{:S(2)}, u32[]{:S(2)}) collective-permute-start(bf16[384,128]{1,0:T(8,128)(2,1)S(1)} %bitcast.15), channel_id=1, source_target_pairs={{0,8},{4,12},{8,16},{12,20},{16,24},{20,28},{1,9},{5,13},{9,17},{1... | collective-permute-start | bytes 294920 | tf_op jit(solution)/shard_map/ppermute | solution.py:22
  27.0 1.0 %copy-start.1 = (bf16[384,128]{1,0:T(8,128)(2,1)}, bf16[384,128]{1,0:T(8,128)(2,1)S(1)}, u32[]{:S(2)}) copy-start(bf16[384,128]{1,0:T(8,128)(2,1)S(1)} %multiply_convert_fusion.layer_out_ref) | copy-start | bytes 294916

commit v2 on v1

--- a/solution.py
+++ b/solution.py
@@ -22,14 +22,19 @@
     return lax.ppermute(value, axis, pairs)
 
 
-def doc_bounds(lengths_ref, position):
-    start, stop, end = 0, 0, 0
-    for k in range(lengths_ref.shape[0]):
-        begin, end = end, end + lengths_ref[k]
+def doc_masks(lengths_ref, offsets, chans):
+    position = lax.axis_index("seq")
+    lengths = lengths_ref[...]
+    start = stop = end = jnp.zeros((1, chans), jnp.int32)
+    for k in range(lengths.shape[1]):
+        begin, end = end, end + jnp.broadcast_to(lengths[:, k : k + 1], end.shape)
         inside = jnp.logical_and(begin <= position, position < end)
-        start = jnp.where(inside, begin, start)
-        stop = jnp.where(inside, end, stop)
-    return start, stop
+        start, stop = jnp.where(inside, begin, start), jnp.where(inside, end, stop)
+    masks = []
+    for offset in offsets:
+        inside = jnp.logical_and(start <= position + offset, position + offset < stop)
+        masks.append(jnp.where(inside, 1.0, 0.0).astype(BF16))
+    return masks
 
 
 def flip_matrix():
@@ -38,30 +43,28 @@
     return (row + col == TILE - 1).astype(F32).astype(BF16)
 
 
-def masks_kernel(lengths_ref, gate_out_ref, skip_ref, masks_ref, gate_ref, skip_out_ref):
-    longest = masks_ref.shape[0] // 2
-    gate_ref[...] = gate_out_ref[...]
+def stage_kernel(lengths_ref, skip_ref, lengths_out_ref, skip_out_ref):
+    lengths_out_ref[...] = lengths_ref[...]
     skip_out_ref[...] = skip_ref[...]
-    position = lax.axis_index("seq")
-    start, stop = doc_bounds(lengths_ref, position)
-    for k in range(longest):
-        for n, ok in ((k, position - k >= start), (longest + k, position + k < stop)):
-            masks_ref[n] = jnp.full(masks_ref.shape[1:], ok.astype(F32)).astype(BF16)
-
-
-def lag_kernel(masks_ref, flipped_ref, before_ref, cots_ref, parts_ref, sources_ref, *, owned, copies, scale):
+
+
+def lag_kernel(
+    lengths_ref, flipped_ref, before_ref, cots_ref, gate_out_ref, parts_ref, sources_ref,
+    *, owned, copies, scale,
+):
+    del gate_out_ref
     evens, rows, chans = cots_ref.shape
     blocks = rows // TILE
-    longest = masks_ref.shape[0] // 2
     count = 2 * evens * blocks
-    before = before_ref[...] * masks_ref[1, 0:1, :]
+    masks = doc_masks(lengths_ref, [-1] + [2 * e for e in range(1, evens)], chans)
+    before = before_ref[...] * masks[0]
     sources = [block[at : at + TILE] for block in (before, flipped_ref[...]) for at in range(0, rows, TILE)]
     for n, tile in enumerate(sources[::-1]):
         sources_ref[n * TILE : (n + 1) * TILE, :] = tile
     zero = jnp.zeros((TILE, chans), BF16)
     wide = []
     for e in range(evens):
-        cots = cots_ref[e] if e == 0 else cots_ref[e] * masks_ref[longest + 2 * e, 0:1, :]
+        cots = cots_ref[e] if e == 0 else cots_ref[e] * masks[e]
         tiles = [zero] + [cots[at : at + TILE] for at in range(0, rows, TILE)] + [zero]
         wide += [jnp.concatenate(tiles[n : n + 2], axis=1) for n in range(blocks + 1)]
     wide = jnp.concatenate(wide, axis=0)
@@ -88,10 +91,11 @@
             parts_ref[p * copies + q, :, :owned] = piece
 
 
-def ahead_kernel(masks_ref, taps_ref, sources_ref, later_ref, earlier_ref, ahead_ref):
+def ahead_kernel(lengths_ref, taps_ref, sources_ref, later_ref, earlier_ref, ahead_ref):
     width = taps_ref.shape[1]
     count = sources_ref.shape[0] // TILE
-    longest = masks_ref.shape[0] // 2
+    further, _, chans = ahead_ref.shape
+    masks = doc_masks(lengths_ref, [2 * m for m in range(1, further + 1)], chans)
     rounded = taps_ref[...].astype(BF16).astype(F32)
     skewed = pltpu.roll(jnp.broadcast_to(rounded, (TILE, width)), 0, 1, stride=1, stride_axis=0)
     flip = flip_matrix()
@@ -106,24 +110,24 @@
         earlier_ref[:, d * TILE : (d + 1) * TILE] = lax.dot_general(
             block, flip, (((0,), (0,)), ((), ())), preferred_element_type=F32
         ).astype(BF16)
-    for m in range(1, longest // 2):
-        mask = masks_ref[longest + 2 * m, 0:1, :]
+    for m in range(1, further + 1):
         for b in range(count // 2):
             first = m * count + b + 1 - count // 2
             part = jnp.dot(
                 earlier_ref[:, first * TILE : (first + count) * TILE], sources_ref[...], preferred_element_type=F32
             )
-            ahead_ref[m - 1, b * TILE : (b + 1) * TILE, :] = part.astype(BF16) * mask
+            ahead_ref[m - 1, b * TILE : (b + 1) * TILE, :] = part.astype(BF16) * masks[m - 1]
 
 
 def near_kernel(
-    masks_ref, value_ref, gate_in_ref, skip_ref, later_ref, earlier_ref, sources_ref, cots_ref,
+    lengths_ref, value_ref, gate_in_ref, skip_ref, later_ref, earlier_ref, sources_ref, cots_ref,
     near_ref, grad_value_ref, grad_gate_ref, future_ref,
 ):
-    longest, rows, _ = cots_ref.shape
+    longest, rows, chans = cots_ref.shape
     blocks = rows // TILE
+    masks = doc_masks(lengths_ref, range(longest), chans)
     for k in range(longest):
-        block = cots_ref[k] if k == 0 else cots_ref[k] * masks_ref[longest + k, 0:1, :]
+        block = cots_ref[k] if k == 0 else cots_ref[k] * masks[k]
         future_ref[k * rows : (k + 1) * rows, :] = block
     skip = skip_ref[...]
     for b in range(blocks):
@@ -150,7 +154,6 @@
 
 PARAMS = pltpu.CompilerParams(vmem_limit_bytes=LIMIT)
 VMEM = pl.BlockSpec(memory_space=pltpu.VMEM)
-SMEM = pl.BlockSpec(memory_space=pltpu.SMEM)
 
 
 def body(value_proj, gate_in, gate_out, skip_gain, filter_taps, doc_lengths, cotangent):
@@ -175,17 +178,16 @@
     odds = shifted(evens, "seq", -1)
     future = jnp.stack([evens, odds], axis=1).reshape(longest, rows, chans)
 
-    masks, gate, skip = pl.pallas_call(
-        masks_kernel,
+    lengths, skip = pl.pallas_call(
+        stage_kernel,
         out_shape=(
-            jax.ShapeDtypeStruct((2 * longest, 16, chans), BF16), block, jax.ShapeDtypeStruct((1, chans), F32)
+            jax.ShapeDtypeStruct((1, doc_lengths.shape[0]), jnp.int32), jax.ShapeDtypeStruct((1, chans), F32)
         ),
-        in_specs=[SMEM, VMEM, VMEM],
-        out_specs=(VMEM,) * 3,
-        compiler_params=PARAMS,
-        name="masks",
-    )(doc_lengths, gate_out, skip_gain.reshape(1, chans))
-
+        in_specs=[VMEM] * 2,
+        out_specs=(VMEM,) * 2,
+        compiler_params=PARAMS,
+        name="stage",
+    )(doc_lengths.reshape(1, -1), skip_gain.reshape(1, chans))
     owned = maxlag // shards
     grad_scale = 1.0 / math.sqrt(shards * rows * chans * groups)
     parts, sources = pl.pallas_call(
@@ -194,12 +196,12 @@
             jax.ShapeDtypeStruct((shards * groups, 1, -(-owned // TILE) * TILE), F32),
             jax.ShapeDtypeStruct((2 * rows, chans), BF16),
         ),
-        in_specs=[VMEM] * 4,
+        in_specs=[VMEM] * 5,
         out_specs=(VMEM,) * 2,
         compiler_params=PARAMS,
         cost_estimate=pl.CostEstimate(flops=LAGF, bytes_accessed=2**20, transcendentals=0),
         name="lags",
-    )(masks, flipped, before, evens)
+    )(lengths, flipped, before, evens, gate_out)
     gathered = lax.all_to_all(parts, ("seq", "ch"), 0, 0, tiled=True)
 
     band = jax.ShapeDtypeStruct((TILE, maxlag), BF16)
@@ -211,7 +213,7 @@
         out_specs=(VMEM,) * 3,
         compiler_params=PARAMS,
         name="ahead",
-    )(masks, filter_taps.reshape(1, maxlag), sources)
+    )(lengths, filter_taps.reshape(1, maxlag), sources)
     far = sum(shifted(ahead[m], "seq", 2 * m + 2).astype(F32) for m in range(further))
 
     near, grad_value, grad_gate = pl.pallas_call(
@@ -223,8 +225,8 @@
         compiler_params=PARAMS,
         cost_estimate=pl.CostEstimate(flops=CONVF, bytes_accessed=2**20, transcendentals=0),
         name="near",
-    )(masks, value_proj, gate_in, skip, later, earlier, sources, future)
-    layer_out = (gate.astype(F32) * (near + far)).astype(BF16)
+    )(lengths, value_proj, gate_in, skip, later, earlier, sources, future)
+    layer_out = (gate_out.astype(F32) * (near + far)).astype(BF16)
     filter_grad = pl.pallas_call(
         sum_kernel,
         out_shape=jax.ShapeDtypeStruct((1, owned), F32),

time: 28.3 us -> 27.7 us (0.979)
  starting transfers between devices: 19.1 us -> 18.5 us
  waiting for transfers between devices: 1.45 us -> 2 us
  Pallas kernels: 4.58 us -> 4.07 us
    all_to_all x1, starting transfers between devices: 8.03 us -> 7.43 us  [body(): gathered = lax.all_to_all(parts, ('seq', 'ch'), 0, 0, tiled=True)]
    pallas_call x1, Pallas kernels: 0.57 us -> 0.01 us  [body(): pl.pallas_call(stage_kernel, out_shape=(jax.ShapeDtypeStruct((1, doc_leng...]
    ppermute x4, waiting for transfers between devices: 1.06 us -> 1.6 us  [shifted(): return lax.ppermute(value, axis, pairs)]
  transfers between devices with their start and end apart: 5 -> 5, of which waited for: 3 -> 3; matrix products, arithmetic and copies ran while one was open for 1% -> 1% of each run, Pallas kernels for 14% -> 13%
where the time goes in v2:
time: 27.7 us; the launch traced here: 27.4 us
  starting transfers between devices  18.5 us (67%)
  Pallas kernels  4.07 us (15%)
  waiting for transfers between devices  2 us (7%)
  other arithmetic  1.15 us (4%)
  local copies, waits for them, and re-layouts  0.84 us (3%)
  between operations  0.83 us (3%)
    ppermute x4, starting transfers between devices, shifted(): return lax.ppermute(value, axis, pairs)  11.1 us
    all_to_all x1, starting transfers between devices, body(): gathered = lax.all_to_all(parts, ('seq', 'ch'), 0, 0, tiled=True)  7.43 us
    ppermute x4, waiting for transfers between devices, shifted(): return lax.ppermute(value, axis, pairs)  1.6 us
    pallas_call x1, Pallas kernels, body(): pl.pallas_call(functools.partial(lag_kernel, owned=owned, copies=groups,...  1.4 us
    pallas_call x1, Pallas kernels, body(): pl.pallas_call(near_kernel, out_shape=(jax.ShapeDtypeStruct((rows, chans)...  1.31 us
    broadcast_in_dim x1, other arithmetic, body(): future = cot_gated[None]  1.01 us
    pallas_call x1, Pallas kernels, body(): pl.pallas_call(ahead_kernel, out_shape=(band, band, jax.ShapeDtypeStruct(...  0.76 us
    unnamed x14, local copies, waits for them, and re-layouts  0.68 us
  transfers between devices with their start and end apart: 5, of which 3 were waited for; matrix products, arithmetic and copies ran while one was open for 1% of the time, Pallas kernels for 13%

profile of v2, /device:TPU:0, one launch (start us, length us, event | category | flops | bytes accessed | tf_op | source)
XLA Modules:
  0.0 27.4 jit_solution(12769943613788018161)
XLA Ops:
  0.6 0.0 copy-start.3
  0.6 0.0 copy-start.2
  0.7 1.0 %fusion.2 = bf16[1,384,128]{2,1,0:T(8,128)(2,1)S(1)} fusion(bf16[384,128]{1,0:T(8,128)(2,1)} %gate_out_ref.1, bf16[384,128]{1,0:T(8,128)(2,1)} %param.13), kind=kLoop, calls=%fused_computation.7 | loop fusion | flops 196608 | bytes 294912 | tf_op jit(solution)/shard_map/broadcast_in_dim | solution.py:169
  1.7 1.3 %collective-permute-start.1 = (bf16[1,384,128]{2,1,0:T(8,128)(2,1)S(1)}, bf16[1,384,128]{2,1,0:T(8,128)(2,1)S(1)}, u32[]{:S(2)}, u32[]{:S(2)}) collective-permute-start(bf16[1,384,128]{2,1,0:T(8,128)(2,1)S(1)} %fusion.2), channel_id=1, source_target_pairs={{8,0},{12,4},{16,8},{20,12},{24,16},{28,20},{9,1},{13,5},{17,9},{2... | collective-permute-start | bytes 294920 | tf_op jit(solution)/shard_map/ppermute | solution.py:22
  3.0 0.0 copy-done.3
  3.0 0.0 copy-done.2
  3.0 0.0 copy-start.6
  3.0 0.1 rev.3
  3.2 4.8 %collective-permute-start = (bf16[384,128]{1,0:T(8,128)(2,1)S(1)}, bf16[384,128]{1,0:T(8,128)(2,1)S(1)}, u32[]{:S(2)}, u32[]{:S(2)}) collective-permute-start(bf16[384,128]{1,0:T(8,128)(2,1)S(1)} %bitcast.13), channel_id=1, source_target_pairs={{0,4},{4,8},{8,12},{12,16},{16,20},{20,24},{24,28},{1,5},{5,9},{9,... | collective-permute-start | bytes 294920 | tf_op jit(solution)/shard_map/ppermute | solution.py:22
  8.0 0.0 copy-done.6
  8.0 0.0 copy-start.4
  8.1 0.0 copy-start.5
  8.1 0.6 %copy-done.4 = s32[3]{0:T(128)S(1)} copy-done((s32[3]{0:T(128)S(1)}, s32[3]{0:T(128)}, u32[]{:S(2)}) %copy-start.4) | copy-done | bytes 36
  8.7 0.0 copy-done.5
  8.7 0.0 copy-start
  8.7 0.7 %collective-permute-done.1 = bf16[1,384,128]{2,1,0:T(8,128)(2,1)S(1)} collective-permute-done((bf16[1,384,128]{2,1,0:T(8,128)(2,1)S(1)}, bf16[1,384,128]{2,1,0:T(8,128)(2,1)S(1)}, u32[]{:S(2)}, u32[]{:S(2)}) %collective-permute-start.1) | collective-permute-done | bytes 98336 | tf_op jit(solution)/shard_map/ppermute | solution.py:22
  9.4 1.3 %collective-permute-start.2 = (bf16[2,384,128]{2,1,0:T(8,128)(2,1)S(1)}, bf16[2,384,128]{2,1,0:T(8,128)(2,1)S(1)}, u32[]{:S(2)}, u32[]{:S(2)}) collective-permute-start(bf16[2,384,128]{2,1,0:T(8,128)(2,1)S(1)} %get-tuple-element.25.cots_ref), channel_id=1, source_target_pairs={{4,0},{8,4},{12,8},{16,12},{20,16},{24,20},{28,24},{5,1},{9,5},{13... | collective-permute-start | bytes 589832 | tf_op jit(solution)/shard_map/ppermute | solution.py:22
  10.7 0.0 collective-permute-done.before_ref
  10.7 0.0 copy-done
  10.7 1.4 %lags.1 = (f32[32,1,256]{2,1,0:T(1,128)}, bf16[768,128]{1,0:T(8,128)(2,1)S(1)}) custom-call(s32[1,3]{1,0:T(1,128)S(1)} %get-tuple-element.14.lengths_ref, bf16[384,128]{1,0:T(8,128)(2,1)S(1)} %bitcast.14, bf16[384,128]{1,0:T(8,128)(2,1)S(1)} %collective-permute-done.before_ref, bf16[2,384,128]{2,1,0:T(8,128)(2,1)S(1)} %get-tuple-element.25.cots_ref, ...), custom_call_target="tpu_custom_call" | custom-call | flops 10000000000 | bytes 1048576 | tf_op jit(solution)/shard_map/lags/pallas_call | solution.py:193
  12.1 7.4 %all-to-all-start = ((f32[32,1,256]{2,1,0:T(1,128)}), f32[32,1,256]{2,1,0:T(1,128)S(1)}, u32[]{:S(2)}, u32[]{:S(2)}) async-start(f32[32,1,256]{2,1,0:T(1,128)} %get-tuple-element.23), calls=%async_computation | async-start | bytes 65536 | tf_op jit(solution)/shard_map/all_to_all | solution.py:205
  19.6 0.8 %ahead.1 = (bf16[128,1536]{1,0:T(8,128)(2,1)S(1)}, bf16[128,1536]{1,0:T(8,128)(2,1)S(1)}, bf16[1,384,128]{2,1,0:T(8,128)(2,1)S(1)}) custom-call(s32[1,3]{1,0:T(1,128)S(1)} %get-tuple-element.14.lengths_ref, f32[1,1536]{1,0:T(1,128)S(1)} %reshape.28.taps_ref, bf16[768,128]{1,0:T(8,128)(2,1)S(1)} %get-tuple-element.16.sources_ref), custom_call_target="tpu_custom_call" | custom-call | tf_op jit(solution)/shard_map/ahead/pallas_call | solution.py:209
  20.3 3.7 %collective-permute-start.3 = (bf16[384,128]{1,0:T(8,128)(2,1)S(1)}, bf16[384,128]{1,0:T(8,128)(2,1)S(1)}, u32[]{:S(2)}, u32[]{:S(2)}) collective-permute-start(bf16[384,128]{1,0:T(8,128)(2,1)S(1)} %bitcast.15), channel_id=1, source_target_pairs={{0,8},{4,12},{8,16},{12,20},{16,24},{20,28},{1,9},{5,13},{9,17},{1... | collective-permute-start | bytes 294920 | tf_op jit(solution)/shard_map/ppermute | solution.py:22
  24.0 0.0 collective-permute-done.2
  24.1 1.3 %near.1 = (f32[384,128]{1,0:T(8,128)S(1)}, bf16[384,128]{1,0:T(8,128)(2,1)}, bf16[384,128]{1,0:T(8,128)(2,1)}) custom-call(s32[1,3]{1,0:T(1,128)S(1)} %get-tuple-element.14.lengths_ref, bf16[384,128]{1,0:T(8,128)(2,1)S(1)} %copy-done.2, bf16[384,128]{1,0:T(8,128)(2,1)S(1)} %copy-done.3, f32[1,128]{1,0:T(1,128)S(1)} %get-tuple-element.15.skip_ref, ...), custom_call_target="tpu_custom_call" | custom-call | flops 10000000000 | bytes 1048576 | tf_op jit(solution)/shard_map/near/pallas_call | solution.py:219
  25.4 0.9 %collective-permute-done.3 = bf16[384,128]{1,0:T(8,128)(2,1)S(1)} collective-permute-done((bf16[384,128]{1,0:T(8,128)(2,1)S(1)}, bf16[384,128]{1,0:T(8,128)(2,1)S(1)}, u32[]{:S(2)}, u32[]{:S(2)}) %collective-permute-start.3) | collective-permute-done | bytes 98336 | tf_op jit(solution)/shard_map/ppermute | solution.py:22
  26.4 0.0 copy-start.1
  26.4 0.4 %all-to-all-done.gathered_ref = f32[32,1,256]{2,1,0:T(1,128)S(1)} async-done(((f32[32,1,256]{2,1,0:T(1,128)}), f32[32,1,256]{2,1,0:T(1,128)S(1)}, u32[]{:S(2)}, u32[]{:S(2)}) %all-to-all-start) | async-done | bytes 32800 | tf_op jit(solution)/shard_map/all_to_all | solution.py:205
  26.8 0.6 %sum.1 = f32[1,192]{1,0:T(1,128)} custom-call(f32[32,1,256]{2,1,0:T(1,128)S(1)} %all-to-all-done.gathered_ref, bf16[384,128]{1,0:T(8,128)(2,1)S(1)} %fusion.1.layer_out_ref), custom_call_target="tpu_custom_call" | custom-call | tf_op jit(solution)/shard_map/sum/pallas_call | solution.py:230
  27.4 0.0 copy-done.1
  (7 shorter events, 0.2 us)
Async XLA Ops:
  0.6 2.3 %copy-start.3 = (bf16[384,128]{1,0:T(8,128)(2,1)S(1)}, bf16[384,128]{1,0:T(8,128)(2,1)}, u32[]{:S(2)}) copy-start(bf16[384,128]{1,0:T(8,128)(2,1)} %gate_in_ref.1) | copy-start | bytes 294916
  0.6 2.3 %copy-start.2 = (bf16[384,128]{1,0:T(8,128)(2,1)S(1)}, bf16[384,128]{1,0:T(8,128)(2,1)}, u32[]{:S(2)}) copy-start(bf16[384,128]{1,0:T(8,128)(2,1)} %value_ref.1) | copy-start | bytes 294916
  1.7 7.7 %collective-permute-start.1 = (bf16[1,384,128]{2,1,0:T(8,128)(2,1)S(1)}, bf16[1,384,128]{2,1,0:T(8,128)(2,1)S(1)}, u32[]{:S(2)}, u32[]{:S(2)}) collective-permute-start(bf16[1,384,128]{2,1,0:T(8,128)(2,1)S(1)} %fusion.2), channel_id=1, source_target_pairs={{8,0},{12,4},{16,8},{20,12},{24,16},{28,20},{9,1},{13,5},{17,9},{2... | collective-permute-start | bytes 294920 | tf_op jit(solution)/shard_map/ppermute | solution.py:22
  3.0 5.0 %copy-start.6 = (f32[1536]{0:T(1024)S(1)}, f32[1536]{0:T(1024)}, u32[]{:S(2)}) copy-start(f32[1536]{0:T(1024)} %param.11) | copy-start | bytes 18436
  3.2 7.5 %collective-permute-start = (bf16[384,128]{1,0:T(8,128)(2,1)S(1)}, bf16[384,128]{1,0:T(8,128)(2,1)S(1)}, u32[]{:S(2)}, u32[]{:S(2)}) collective-permute-start(bf16[384,128]{1,0:T(8,128)(2,1)S(1)} %bitcast.13), channel_id=1, source_target_pairs={{0,4},{4,8},{8,12},{12,16},{16,20},{20,24},{24,28},{1,5},{5,9},{9,... | collective-permute-start | bytes 294920 | tf_op jit(solution)/shard_map/ppermute | solution.py:22
  8.0 0.7 %copy-start.4 = (s32[3]{0:T(128)S(1)}, s32[3]{0:T(128)}, u32[]{:S(2)}) copy-start(s32[3]{0:T(128)} %param.12) | copy-start | bytes 40
  8.1 0.7 %copy-start.5 = (f32[128]{0:T(128)S(1)}, f32[128]{0:T(128)}, u32[]{:S(2)}) copy-start(f32[128]{0:T(128)} %param.10) | copy-start | bytes 1540
  8.7 2.0 %copy-start = (bf16[384,128]{1,0:T(8,128)(2,1)S(1)}, bf16[384,128]{1,0:T(8,128)(2,1)}, u32[]{:S(2)}) copy-start(bf16[384,128]{1,0:T(8,128)(2,1)} %gate_out_ref.1) | copy-start | bytes 294916
  9.4 14.6 %collective-permute-start.2 = (bf16[2,384,128]{2,1,0:T(8,128)(2,1)S(1)}, bf16[2,384,128]{2,1,0:T(8,128)(2,1)S(1)}, u32[]{:S(2)}, u32[]{:S(2)}) collective-permute-start(bf16[2,384,128]{2,1,0:T(8,128)(2,1)S(1)} %get-tuple-element.25.cots_ref), channel_id=1, source_target_pairs={{4,0},{8,4},{12,8},{16,12},{20,16},{24,20},{28,24},{5,1},{9,5},{13... | collective-permute-start | bytes 589832 | tf_op jit(solution)/shard_map/ppermute | solution.py:22
  12.1 14.7 %all-to-all-start = ((f32[32,1,256]{2,1,0:T(1,128)}), f32[32,1,256]{2,1,0:T(1,128)S(1)}, u32[]{:S(2)}, u32[]{:S(2)}) async-start(f32[32,1,256]{2,1,0:T(1,128)} %get-tuple-element.23), calls=%async_computation | async-start | bytes 65536 | tf_op jit(solution)/shard_map/all_to_all | solution.py:205
  20.3 6.0 %collective-permute-start.3 = (bf16[384,128]{1,0:T(8,128)(2,1)S(1)}, bf16[384,128]{1,0:T(8,128)(2,1)S(1)}, u32[]{:S(2)}, u32[]{:S(2)}) collective-permute-start(bf16[384,128]{1,0:T(8,128)(2,1)S(1)} %bitcast.15), channel_id=1, source_target_pairs={{0,8},{4,12},{8,16},{12,20},{16,24},{20,28},{1,9},{5,13},{9,17},{1... | collective-permute-start | bytes 294920 | tf_op jit(solution)/shard_map/ppermute | solution.py:22
  26.4 1.0 %copy-start.1 = (bf16[384,128]{1,0:T(8,128)(2,1)}, bf16[384,128]{1,0:T(8,128)(2,1)S(1)}, u32[]{:S(2)}) copy-start(bf16[384,128]{1,0:T(8,128)(2,1)S(1)} %fusion.1.layer_out_ref) | copy-start | bytes 294916

commit v3 on v2

--- a/solution.py
+++ b/solution.py
@@ -20,6 +20,11 @@
     length = lax.axis_size(axis)
     pairs = [(i, i + by) for i in range(length) if 0 <= i + by < length]
     return lax.ppermute(value, axis, pairs)
+
+
+def rotated(value, axis, by):
+    length = lax.axis_size(axis)
+    return lax.ppermute(value, axis, [(i, (i + by) % length) for i in range(length)])
 
 
 def doc_masks(lengths_ref, offsets, chans):
@@ -50,45 +55,57 @@
 
 def lag_kernel(
     lengths_ref, flipped_ref, before_ref, cots_ref, gate_out_ref, parts_ref, sources_ref,
-    *, owned, copies, scale,
+    *, owned, copies, scale, shards,
 ):
     del gate_out_ref
     evens, rows, chans = cots_ref.shape
     blocks = rows // TILE
-    count = 2 * evens * blocks
     masks = doc_masks(lengths_ref, [-1] + [2 * e for e in range(1, evens)], chans)
     before = before_ref[...] * masks[0]
     sources = [block[at : at + TILE] for block in (before, flipped_ref[...]) for at in range(0, rows, TILE)]
+    zero = jnp.zeros((chans, TILE), BF16)
+
+    def write_parts(used):
+        wide = []
+        for e in range(used):
+            cots = cots_ref[e] if e == 0 else cots_ref[e] * masks[e]
+            tiles = [cots[at : at + TILE].astype(F32).T.astype(BF16) for at in range(0, rows, TILE)]
+            tiles = [zero] + tiles + [zero]
+            wide += [jnp.concatenate(tiles[n : n + 2], axis=0) for n in range(blocks + 1)]
+        wide = jnp.concatenate(wide, axis=1)
+        sums = [None] * (2 * used * blocks)
+        for x in range(0, 2 * blocks, 2):
+            source = jnp.concatenate(sources[x : x + 2], axis=1)
+            product = jnp.dot(source, wide, preferred_element_type=F32)
+            for e in range(used):
+                for n in range(blocks + 1):
+                    d = 2 * blocks * e + n - 1 + blocks - x
+                    if d >= 0:
+                        at = (e * (blocks + 1) + n) * TILE
+                        piece = product[:, at : at + TILE]
+                        sums[d] = piece if sums[d] is None else sums[d] + piece
+        row = lax.broadcasted_iota(jnp.int32, (TILE, TILE), 0)
+        col = lax.broadcasted_iota(jnp.int32, (TILE, TILE), 1)
+        sums[0] = jnp.where(row + col >= TILE - 1, sums[0], 0.0)
+        width = len(sums) * TILE
+        skewed = pltpu.roll(jnp.concatenate(sums, axis=1), width - TILE + 1, 1, stride=1, stride_axis=0)
+        lags = jnp.sum(skewed, axis=0, keepdims=True) * scale
+        for p in range(parts_ref.shape[0] // copies):
+            some = min(max(width - p * owned, 0), owned)
+            pieces = [lags[:, p * owned : p * owned + some]] if some > 0 else []
+            pieces += [jnp.zeros((1, owned - some), F32)] if some < owned else []
+            piece = pieces[0] if len(pieces) == 1 else jnp.concatenate(pieces, axis=1)
+            for q in range(copies):
+                parts_ref[p * copies + q, :, :owned] = piece
+
+    if evens == 1:
+        write_parts(1)
+    else:
+        later = lax.axis_index("seq") + 2 < shards
+        pl.when(later)(functools.partial(write_parts, evens))
+        pl.when(jnp.logical_not(later))(functools.partial(write_parts, 1))
     for n, tile in enumerate(sources[::-1]):
         sources_ref[n * TILE : (n + 1) * TILE, :] = tile
-    zero = jnp.zeros((TILE, chans), BF16)
-    wide = []
-    for e in range(evens):
-        cots = cots_ref[e] if e == 0 else cots_ref[e] * masks[e]
-        tiles = [zero] + [cots[at : at + TILE] for at in range(0, rows, TILE)] + [zero]
-        wide += [jnp.concatenate(tiles[n : n + 2], axis=1) for n in range(blocks + 1)]
-    wide = jnp.concatenate(wide, axis=0)
-    sums = [None] * count
-    for x in range(0, 2 * blocks, 2):
-        source = jnp.concatenate(sources[x : x + 2], axis=1)
-        product = lax.dot_general(source, wide, (((1,), (1,)), ((), ())), preferred_element_type=F32)
-        for e in range(evens):
-            for n in range(blocks + 1):
-                d = 2 * blocks * e + n - 1 + blocks - x
-                if d >= 0:
-                    at = (e * (blocks + 1) + n) * TILE
-                    piece = product[:, at : at + TILE]
-                    sums[d] = piece if sums[d] is None else sums[d] + piece
-    row = lax.broadcasted_iota(jnp.int32, (TILE, TILE), 0)
-    col = lax.broadcasted_iota(jnp.int32, (TILE, TILE), 1)
-    sums[0] = jnp.where(row + col >= TILE - 1, sums[0], 0.0)
-    width = count * TILE
-    skewed = pltpu.roll(jnp.concatenate(sums, axis=1), width - TILE + 1, 1, stride=1, stride_axis=0)
-    lags = jnp.sum(skewed, axis=0, keepdims=True) * scale
-    for p in range(width // owned):
-        piece = lags[:, p * owned : (p + 1) * owned]
-        for q in range(copies):
-            parts_ref[p * copies + q, :, :owned] = piece
 
 
 def ahead_kernel(lengths_ref, taps_ref, sources_ref, later_ref, earlier_ref, ahead_ref):
@@ -163,6 +180,7 @@
     shards, groups = lax.axis_size("seq"), lax.axis_size("ch")
     block = jax.ShapeDtypeStruct((rows, chans), BF16)
     cot_gated = (cotangent.astype(F32) * gate_out.astype(F32)).astype(BF16)
+    gate_in, cot_gated = lax.optimization_barrier((gate_in, cot_gated))
     gated = (gate_in.astype(F32) * value_proj.astype(F32)).astype(BF16)
     flipped = gated.reshape(rows // TILE, TILE, chans)[:, ::-1].reshape(rows, chans)
 
@@ -171,11 +189,11 @@
     while span > 2:
         span //= 2
         future = jnp.concatenate([future, shifted(future, "seq", -span)], axis=0)
-    before = shifted(flipped, "seq", 1)
+    before = rotated(flipped, "seq", 1)
     bits = max(future.shape[0].bit_length() - 1, 1)
     order = sorted(range(future.shape[0]), key=lambda n: int(format(n, f"0{bits}b")[::-1], 2))
     evens = future if len(order) <= 2 else jnp.stack([future[n] for n in order])
-    odds = shifted(evens, "seq", -1)
+    odds = rotated(evens, "seq", -1)
     future = jnp.stack([evens, odds], axis=1).reshape(longest, rows, chans)
 
     lengths, skip = pl.pallas_call(
@@ -191,7 +209,7 @@
     owned = maxlag // shards
     grad_scale = 1.0 / math.sqrt(shards * rows * chans * groups)
     parts, sources = pl.pallas_call(
-        functools.partial(lag_kernel, owned=owned, copies=groups, scale=grad_scale),
+        functools.partial(lag_kernel, owned=owned, copies=groups, scale=grad_scale, shards=shards),
         out_shape=(
             jax.ShapeDtypeStruct((shards * groups, 1, -(-owned // TILE) * TILE), F32),
             jax.ShapeDtypeStruct((2 * rows, chans), BF16),

time: 27.7 us -> 26.7 us (0.964)
  starting transfers between devices: 18.5 us -> 14.2 us
  waiting for transfers between devices: 2 us -> 5.44 us
    ppermute x0 -> x2, starting transfers between devices: none -> 6.75 us  [rotated(): lax.ppermute(value, axis, [(i, (i + by) % length) for i in range(length)])]
    ppermute x4 -> x2, starting transfers between devices: 11.1 us -> 4.89 us  [shifted(): return lax.ppermute(value, axis, pairs)]
    all_to_all x1, starting transfers between devices: 7.43 us -> 2.55 us  [body(): gathered = lax.all_to_all(parts, ('seq', 'ch'), 0, 0, tiled=True)]
    ppermute x4 -> x2, waiting for transfers between devices: 1.6 us -> 3.47 us  [shifted(): return lax.ppermute(value, axis, pairs)]
    ppermute x0 -> x2, waiting for transfers between devices: none -> 1.48 us  [rotated(): lax.ppermute(value, axis, [(i, (i + by) % length) for i in range(length)])]
    broadcast_in_dim x1 -> x0, other arithmetic: 1.01 us -> none  [body(): future = cot_gated[None]]
    convert_element_type x0 -> x1, other arithmetic: none -> 1.01 us  [body(): cot_gated = (cotangent.astype(F32) * gate_out.astype(F32)).astype(BF16)]
  transfers between devices with their start and end apart: 5 -> 5, of which waited for: 3 -> 4; matrix products, arithmetic and copies ran while one was open for 1% -> 1% of each run, Pallas kernels for 13% -> 13%
where the time goes in v3:
time: 26.7 us; the launch traced here: 26.5 us
  starting transfers between devices  14.2 us (53%)
  waiting for transfers between devices  5.44 us (20%)
  Pallas kernels  4.1 us (15%)
  other arithmetic  1.15 us (4%)
  local copies, waits for them, and re-layouts  0.84 us (3%)
  between operations  0.78 us (3%)
    ppermute x2, starting transfers between devices, rotated(): lax.ppermute(value, axis, [(i, (i + by) % length) for i in range(length)])  6.75 us
    ppermute x2, starting transfers between devices, shifted(): return lax.ppermute(value, axis, pairs)  4.89 us
    ppermute x2, waiting for transfers between devices, shifted(): return lax.ppermute(value, axis, pairs)  3.47 us
    all_to_all x1, starting transfers between devices, body(): gathered = lax.all_to_all(parts, ('seq', 'ch'), 0, 0, tiled=True)  2.55 us
    ppermute x2, waiting for transfers between devices, rotated(): lax.ppermute(value, axis, [(i, (i + by) % length) for i in range(length)])  1.48 us
    pallas_call x1, Pallas kernels, body(): pl.pallas_call(functools.partial(lag_kernel, owned=owned, copies=groups,...  1.44 us
    pallas_call x1, Pallas kernels, body(): pl.pallas_call(near_kernel, out_shape=(jax.ShapeDtypeStruct((rows, chans)...  1.31 us
    convert_element_type x1, other arithmetic, body(): cot_gated = (cotangent.astype(F32) * gate_out.astype(F32)).astype(BF16)  1.01 us
  transfers between devices with their start and end apart: 5, of which 4 were waited for; matrix products, arithmetic and copies ran while one was open for 1% of the time, Pallas kernels for 13%

profile of v3, /device:TPU:0, one launch (start us, length us, event | category | flops | bytes accessed | tf_op | source)
XLA Modules:
  0.0 26.5 jit_solution(10534849205690842278)
XLA Ops:
  0.6 0.0 copy-start.3
  0.6 0.0 copy-start.2
  0.7 1.0 %fusion = bf16[384,128]{1,0:T(8,128)(2,1)S(1)} fusion(bf16[384,128]{1,0:T(8,128)(2,1)} %gate_out_ref.1, bf16[384,128]{1,0:T(8,128)(2,1)} %param.13), kind=kLoop, calls=%fused_computation.3 | loop fusion | flops 196608 | bytes 294912 | tf_op jit(solution)/shard_map/convert_element_type | solution.py:182
  1.7 1.3 %collective-permute-start.1 = (bf16[1,384,128]{2,1,0:T(8,128)(2,1)S(1)}, bf16[1,384,128]{2,1,0:T(8,128)(2,1)S(1)}, u32[]{:S(2)}, u32[]{:S(2)}) collective-permute-start(bf16[1,384,128]{2,1,0:T(8,128)(2,1)S(1)} %bitcast.17), channel_id=1, source_target_pairs={{8,0},{12,4},{16,8},{20,12},{24,16},{28,20},{9,1},{13,5},{17,9},{2... | collective-permute-start | bytes 294920 | tf_op jit(solution)/shard_map/ppermute | solution.py:22
  3.0 0.0 copy-done.3
  3.0 0.0 copy-done.2
  3.0 0.0 copy-start.6
  3.0 0.1 rev.3
  3.2 3.0 %collective-permute-start = (bf16[384,128]{1,0:T(8,128)(2,1)S(1)}, bf16[384,128]{1,0:T(8,128)(2,1)S(1)}, u32[]{:S(2)}, u32[]{:S(2)}) collective-permute-start(bf16[384,128]{1,0:T(8,128)(2,1)S(1)} %bitcast.12), channel_id=1, source_target_pairs={{0,4},{4,8},{8,12},{12,16},{16,20},{20,24},{24,28},{28,0},{1,5},{5... | collective-permute-start | bytes 294920 | tf_op jit(solution)/shard_map/ppermute | solution.py:27
  6.2 0.0 copy-done.6
  6.2 0.0 copy-start.4
  6.2 0.0 copy-start.5
  6.2 0.6 %copy-done.4 = s32[3]{0:T(128)S(1)} copy-done((s32[3]{0:T(128)S(1)}, s32[3]{0:T(128)}, u32[]{:S(2)}) %copy-start.4) | copy-done | bytes 36
  6.8 0.0 copy-done.5
  6.8 0.0 copy-start
  6.8 2.5 %collective-permute-done.1 = bf16[1,384,128]{2,1,0:T(8,128)(2,1)S(1)} collective-permute-done((bf16[1,384,128]{2,1,0:T(8,128)(2,1)S(1)}, bf16[1,384,128]{2,1,0:T(8,128)(2,1)S(1)}, u32[]{:S(2)}, u32[]{:S(2)}) %collective-permute-start.1) | collective-permute-done | bytes 98336 | tf_op jit(solution)/shard_map/ppermute | solution.py:22
  9.4 3.8 %collective-permute-start.2 = (bf16[2,384,128]{2,1,0:T(8,128)(2,1)S(1)}, bf16[2,384,128]{2,1,0:T(8,128)(2,1)S(1)}, u32[]{:S(2)}, u32[]{:S(2)}) collective-permute-start(bf16[2,384,128]{2,1,0:T(8,128)(2,1)S(1)} %get-tuple-element.29.cots_ref), channel_id=1, source_target_pairs={{0,28},{4,0},{8,4},{12,8},{16,12},{20,16},{24,20},{28,24},{1,29},{... | collective-permute-start | bytes 589832 | tf_op jit(solution)/shard_map/ppermute | solution.py:27
  13.2 1.5 %collective-permute-done.before_ref = bf16[384,128]{1,0:T(8,128)(2,1)S(1)} collective-permute-done((bf16[384,128]{1,0:T(8,128)(2,1)S(1)}, bf16[384,128]{1,0:T(8,128)(2,1)S(1)}, u32[]{:S(2)}, u32[]{:S(2)}) %collective-permute-start) | collective-permute-done | bytes 98336 | tf_op jit(solution)/shard_map/ppermute | solution.py:27
  14.7 0.0 copy-done
  14.7 1.4 %lags.1 = (f32[32,1,256]{2,1,0:T(1,128)}, bf16[768,128]{1,0:T(8,128)(2,1)S(1)}) custom-call(s32[1,3]{1,0:T(1,128)S(1)} %get-tuple-element.16.lengths_ref, bf16[384,128]{1,0:T(8,128)(2,1)S(1)} %bitcast.13, bf16[384,128]{1,0:T(8,128)(2,1)S(1)} %collective-permute-done.before_ref, bf16[2,384,128]{2,1,0:T(8,128)(2,1)S(1)} %get-tuple-element.29.cots_ref, ...), custom_call_target="tpu_custom_call" | custom-call | flops 10000000000 | bytes 1048576 | tf_op jit(solution)/shard_map/lags/pallas_call | solution.py:211
  16.1 2.5 %all-to-all-start = ((f32[32,1,256]{2,1,0:T(1,128)}), f32[32,1,256]{2,1,0:T(1,128)S(1)}, u32[]{:S(2)}, u32[]{:S(2)}) async-start(f32[32,1,256]{2,1,0:T(1,128)} %get-tuple-element.27), calls=%async_computation | async-start | bytes 65536 | tf_op jit(solution)/shard_map/all_to_all | solution.py:223
  18.7 0.8 %ahead.1 = (bf16[128,1536]{1,0:T(8,128)(2,1)S(1)}, bf16[128,1536]{1,0:T(8,128)(2,1)S(1)}, bf16[1,384,128]{2,1,0:T(8,128)(2,1)S(1)}) custom-call(s32[1,3]{1,0:T(1,128)S(1)} %get-tuple-element.16.lengths_ref, f32[1,1536]{1,0:T(1,128)S(1)} %reshape.28.taps_ref, bf16[768,128]{1,0:T(8,128)(2,1)S(1)} %get-tuple-element.20.sources_ref), custom_call_target="tpu_custom_call" | custom-call | tf_op jit(solution)/shard_map/ahead/pallas_call | solution.py:227
  19.4 3.6 %collective-permute-start.3 = (bf16[384,128]{1,0:T(8,128)(2,1)S(1)}, bf16[384,128]{1,0:T(8,128)(2,1)S(1)}, u32[]{:S(2)}, u32[]{:S(2)}) collective-permute-start(bf16[384,128]{1,0:T(8,128)(2,1)S(1)} %bitcast.14), channel_id=1, source_target_pairs={{0,8},{4,12},{8,16},{12,20},{16,24},{20,28},{1,9},{5,13},{9,17},{1... | collective-permute-start | bytes 294920 | tf_op jit(solution)/shard_map/ppermute | solution.py:22
  23.0 0.0 collective-permute-done.2
  23.1 1.3 %near.1 = (f32[384,128]{1,0:T(8,128)S(1)}, bf16[384,128]{1,0:T(8,128)(2,1)}, bf16[384,128]{1,0:T(8,128)(2,1)}) custom-call(s32[1,3]{1,0:T(1,128)S(1)} %get-tuple-element.16.lengths_ref, bf16[384,128]{1,0:T(8,128)(2,1)S(1)} %copy-done.2, bf16[384,128]{1,0:T(8,128)(2,1)S(1)} %copy-done.3, f32[1,128]{1,0:T(1,128)S(1)} %get-tuple-element.18.skip_ref, ...), custom_call_target="tpu_custom_call" | custom-call | flops 10000000000 | bytes 1048576 | tf_op jit(solution)/shard_map/near/pallas_call | solution.py:237
  24.4 0.9 %collective-permute-done.3 = bf16[384,128]{1,0:T(8,128)(2,1)S(1)} collective-permute-done((bf16[384,128]{1,0:T(8,128)(2,1)S(1)}, bf16[384,128]{1,0:T(8,128)(2,1)S(1)}, u32[]{:S(2)}, u32[]{:S(2)}) %collective-permute-start.3) | collective-permute-done | bytes 98336 | tf_op jit(solution)/shard_map/ppermute | solution.py:22
  25.4 0.0 copy-start.1
  25.4 0.5 %all-to-all-done.gathered_ref = f32[32,1,256]{2,1,0:T(1,128)S(1)} async-done(((f32[32,1,256]{2,1,0:T(1,128)}), f32[32,1,256]{2,1,0:T(1,128)S(1)}, u32[]{:S(2)}, u32[]{:S(2)}) %all-to-all-start) | async-done | bytes 32800 | tf_op jit(solution)/shard_map/all_to_all | solution.py:223
  25.9 0.6 %sum.1 = f32[1,192]{1,0:T(1,128)} custom-call(f32[32,1,256]{2,1,0:T(1,128)S(1)} %all-to-all-done.gathered_ref, bf16[384,128]{1,0:T(8,128)(2,1)S(1)} %fusion.1.layer_out_ref), custom_call_target="tpu_custom_call" | custom-call | tf_op jit(solution)/shard_map/sum/pallas_call | solution.py:248
  26.5 0.0 copy-done.1
  (7 shorter events, 0.2 us)
Async XLA Ops:
  0.6 2.3 %copy-start.3 = (bf16[384,128]{1,0:T(8,128)(2,1)S(1)}, bf16[384,128]{1,0:T(8,128)(2,1)}, u32[]{:S(2)}) copy-start(bf16[384,128]{1,0:T(8,128)(2,1)} %gate_in_ref) | copy-start | bytes 294916
  0.6 2.3 %copy-start.2 = (bf16[384,128]{1,0:T(8,128)(2,1)S(1)}, bf16[384,128]{1,0:T(8,128)(2,1)}, u32[]{:S(2)}) copy-start(bf16[384,128]{1,0:T(8,128)(2,1)} %value_ref.1) | copy-start | bytes 294916
  1.7 7.7 %collective-permute-start.1 = (bf16[1,384,128]{2,1,0:T(8,128)(2,1)S(1)}, bf16[1,384,128]{2,1,0:T(8,128)(2,1)S(1)}, u32[]{:S(2)}, u32[]{:S(2)}) collective-permute-start(bf16[1,384,128]{2,1,0:T(8,128)(2,1)S(1)} %bitcast.17), channel_id=1, source_target_pairs={{8,0},{12,4},{16,8},{20,12},{24,16},{28,20},{9,1},{13,5},{17,9},{2... | collective-permute-start | bytes 294920 | tf_op jit(solution)/shard_map/ppermute | solution.py:22
  3.0 3.1 %copy-start.6 = (f32[1536]{0:T(1024)S(1)}, f32[1536]{0:T(1024)}, u32[]{:S(2)}) copy-start(f32[1536]{0:T(1024)} %param.11) | copy-start | bytes 18436
  3.2 11.5 %collective-permute-start = (bf16[384,128]{1,0:T(8,128)(2,1)S(1)}, bf16[384,128]{1,0:T(8,128)(2,1)S(1)}, u32[]{:S(2)}, u32[]{:S(2)}) collective-permute-start(bf16[384,128]{1,0:T(8,128)(2,1)S(1)} %bitcast.12), channel_id=1, source_target_pairs={{0,4},{4,8},{8,12},{12,16},{16,20},{20,24},{24,28},{28,0},{1,5},{5... | collective-permute-start | bytes 294920 | tf_op jit(solution)/shard_map/ppermute | solution.py:27
  6.2 0.7 %copy-start.4 = (s32[3]{0:T(128)S(1)}, s32[3]{0:T(128)}, u32[]{:S(2)}) copy-start(s32[3]{0:T(128)} %param.12) | copy-start | bytes 40
  6.2 0.7 %copy-start.5 = (f32[128]{0:T(128)S(1)}, f32[128]{0:T(128)}, u32[]{:S(2)}) copy-start(f32[128]{0:T(128)} %param.10) | copy-start | bytes 1540
  6.8 7.8 %copy-start = (bf16[384,128]{1,0:T(8,128)(2,1)S(1)}, bf16[384,128]{1,0:T(8,128)(2,1)}, u32[]{:S(2)}) copy-start(bf16[384,128]{1,0:T(8,128)(2,1)} %gate_out_ref.1) | copy-start | bytes 294916
  9.4 13.6 %collective-permute-start.2 = (bf16[2,384,128]{2,1,0:T(8,128)(2,1)S(1)}, bf16[2,384,128]{2,1,0:T(8,128)(2,1)S(1)}, u32[]{:S(2)}, u32[]{:S(2)}) collective-permute-start(bf16[2,384,128]{2,1,0:T(8,128)(2,1)S(1)} %get-tuple-element.29.cots_ref), channel_id=1, source_target_pairs={{0,28},{4,0},{8,4},{12,8},{16,12},{20,16},{24,20},{28,24},{1,29},{... | collective-permute-start | bytes 589832 | tf_op jit(solution)/shard_map/ppermute | solution.py:27
  16.1 9.8 %all-to-all-start = ((f32[32,1,256]{2,1,0:T(1,128)}), f32[32,1,256]{2,1,0:T(1,128)S(1)}, u32[]{:S(2)}, u32[]{:S(2)}) async-start(f32[32,1,256]{2,1,0:T(1,128)} %get-tuple-element.27), calls=%async_computation | async-start | bytes 65536 | tf_op jit(solution)/shard_map/all_to_all | solution.py:223
  19.4 5.9 %collective-permute-start.3 = (bf16[384,128]{1,0:T(8,128)(2,1)S(1)}, bf16[384,128]{1,0:T(8,128)(2,1)S(1)}, u32[]{:S(2)}, u32[]{:S(2)}) collective-permute-start(bf16[384,128]{1,0:T(8,128)(2,1)S(1)} %bitcast.14), channel_id=1, source_target_pairs={{0,8},{4,12},{8,16},{12,20},{16,24},{20,28},{1,9},{5,13},{9,17},{1... | collective-permute-start | bytes 294920 | tf_op jit(solution)/shard_map/ppermute | solution.py:22
  25.4 1.1 %copy-start.1 = (bf16[384,128]{1,0:T(8,128)(2,1)}, bf16[384,128]{1,0:T(8,128)(2,1)S(1)}, u32[]{:S(2)}) copy-start(bf16[384,128]{1,0:T(8,128)(2,1)S(1)} %fusion.1.layer_out_ref) | copy-start | bytes 294916

commit v4 on v3

--- a/solution.py
+++ b/solution.py
@@ -48,19 +48,25 @@
     return (row + col == TILE - 1).astype(F32).astype(BF16)
 
 
-def stage_kernel(lengths_ref, skip_ref, lengths_out_ref, skip_out_ref):
+def stage_kernel(lengths_ref, skip_ref, cots_ref, lengths_out_ref, skip_out_ref, turned_ref, masks_ref):
     lengths_out_ref[...] = lengths_ref[...]
     skip_out_ref[...] = skip_ref[...]
+    rows, chans = cots_ref.shape
+    for at in range(0, rows, TILE):
+        turned_ref[:, at : at + TILE] = cots_ref[at : at + TILE, :].astype(F32).T.astype(BF16)
+    evens = masks_ref.shape[0]
+    for n, mask in enumerate(doc_masks(lengths_ref, [-1] + [2 * e for e in range(1, evens)], chans)):
+        masks_ref[n] = jnp.broadcast_to(mask.astype(F32), masks_ref.shape[1:])
 
 
 def lag_kernel(
-    lengths_ref, flipped_ref, before_ref, cots_ref, gate_out_ref, parts_ref, sources_ref,
+    masks_ref, flipped_ref, before_ref, turned_ref, cots_ref, gate_out_ref, parts_ref, sources_ref,
     *, owned, copies, scale, shards,
 ):
     del gate_out_ref
     evens, rows, chans = cots_ref.shape
     blocks = rows // TILE
-    masks = doc_masks(lengths_ref, [-1] + [2 * e for e in range(1, evens)], chans)
+    masks = [masks_ref[n, 0:1, :].astype(BF16) for n in range(evens)]
     before = before_ref[...] * masks[0]
     sources = [block[at : at + TILE] for block in (before, flipped_ref[...]) for at in range(0, rows, TILE)]
     zero = jnp.zeros((chans, TILE), BF16)
@@ -68,8 +74,11 @@
     def write_parts(used):
         wide = []
         for e in range(used):
-            cots = cots_ref[e] if e == 0 else cots_ref[e] * masks[e]
-            tiles = [cots[at : at + TILE].astype(F32).T.astype(BF16) for at in range(0, rows, TILE)]
+            if e == 0:
+                tiles = [turned_ref[:, at : at + TILE] for at in range(0, rows, TILE)]
+            else:
+                cots = cots_ref[e] * masks[e]
+                tiles = [cots[at : at + TILE].astype(F32).T.astype(BF16) for at in range(0, rows, TILE)]
             tiles = [zero] + tiles + [zero]
             wide += [jnp.concatenate(tiles[n : n + 2], axis=0) for n in range(blocks + 1)]
         wide = jnp.concatenate(wide, axis=1)
@@ -180,7 +189,6 @@
     shards, groups = lax.axis_size("seq"), lax.axis_size("ch")
     block = jax.ShapeDtypeStruct((rows, chans), BF16)
     cot_gated = (cotangent.astype(F32) * gate_out.astype(F32)).astype(BF16)
-    gate_in, cot_gated = lax.optimization_barrier((gate_in, cot_gated))
     gated = (gate_in.astype(F32) * value_proj.astype(F32)).astype(BF16)
     flipped = gated.reshape(rows // TILE, TILE, chans)[:, ::-1].reshape(rows, chans)
 
@@ -196,16 +204,19 @@
     odds = rotated(evens, "seq", -1)
     future = jnp.stack([evens, odds], axis=1).reshape(longest, rows, chans)
 
-    lengths, skip = pl.pallas_call(
+    lengths, skip, turned, masks = pl.pallas_call(
         stage_kernel,
         out_shape=(
-            jax.ShapeDtypeStruct((1, doc_lengths.shape[0]), jnp.int32), jax.ShapeDtypeStruct((1, chans), F32)
+            jax.ShapeDtypeStruct((1, doc_lengths.shape[0]), jnp.int32),
+            jax.ShapeDtypeStruct((1, chans), F32),
+            jax.ShapeDtypeStruct((chans, rows), BF16),
+            jax.ShapeDtypeStruct((evens.shape[0], 8, chans), F32),
         ),
-        in_specs=[VMEM] * 2,
-        out_specs=(VMEM,) * 2,
+        in_specs=[VMEM] * 3,
+        out_specs=(VMEM,) * 4,
         compiler_params=PARAMS,
         name="stage",
-    )(doc_lengths.reshape(1, -1), skip_gain.reshape(1, chans))
+    )(doc_lengths.reshape(1, -1), skip_gain.reshape(1, chans), cot_gated)
     owned = maxlag // shards
     grad_scale = 1.0 / math.sqrt(shards * rows * chans * groups)
     parts, sources = pl.pallas_call(
@@ -214,12 +225,12 @@
             jax.ShapeDtypeStruct((shards * groups, 1, -(-owned // TILE) * TILE), F32),
             jax.ShapeDtypeStruct((2 * rows, chans), BF16),
         ),
-        in_specs=[VMEM] * 5,
+        in_specs=[VMEM] * 6,
         out_specs=(VMEM,) * 2,
         compiler_params=PARAMS,
         cost_estimate=pl.CostEstimate(flops=LAGF, bytes_accessed=2**20, transcendentals=0),
         name="lags",
-    )(lengths, flipped, before, evens, gate_out)
+    )(masks, flipped, before, turned, evens, gate_out)
     gathered = lax.all_to_all(parts, ("seq", "ch"), 0, 0, tiled=True)
 
     band = jax.ShapeDtypeStruct((TILE, maxlag), BF16)

time: 26.7 us -> 26.6 us (level)
  no operation moved by 1% of the time
where the time goes in v4:
time: 26.6 us; the launch traced here: 26.4 us
  starting transfers between devices  14.2 us (53%)
  waiting for transfers between devices  5.3 us (20%)
  Pallas kernels  4.13 us (16%)
  other arithmetic  1.15 us (4%)
  local copies, waits for them, and re-layouts  0.84 us (3%)
  between operations  0.8 us (3%)
    ppermute x2, starting transfers between devices, rotated(): lax.ppermute(value, axis, [(i, (i + by) % length) for i in range(length)])  6.75 us
    ppermute x2, starting transfers between devices, shifted(): return lax.ppermute(value, axis, pairs)  4.89 us
    ppermute x2, waiting for transfers between devices, shifted(): return lax.ppermute(value, axis, pairs)  3.34 us
    all_to_all x1, starting transfers between devices, body(): gathered = lax.all_to_all(parts, ('seq', 'ch'), 0, 0, tiled=True)  2.55 us
    ppermute x2, waiting for transfers between devices, rotated(): lax.ppermute(value, axis, [(i, (i + by) % length) for i in range(length)])  1.48 us
    pallas_call x1, Pallas kernels, body(): pl.pallas_call(functools.partial(lag_kernel, owned=owned, copies=groups,...  1.34 us
    pallas_call x1, Pallas kernels, body(): pl.pallas_call(near_kernel, out_shape=(jax.ShapeDtypeStruct((rows, chans)...  1.31 us
    convert_element_type x1, other arithmetic, body(): cot_gated = (cotangent.astype(F32) * gate_out.astype(F32)).astype(BF16)  1.01 us
  transfers between devices with their start and end apart: 5, of which 4 were waited for; matrix products, arithmetic and copies ran while one was open for 1% of the time, Pallas kernels for 13%

profile of v4, /device:TPU:0, one launch (start us, length us, event | category | flops | bytes accessed | tf_op | source)
XLA Modules:
  0.0 26.4 jit_solution(7062120754877397370)
XLA Ops:
  0.6 0.0 copy-start.3
  0.6 0.0 copy-start.2
  0.7 1.0 %fusion.cots_ref = bf16[384,128]{1,0:T(8,128)(2,1)S(1)} fusion(bf16[384,128]{1,0:T(8,128)(2,1)} %gate_out_ref.1, bf16[384,128]{1,0:T(8,128)(2,1)} %param.13), kind=kLoop, calls=%fused_computation.3 | loop fusion | flops 196608 | bytes 294912 | tf_op jit(solution)/shard_map/convert_element_type | solution.py:191
  1.7 1.3 %collective-permute-start.1 = (bf16[1,384,128]{2,1,0:T(8,128)(2,1)S(1)}, bf16[1,384,128]{2,1,0:T(8,128)(2,1)S(1)}, u32[]{:S(2)}, u32[]{:S(2)}) collective-permute-start(bf16[1,384,128]{2,1,0:T(8,128)(2,1)S(1)} %bitcast.11), channel_id=1, source_target_pairs={{8,0},{12,4},{16,8},{20,12},{24,16},{28,20},{9,1},{13,5},{17,9},{2... | collective-permute-start | bytes 294920 | tf_op jit(solution)/shard_map/ppermute | solution.py:22
  3.0 0.0 copy-done.3
  3.0 0.0 copy-done.2
  3.0 0.0 copy-start.6
  3.0 0.1 rev.3
  3.2 3.0 %collective-permute-start = (bf16[384,128]{1,0:T(8,128)(2,1)S(1)}, bf16[384,128]{1,0:T(8,128)(2,1)S(1)}, u32[]{:S(2)}, u32[]{:S(2)}) collective-permute-start(bf16[384,128]{1,0:T(8,128)(2,1)S(1)} %bitcast.14), channel_id=1, source_target_pairs={{0,4},{4,8},{8,12},{12,16},{16,20},{20,24},{24,28},{28,0},{1,5},{5... | collective-permute-start | bytes 294920 | tf_op jit(solution)/shard_map/ppermute | solution.py:27
  6.2 0.0 copy-done.6
  6.2 0.0 copy-start.4
  6.2 0.0 copy-start.5
  6.2 0.6 %copy-done.4 = s32[3]{0:T(128)S(1)} copy-done((s32[3]{0:T(128)S(1)}, s32[3]{0:T(128)}, u32[]{:S(2)}) %copy-start.4) | copy-done | bytes 36
  6.8 0.0 copy-done.5
  6.8 0.1 stage.1
  7.0 0.0 copy-start
  7.0 2.4 %collective-permute-done.1 = bf16[1,384,128]{2,1,0:T(8,128)(2,1)S(1)} collective-permute-done((bf16[1,384,128]{2,1,0:T(8,128)(2,1)S(1)}, bf16[1,384,128]{2,1,0:T(8,128)(2,1)S(1)}, u32[]{:S(2)}, u32[]{:S(2)}) %collective-permute-start.1) | collective-permute-done | bytes 98336 | tf_op jit(solution)/shard_map/ppermute | solution.py:22
  9.4 3.8 %collective-permute-start.2 = (bf16[2,384,128]{2,1,0:T(8,128)(2,1)S(1)}, bf16[2,384,128]{2,1,0:T(8,128)(2,1)S(1)}, u32[]{:S(2)}, u32[]{:S(2)}) collective-permute-start(bf16[2,384,128]{2,1,0:T(8,128)(2,1)S(1)} %get-tuple-element.29.cots_ref), channel_id=1, source_target_pairs={{0,28},{4,0},{8,4},{12,8},{16,12},{20,16},{24,20},{28,24},{1,29},{... | collective-permute-start | bytes 589832 | tf_op jit(solution)/shard_map/ppermute | solution.py:27
  13.2 1.5 %collective-permute-done.before_ref = bf16[384,128]{1,0:T(8,128)(2,1)S(1)} collective-permute-done((bf16[384,128]{1,0:T(8,128)(2,1)S(1)}, bf16[384,128]{1,0:T(8,128)(2,1)S(1)}, u32[]{:S(2)}, u32[]{:S(2)}) %collective-permute-start) | collective-permute-done | bytes 98336 | tf_op jit(solution)/shard_map/ppermute | solution.py:27
  14.7 0.0 copy-done
  14.7 1.3 %lags.1 = (f32[32,1,256]{2,1,0:T(1,128)}, bf16[768,128]{1,0:T(8,128)(2,1)S(1)}) custom-call(f32[2,8,128]{2,1,0:T(8,128)S(1)} %get-tuple-element.18.masks_ref, bf16[384,128]{1,0:T(8,128)(2,1)S(1)} %bitcast.15, bf16[384,128]{1,0:T(8,128)(2,1)S(1)} %collective-permute-done.before_ref, bf16[128,384]{1,0:T(8,128)(2,1)S(1)} %get-tuple-element.19.turned_ref, ...), custom_call_target="tpu_custom_call" | custom-call | flops 10000000000 | bytes 1048576 | tf_op jit(solution)/shard_map/lags/pallas_call | solution.py:222
  16.0 2.5 %all-to-all-start = ((f32[32,1,256]{2,1,0:T(1,128)}), f32[32,1,256]{2,1,0:T(1,128)S(1)}, u32[]{:S(2)}, u32[]{:S(2)}) async-start(f32[32,1,256]{2,1,0:T(1,128)} %get-tuple-element.27), calls=%async_computation | async-start | bytes 65536 | tf_op jit(solution)/shard_map/all_to_all | solution.py:234
  18.6 0.8 %ahead.1 = (bf16[128,1536]{1,0:T(8,128)(2,1)S(1)}, bf16[128,1536]{1,0:T(8,128)(2,1)S(1)}, bf16[1,384,128]{2,1,0:T(8,128)(2,1)S(1)}) custom-call(s32[1,3]{1,0:T(1,128)S(1)} %get-tuple-element.16.lengths_ref, f32[1,1536]{1,0:T(1,128)S(1)} %reshape.28.taps_ref, bf16[768,128]{1,0:T(8,128)(2,1)S(1)} %get-tuple-element.20.sources_ref), custom_call_target="tpu_custom_call" | custom-call | tf_op jit(solution)/shard_map/ahead/pallas_call | solution.py:238
  19.3 3.6 %collective-permute-start.3 = (bf16[384,128]{1,0:T(8,128)(2,1)S(1)}, bf16[384,128]{1,0:T(8,128)(2,1)S(1)}, u32[]{:S(2)}, u32[]{:S(2)}) collective-permute-start(bf16[384,128]{1,0:T(8,128)(2,1)S(1)} %bitcast.18), channel_id=1, source_target_pairs={{0,8},{4,12},{8,16},{12,20},{16,24},{20,28},{1,9},{5,13},{9,17},{1... | collective-permute-start | bytes 294920 | tf_op jit(solution)/shard_map/ppermute | solution.py:22
  22.9 0.0 collective-permute-done.2
  23.0 1.3 %near.1 = (f32[384,128]{1,0:T(8,128)S(1)}, bf16[384,128]{1,0:T(8,128)(2,1)}, bf16[384,128]{1,0:T(8,128)(2,1)}) custom-call(s32[1,3]{1,0:T(1,128)S(1)} %get-tuple-element.16.lengths_ref, bf16[384,128]{1,0:T(8,128)(2,1)S(1)} %copy-done.2, bf16[384,128]{1,0:T(8,128)(2,1)S(1)} %copy-done.3, f32[1,128]{1,0:T(1,128)S(1)} %get-tuple-element.17.skip_ref, ...), custom_call_target="tpu_custom_call" | custom-call | flops 10000000000 | bytes 1048576 | tf_op jit(solution)/shard_map/near/pallas_call | solution.py:248
  24.3 0.9 %collective-permute-done.3 = bf16[384,128]{1,0:T(8,128)(2,1)S(1)} collective-permute-done((bf16[384,128]{1,0:T(8,128)(2,1)S(1)}, bf16[384,128]{1,0:T(8,128)(2,1)S(1)}, u32[]{:S(2)}, u32[]{:S(2)}) %collective-permute-start.3) | collective-permute-done | bytes 98336 | tf_op jit(solution)/shard_map/ppermute | solution.py:22
  25.3 0.0 copy-start.1
  25.3 0.5 %all-to-all-done.gathered_ref = f32[32,1,256]{2,1,0:T(1,128)S(1)} async-done(((f32[32,1,256]{2,1,0:T(1,128)}), f32[32,1,256]{2,1,0:T(1,128)S(1)}, u32[]{:S(2)}, u32[]{:S(2)}) %all-to-all-start) | async-done | bytes 32800 | tf_op jit(solution)/shard_map/all_to_all | solution.py:234
  25.8 0.6 %sum.1 = f32[1,192]{1,0:T(1,128)} custom-call(f32[32,1,256]{2,1,0:T(1,128)S(1)} %all-to-all-done.gathered_ref, bf16[384,128]{1,0:T(8,128)(2,1)S(1)} %fusion.1.layer_out_ref), custom_call_target="tpu_custom_call" | custom-call | tf_op jit(solution)/shard_map/sum/pallas_call | solution.py:259
  26.4 0.0 copy-done.1
  (6 shorter events, 0.2 us)
Async XLA Ops:
  0.6 2.3 %copy-start.3 = (bf16[384,128]{1,0:T(8,128)(2,1)S(1)}, bf16[384,128]{1,0:T(8,128)(2,1)}, u32[]{:S(2)}) copy-start(bf16[384,128]{1,0:T(8,128)(2,1)} %gate_in_ref.1) | copy-start | bytes 294916
  0.6 2.3 %copy-start.2 = (bf16[384,128]{1,0:T(8,128)(2,1)S(1)}, bf16[384,128]{1,0:T(8,128)(2,1)}, u32[]{:S(2)}) copy-start(bf16[384,128]{1,0:T(8,128)(2,1)} %value_ref.1) | copy-start | bytes 294916
  1.7 7.7 %collective-permute-start.1 = (bf16[1,384,128]{2,1,0:T(8,128)(2,1)S(1)}, bf16[1,384,128]{2,1,0:T(8,128)(2,1)S(1)}, u32[]{:S(2)}, u32[]{:S(2)}) collective-permute-start(bf16[1,384,128]{2,1,0:T(8,128)(2,1)S(1)} %bitcast.11), channel_id=1, source_target_pairs={{8,0},{12,4},{16,8},{20,12},{24,16},{28,20},{9,1},{13,5},{17,9},{2... | collective-permute-start | bytes 294920 | tf_op jit(solution)/shard_map/ppermute | solution.py:22
  3.0 3.1 %copy-start.6 = (f32[1536]{0:T(1024)S(1)}, f32[1536]{0:T(1024)}, u32[]{:S(2)}) copy-start(f32[1536]{0:T(1024)} %param.11) | copy-start | bytes 18436
  3.2 11.5 %collective-permute-start = (bf16[384,128]{1,0:T(8,128)(2,1)S(1)}, bf16[384,128]{1,0:T(8,128)(2,1)S(1)}, u32[]{:S(2)}, u32[]{:S(2)}) collective-permute-start(bf16[384,128]{1,0:T(8,128)(2,1)S(1)} %bitcast.14), channel_id=1, source_target_pairs={{0,4},{4,8},{8,12},{12,16},{16,20},{20,24},{24,28},{28,0},{1,5},{5... | collective-permute-start | bytes 294920 | tf_op jit(solution)/shard_map/ppermute | solution.py:27
  6.2 0.7 %copy-start.4 = (s32[3]{0:T(128)S(1)}, s32[3]{0:T(128)}, u32[]{:S(2)}) copy-start(s32[3]{0:T(128)} %param.12) | copy-start | bytes 40
  6.2 0.7 %copy-start.5 = (f32[128]{0:T(128)S(1)}, f32[128]{0:T(128)}, u32[]{:S(2)}) copy-start(f32[128]{0:T(128)} %param.10) | copy-start | bytes 1540
  7.0 7.7 %copy-start = (bf16[384,128]{1,0:T(8,128)(2,1)S(1)}, bf16[384,128]{1,0:T(8,128)(2,1)}, u32[]{:S(2)}) copy-start(bf16[384,128]{1,0:T(8,128)(2,1)} %gate_out_ref.1) | copy-start | bytes 294916
  9.4 13.5 %collective-permute-start.2 = (bf16[2,384,128]{2,1,0:T(8,128)(2,1)S(1)}, bf16[2,384,128]{2,1,0:T(8,128)(2,1)S(1)}, u32[]{:S(2)}, u32[]{:S(2)}) collective-permute-start(bf16[2,384,128]{2,1,0:T(8,128)(2,1)S(1)} %get-tuple-element.29.cots_ref), channel_id=1, source_target_pairs={{0,28},{4,0},{8,4},{12,8},{16,12},{20,16},{24,20},{28,24},{1,29},{... | collective-permute-start | bytes 589832 | tf_op jit(solution)/shard_map/ppermute | solution.py:27
  16.0 9.8 %all-to-all-start = ((f32[32,1,256]{2,1,0:T(1,128)}), f32[32,1,256]{2,1,0:T(1,128)S(1)}, u32[]{:S(2)}, u32[]{:S(2)}) async-start(f32[32,1,256]{2,1,0:T(1,128)} %get-tuple-element.27), calls=%async_computation | async-start | bytes 65536 | tf_op jit(solution)/shard_map/all_to_all | solution.py:234
  19.3 5.9 %collective-permute-start.3 = (bf16[384,128]{1,0:T(8,128)(2,1)S(1)}, bf16[384,128]{1,0:T(8,128)(2,1)S(1)}, u32[]{:S(2)}, u32[]{:S(2)}) collective-permute-start(bf16[384,128]{1,0:T(8,128)(2,1)S(1)} %bitcast.18), channel_id=1, source_target_pairs={{0,8},{4,12},{8,16},{12,20},{16,24},{20,28},{1,9},{5,13},{9,17},{1... | collective-permute-start | bytes 294920 | tf_op jit(solution)/shard_map/ppermute | solution.py:22
  25.3 1.1 %copy-start.1 = (bf16[384,128]{1,0:T(8,128)(2,1)}, bf16[384,128]{1,0:T(8,128)(2,1)S(1)}, u32[]{:S(2)}) copy-start(bf16[384,128]{1,0:T(8,128)(2,1)S(1)} %fusion.1.layer_out_ref) | copy-start | bytes 294916

commit v5 on v4

--- a/solution.py
+++ b/solution.py
@@ -105,7 +105,7 @@
             pieces += [jnp.zeros((1, owned - some), F32)] if some < owned else []
             piece = pieces[0] if len(pieces) == 1 else jnp.concatenate(pieces, axis=1)
             for q in range(copies):
-                parts_ref[p * copies + q, :, :owned] = piece
+                parts_ref[q * shards + p, :, :owned] = piece
 
     if evens == 1:
         write_parts(1)
@@ -231,7 +231,7 @@
         cost_estimate=pl.CostEstimate(flops=LAGF, bytes_accessed=2**20, transcendentals=0),
         name="lags",
     )(masks, flipped, before, turned, evens, gate_out)
-    gathered = lax.all_to_all(parts, ("seq", "ch"), 0, 0, tiled=True)
+    gathered = lax.all_to_all(parts, ("ch", "seq"), 0, 0, tiled=True)
 
     band = jax.ShapeDtypeStruct((TILE, maxlag), BF16)
     further = longest // 2 - 1

time: 26.6 us -> 26.6 us (level)
  no operation moved by 1% of the time
where the time goes in v5:
time: 26.6 us; the launch traced here: 26.3 us
  starting transfers between devices  14.2 us (53%)
  waiting for transfers between devices  5.24 us (20%)
  Pallas kernels  4.13 us (16%)
  other arithmetic  1.15 us (4%)
  local copies, waits for them, and re-layouts  0.84 us (3%)
  between operations  0.8 us (3%)
    ppermute x2, starting transfers between devices, rotated(): lax.ppermute(value, axis, [(i, (i + by) % length) for i in range(length)])  6.75 us
    ppermute x2, starting transfers between devices, shifted(): return lax.ppermute(value, axis, pairs)  4.89 us
    ppermute x2, waiting for transfers between devices, shifted(): return lax.ppermute(value, axis, pairs)  3.34 us
    all_to_all x1, starting transfers between devices, body(): gathered = lax.all_to_all(parts, ('ch', 'seq'), 0, 0, tiled=True)  2.55 us
    ppermute x2, waiting for transfers between devices, rotated(): lax.ppermute(value, axis, [(i, (i + by) % length) for i in range(length)])  1.48 us
    pallas_call x1, Pallas kernels, body(): pl.pallas_call(functools.partial(lag_kernel, owned=owned, copies=groups,...  1.34 us
    pallas_call x1, Pallas kernels, body(): pl.pallas_call(near_kernel, out_shape=(jax.ShapeDtypeStruct((rows, chans)...  1.31 us
    convert_element_type x1, other arithmetic, body(): cot_gated = (cotangent.astype(F32) * gate_out.astype(F32)).astype(BF16)  1.01 us
  transfers between devices with their start and end apart: 5, of which 4 were waited for; matrix products, arithmetic and copies ran while one was open for 1% of the time, Pallas kernels for 13%

profile of v5, /device:TPU:0, one launch (start us, length us, event | category | flops | bytes accessed | tf_op | source)
XLA Modules:
  0.0 26.3 jit_solution(2896229362076490900)
XLA Ops:
  0.6 0.0 copy-start.3
  0.6 0.0 copy-start.2
  0.7 1.0 %fusion.cots_ref = bf16[384,128]{1,0:T(8,128)(2,1)S(1)} fusion(bf16[384,128]{1,0:T(8,128)(2,1)} %gate_out_ref.1, bf16[384,128]{1,0:T(8,128)(2,1)} %param.13), kind=kLoop, calls=%fused_computation.3 | loop fusion | flops 196608 | bytes 294912 | tf_op jit(solution)/shard_map/convert_element_type | solution.py:191
  1.7 1.3 %collective-permute-start.1 = (bf16[1,384,128]{2,1,0:T(8,128)(2,1)S(1)}, bf16[1,384,128]{2,1,0:T(8,128)(2,1)S(1)}, u32[]{:S(2)}, u32[]{:S(2)}) collective-permute-start(bf16[1,384,128]{2,1,0:T(8,128)(2,1)S(1)} %bitcast.11), channel_id=1, source_target_pairs={{8,0},{12,4},{16,8},{20,12},{24,16},{28,20},{9,1},{13,5},{17,9},{2... | collective-permute-start | bytes 294920 | tf_op jit(solution)/shard_map/ppermute | solution.py:22
  3.0 0.0 copy-done.3
  3.0 0.0 copy-done.2
  3.0 0.0 copy-start.6
  3.0 0.1 rev.3
  3.2 3.0 %collective-permute-start = (bf16[384,128]{1,0:T(8,128)(2,1)S(1)}, bf16[384,128]{1,0:T(8,128)(2,1)S(1)}, u32[]{:S(2)}, u32[]{:S(2)}) collective-permute-start(bf16[384,128]{1,0:T(8,128)(2,1)S(1)} %bitcast.14), channel_id=1, source_target_pairs={{0,4},{4,8},{8,12},{12,16},{16,20},{20,24},{24,28},{28,0},{1,5},{5... | collective-permute-start | bytes 294920 | tf_op jit(solution)/shard_map/ppermute | solution.py:27
  6.2 0.0 copy-done.6
  6.2 0.0 copy-start.4
  6.2 0.0 copy-start.5
  6.2 0.6 %copy-done.4 = s32[3]{0:T(128)S(1)} copy-done((s32[3]{0:T(128)S(1)}, s32[3]{0:T(128)}, u32[]{:S(2)}) %copy-start.4) | copy-done | bytes 36
  6.8 0.0 copy-done.5
  6.8 0.1 stage.1
  7.0 0.0 copy-start
  7.0 2.4 %collective-permute-done.1 = bf16[1,384,128]{2,1,0:T(8,128)(2,1)S(1)} collective-permute-done((bf16[1,384,128]{2,1,0:T(8,128)(2,1)S(1)}, bf16[1,384,128]{2,1,0:T(8,128)(2,1)S(1)}, u32[]{:S(2)}, u32[]{:S(2)}) %collective-permute-start.1) | collective-permute-done | bytes 98336 | tf_op jit(solution)/shard_map/ppermute | solution.py:22
  9.4 3.8 %collective-permute-start.2 = (bf16[2,384,128]{2,1,0:T(8,128)(2,1)S(1)}, bf16[2,384,128]{2,1,0:T(8,128)(2,1)S(1)}, u32[]{:S(2)}, u32[]{:S(2)}) collective-permute-start(bf16[2,384,128]{2,1,0:T(8,128)(2,1)S(1)} %get-tuple-element.29.cots_ref), channel_id=1, source_target_pairs={{0,28},{4,0},{8,4},{12,8},{16,12},{20,16},{24,20},{28,24},{1,29},{... | collective-permute-start | bytes 589832 | tf_op jit(solution)/shard_map/ppermute | solution.py:27
  13.2 1.5 %collective-permute-done.before_ref = bf16[384,128]{1,0:T(8,128)(2,1)S(1)} collective-permute-done((bf16[384,128]{1,0:T(8,128)(2,1)S(1)}, bf16[384,128]{1,0:T(8,128)(2,1)S(1)}, u32[]{:S(2)}, u32[]{:S(2)}) %collective-permute-start) | collective-permute-done | bytes 98336 | tf_op jit(solution)/shard_map/ppermute | solution.py:27
  14.7 0.0 copy-done
  14.7 1.3 %lags.1 = (f32[32,1,256]{2,1,0:T(1,128)}, bf16[768,128]{1,0:T(8,128)(2,1)S(1)}) custom-call(f32[2,8,128]{2,1,0:T(8,128)S(1)} %get-tuple-element.18.masks_ref, bf16[384,128]{1,0:T(8,128)(2,1)S(1)} %bitcast.15, bf16[384,128]{1,0:T(8,128)(2,1)S(1)} %collective-permute-done.before_ref, bf16[128,384]{1,0:T(8,128)(2,1)S(1)} %get-tuple-element.19.turned_ref, ...), custom_call_target="tpu_custom_call" | custom-call | flops 10000000000 | bytes 1048576 | tf_op jit(solution)/shard_map/lags/pallas_call | solution.py:222
  16.0 2.5 %all-to-all-start = ((f32[32,1,256]{2,1,0:T(1,128)}), f32[32,1,256]{2,1,0:T(1,128)S(1)}, u32[]{:S(2)}, u32[]{:S(2)}) async-start(f32[32,1,256]{2,1,0:T(1,128)} %get-tuple-element.27), calls=%async_computation | async-start | bytes 65536 | tf_op jit(solution)/shard_map/all_to_all | solution.py:234
  18.6 0.8 %ahead.1 = (bf16[128,1536]{1,0:T(8,128)(2,1)S(1)}, bf16[128,1536]{1,0:T(8,128)(2,1)S(1)}, bf16[1,384,128]{2,1,0:T(8,128)(2,1)S(1)}) custom-call(s32[1,3]{1,0:T(1,128)S(1)} %get-tuple-element.16.lengths_ref, f32[1,1536]{1,0:T(1,128)S(1)} %reshape.28.taps_ref, bf16[768,128]{1,0:T(8,128)(2,1)S(1)} %get-tuple-element.20.sources_ref), custom_call_target="tpu_custom_call" | custom-call | tf_op jit(solution)/shard_map/ahead/pallas_call | solution.py:238
  19.3 3.6 %collective-permute-start.3 = (bf16[384,128]{1,0:T(8,128)(2,1)S(1)}, bf16[384,128]{1,0:T(8,128)(2,1)S(1)}, u32[]{:S(2)}, u32[]{:S(2)}) collective-permute-start(bf16[384,128]{1,0:T(8,128)(2,1)S(1)} %bitcast.18), channel_id=1, source_target_pairs={{0,8},{4,12},{8,16},{12,20},{16,24},{20,28},{1,9},{5,13},{9,17},{1... | collective-permute-start | bytes 294920 | tf_op jit(solution)/shard_map/ppermute | solution.py:22
  22.9 0.0 collective-permute-done.2
  23.0 1.3 %near.1 = (f32[384,128]{1,0:T(8,128)S(1)}, bf16[384,128]{1,0:T(8,128)(2,1)}, bf16[384,128]{1,0:T(8,128)(2,1)}) custom-call(s32[1,3]{1,0:T(1,128)S(1)} %get-tuple-element.16.lengths_ref, bf16[384,128]{1,0:T(8,128)(2,1)S(1)} %copy-done.2, bf16[384,128]{1,0:T(8,128)(2,1)S(1)} %copy-done.3, f32[1,128]{1,0:T(1,128)S(1)} %get-tuple-element.17.skip_ref, ...), custom_call_target="tpu_custom_call" | custom-call | flops 10000000000 | bytes 1048576 | tf_op jit(solution)/shard_map/near/pallas_call | solution.py:248
  24.3 0.9 %collective-permute-done.3 = bf16[384,128]{1,0:T(8,128)(2,1)S(1)} collective-permute-done((bf16[384,128]{1,0:T(8,128)(2,1)S(1)}, bf16[384,128]{1,0:T(8,128)(2,1)S(1)}, u32[]{:S(2)}, u32[]{:S(2)}) %collective-permute-start.3) | collective-permute-done | bytes 98336 | tf_op jit(solution)/shard_map/ppermute | solution.py:22
  25.3 0.0 copy-start.1
  25.3 0.4 %all-to-all-done.gathered_ref = f32[32,1,256]{2,1,0:T(1,128)S(1)} async-done(((f32[32,1,256]{2,1,0:T(1,128)}), f32[32,1,256]{2,1,0:T(1,128)S(1)}, u32[]{:S(2)}, u32[]{:S(2)}) %all-to-all-start) | async-done | bytes 32800 | tf_op jit(solution)/shard_map/all_to_all | solution.py:234
  25.7 0.6 %sum.1 = f32[1,192]{1,0:T(1,128)} custom-call(f32[32,1,256]{2,1,0:T(1,128)S(1)} %all-to-all-done.gathered_ref, bf16[384,128]{1,0:T(8,128)(2,1)S(1)} %fusion.1.layer_out_ref), custom_call_target="tpu_custom_call" | custom-call | tf_op jit(solution)/shard_map/sum/pallas_call | solution.py:259
  26.3 0.0 copy-done.1
  (6 shorter events, 0.2 us)
Async XLA Ops:
  0.6 2.3 %copy-start.3 = (bf16[384,128]{1,0:T(8,128)(2,1)S(1)}, bf16[384,128]{1,0:T(8,128)(2,1)}, u32[]{:S(2)}) copy-start(bf16[384,128]{1,0:T(8,128)(2,1)} %gate_in_ref.1) | copy-start | bytes 294916
  0.6 2.3 %copy-start.2 = (bf16[384,128]{1,0:T(8,128)(2,1)S(1)}, bf16[384,128]{1,0:T(8,128)(2,1)}, u32[]{:S(2)}) copy-start(bf16[384,128]{1,0:T(8,128)(2,1)} %value_ref.1) | copy-start | bytes 294916
  1.7 7.7 %collective-permute-start.1 = (bf16[1,384,128]{2,1,0:T(8,128)(2,1)S(1)}, bf16[1,384,128]{2,1,0:T(8,128)(2,1)S(1)}, u32[]{:S(2)}, u32[]{:S(2)}) collective-permute-start(bf16[1,384,128]{2,1,0:T(8,128)(2,1)S(1)} %bitcast.11), channel_id=1, source_target_pairs={{8,0},{12,4},{16,8},{20,12},{24,16},{28,20},{9,1},{13,5},{17,9},{2... | collective-permute-start | bytes 294920 | tf_op jit(solution)/shard_map/ppermute | solution.py:22
  3.0 3.1 %copy-start.6 = (f32[1536]{0:T(1024)S(1)}, f32[1536]{0:T(1024)}, u32[]{:S(2)}) copy-start(f32[1536]{0:T(1024)} %param.11) | copy-start | bytes 18436
  3.2 11.5 %collective-permute-start = (bf16[384,128]{1,0:T(8,128)(2,1)S(1)}, bf16[384,128]{1,0:T(8,128)(2,1)S(1)}, u32[]{:S(2)}, u32[]{:S(2)}) collective-permute-start(bf16[384,128]{1,0:T(8,128)(2,1)S(1)} %bitcast.14), channel_id=1, source_target_pairs={{0,4},{4,8},{8,12},{12,16},{16,20},{20,24},{24,28},{28,0},{1,5},{5... | collective-permute-start | bytes 294920 | tf_op jit(solution)/shard_map/ppermute | solution.py:27
  6.2 0.7 %copy-start.4 = (s32[3]{0:T(128)S(1)}, s32[3]{0:T(128)}, u32[]{:S(2)}) copy-start(s32[3]{0:T(128)} %param.12) | copy-start | bytes 40
  6.2 0.7 %copy-start.5 = (f32[128]{0:T(128)S(1)}, f32[128]{0:T(128)}, u32[]{:S(2)}) copy-start(f32[128]{0:T(128)} %param.10) | copy-start | bytes 1540
  7.0 7.7 %copy-start = (bf16[384,128]{1,0:T(8,128)(2,1)S(1)}, bf16[384,128]{1,0:T(8,128)(2,1)}, u32[]{:S(2)}) copy-start(bf16[384,128]{1,0:T(8,128)(2,1)} %gate_out_ref.1) | copy-start | bytes 294916
  9.4 13.5 %collective-permute-start.2 = (bf16[2,384,128]{2,1,0:T(8,128)(2,1)S(1)}, bf16[2,384,128]{2,1,0:T(8,128)(2,1)S(1)}, u32[]{:S(2)}, u32[]{:S(2)}) collective-permute-start(bf16[2,384,128]{2,1,0:T(8,128)(2,1)S(1)} %get-tuple-element.29.cots_ref), channel_id=1, source_target_pairs={{0,28},{4,0},{8,4},{12,8},{16,12},{20,16},{24,20},{28,24},{1,29},{... | collective-permute-start | bytes 589832 | tf_op jit(solution)/shard_map/ppermute | solution.py:27
  16.0 9.7 %all-to-all-start = ((f32[32,1,256]{2,1,0:T(1,128)}), f32[32,1,256]{2,1,0:T(1,128)S(1)}, u32[]{:S(2)}, u32[]{:S(2)}) async-start(f32[32,1,256]{2,1,0:T(1,128)} %get-tuple-element.27), calls=%async_computation | async-start | bytes 65536 | tf_op jit(solution)/shard_map/all_to_all | solution.py:234
  19.3 5.9 %collective-permute-start.3 = (bf16[384,128]{1,0:T(8,128)(2,1)S(1)}, bf16[384,128]{1,0:T(8,128)(2,1)S(1)}, u32[]{:S(2)}, u32[]{:S(2)}) collective-permute-start(bf16[384,128]{1,0:T(8,128)(2,1)S(1)} %bitcast.18), channel_id=1, source_target_pairs={{0,8},{4,12},{8,16},{12,20},{16,24},{20,28},{1,9},{5,13},{9,17},{1... | collective-permute-start | bytes 294920 | tf_op jit(solution)/shard_map/ppermute | solution.py:22
  25.3 1.0 %copy-start.1 = (bf16[384,128]{1,0:T(8,128)(2,1)}, bf16[384,128]{1,0:T(8,128)(2,1)S(1)}, u32[]{:S(2)}) copy-start(bf16[384,128]{1,0:T(8,128)(2,1)S(1)} %fusion.1.layer_out_ref) | copy-start | bytes 294916

commit v6 on v5

--- a/solution.py
+++ b/solution.py
@@ -71,7 +71,9 @@
     sources = [block[at : at + TILE] for block in (before, flipped_ref[...]) for at in range(0, rows, TILE)]
     zero = jnp.zeros((chans, TILE), BF16)
 
-    def write_parts(used):
+    def write_parts(used, tiles_before):
+        placed = sources[blocks - tiles_before :]
+        placed = placed + [jnp.zeros_like(placed[0])] * (len(placed) % 2)
         wide = []
         for e in range(used):
             if e == 0:
@@ -83,12 +85,12 @@
             wide += [jnp.concatenate(tiles[n : n + 2], axis=0) for n in range(blocks + 1)]
         wide = jnp.concatenate(wide, axis=1)
         sums = [None] * (2 * used * blocks)
-        for x in range(0, 2 * blocks, 2):
-            source = jnp.concatenate(sources[x : x + 2], axis=1)
+        for x in range(0, len(placed), 2):
+            source = jnp.concatenate(placed[x : x + 2], axis=1)
             product = jnp.dot(source, wide, preferred_element_type=F32)
             for e in range(used):
                 for n in range(blocks + 1):
-                    d = 2 * blocks * e + n - 1 + blocks - x
+                    d = 2 * blocks * e + n - 1 + tiles_before - x
                     if d >= 0:
                         at = (e * (blocks + 1) + n) * TILE
                         piece = product[:, at : at + TILE]
@@ -96,6 +98,7 @@
         row = lax.broadcasted_iota(jnp.int32, (TILE, TILE), 0)
         col = lax.broadcasted_iota(jnp.int32, (TILE, TILE), 1)
         sums[0] = jnp.where(row + col >= TILE - 1, sums[0], 0.0)
+        sums = [jnp.zeros((TILE, TILE), F32) if piece is None else piece for piece in sums]
         width = len(sums) * TILE
         skewed = pltpu.roll(jnp.concatenate(sums, axis=1), width - TILE + 1, 1, stride=1, stride_axis=0)
         lags = jnp.sum(skewed, axis=0, keepdims=True) * scale
@@ -108,11 +111,13 @@
                 parts_ref[q * shards + p, :, :owned] = piece
 
     if evens == 1:
-        write_parts(1)
+        write_parts(1, blocks)
     else:
-        later = lax.axis_index("seq") + 2 < shards
-        pl.when(later)(functools.partial(write_parts, evens))
-        pl.when(jnp.logical_not(later))(functools.partial(write_parts, 1))
+        position = lax.axis_index("seq")
+        later = position + 2 < shards
+        pl.when(jnp.logical_and(later, position > 0))(functools.partial(write_parts, evens, blocks))
+        pl.when(jnp.logical_and(later, position == 0))(functools.partial(write_parts, evens, 0))
+        pl.when(jnp.logical_not(later))(functools.partial(write_parts, 1, blocks))
     for n, tile in enumerate(sources[::-1]):
         sources_ref[n * TILE : (n + 1) * TILE, :] = tile
 

time: 26.6 us -> 26.5 us (level)
  no operation moved by 1% of the time
where the time goes in v6:
time: 26.5 us; the launch traced here: 26.2 us
  starting transfers between devices  14.2 us (54%)
  waiting for transfers between devices  5.24 us (20%)
  Pallas kernels  4.01 us (15%)
  other arithmetic  1.15 us (4%)
  local copies, waits for them, and re-layouts  0.84 us (3%)
  between operations  0.8 us (3%)
    ppermute x2, starting transfers between devices, rotated(): lax.ppermute(value, axis, [(i, (i + by) % length) for i in range(length)])  6.75 us
    ppermute x2, starting transfers between devices, shifted(): return lax.ppermute(value, axis, pairs)  4.89 us
    ppermute x2, waiting for transfers between devices, shifted(): return lax.ppermute(value, axis, pairs)  3.34 us
    all_to_all x1, starting transfers between devices, body(): gathered = lax.all_to_all(parts, ('ch', 'seq'), 0, 0, tiled=True)  2.55 us
    ppermute x2, waiting for transfers between devices, rotated(): lax.ppermute(value, axis, [(i, (i + by) % length) for i in range(length)])  1.48 us
    pallas_call x1, Pallas kernels, body(): pl.pallas_call(near_kernel, out_shape=(jax.ShapeDtypeStruct((rows, chans)...  1.31 us
    pallas_call x1, Pallas kernels, body(): pl.pallas_call(functools.partial(lag_kernel, owned=owned, copies=groups,...  1.23 us
    convert_element_type x1, other arithmetic, body(): cot_gated = (cotangent.astype(F32) * gate_out.astype(F32)).astype(BF16)  1.01 us
  transfers between devices with their start and end apart: 5, of which 4 were waited for; matrix products, arithmetic and copies ran while one was open for 1% of the time, Pallas kernels for 13%

profile of v6, /device:TPU:0, one launch (start us, length us, event | category | flops | bytes accessed | tf_op | source)
XLA Modules:
  0.0 26.2 jit_solution(15992841280472865506)
XLA Ops:
  0.6 0.0 copy-start.3
  0.6 0.0 copy-start.2
  0.7 1.0 %fusion.cots_ref = bf16[384,128]{1,0:T(8,128)(2,1)S(1)} fusion(bf16[384,128]{1,0:T(8,128)(2,1)} %gate_out_ref.1, bf16[384,128]{1,0:T(8,128)(2,1)} %param.13), kind=kLoop, calls=%fused_computation.3 | loop fusion | flops 196608 | bytes 294912 | tf_op jit(solution)/shard_map/convert_element_type | solution.py:196
  1.7 1.3 %collective-permute-start.1 = (bf16[1,384,128]{2,1,0:T(8,128)(2,1)S(1)}, bf16[1,384,128]{2,1,0:T(8,128)(2,1)S(1)}, u32[]{:S(2)}, u32[]{:S(2)}) collective-permute-start(bf16[1,384,128]{2,1,0:T(8,128)(2,1)S(1)} %bitcast.11), channel_id=1, source_target_pairs={{8,0},{12,4},{16,8},{20,12},{24,16},{28,20},{9,1},{13,5},{17,9},{2... | collective-permute-start | bytes 294920 | tf_op jit(solution)/shard_map/ppermute | solution.py:22
  3.0 0.0 copy-done.3
  3.0 0.0 copy-done.2
  3.0 0.0 copy-start.6
  3.0 0.1 rev.3
  3.2 3.0 %collective-permute-start = (bf16[384,128]{1,0:T(8,128)(2,1)S(1)}, bf16[384,128]{1,0:T(8,128)(2,1)S(1)}, u32[]{:S(2)}, u32[]{:S(2)}) collective-permute-start(bf16[384,128]{1,0:T(8,128)(2,1)S(1)} %bitcast.14), channel_id=1, source_target_pairs={{0,4},{4,8},{8,12},{12,16},{16,20},{20,24},{24,28},{28,0},{1,5},{5... | collective-permute-start | bytes 294920 | tf_op jit(solution)/shard_map/ppermute | solution.py:27
  6.2 0.0 copy-done.6
  6.2 0.0 copy-start.4
  6.2 0.0 copy-start.5
  6.2 0.6 %copy-done.4 = s32[3]{0:T(128)S(1)} copy-done((s32[3]{0:T(128)S(1)}, s32[3]{0:T(128)}, u32[]{:S(2)}) %copy-start.4) | copy-done | bytes 36
  6.8 0.0 copy-done.5
  6.8 0.1 stage.1
  7.0 0.0 copy-start
  7.0 2.4 %collective-permute-done.1 = bf16[1,384,128]{2,1,0:T(8,128)(2,1)S(1)} collective-permute-done((bf16[1,384,128]{2,1,0:T(8,128)(2,1)S(1)}, bf16[1,384,128]{2,1,0:T(8,128)(2,1)S(1)}, u32[]{:S(2)}, u32[]{:S(2)}) %collective-permute-start.1) | collective-permute-done | bytes 98336 | tf_op jit(solution)/shard_map/ppermute | solution.py:22
  9.4 3.8 %collective-permute-start.2 = (bf16[2,384,128]{2,1,0:T(8,128)(2,1)S(1)}, bf16[2,384,128]{2,1,0:T(8,128)(2,1)S(1)}, u32[]{:S(2)}, u32[]{:S(2)}) collective-permute-start(bf16[2,384,128]{2,1,0:T(8,128)(2,1)S(1)} %get-tuple-element.29.cots_ref), channel_id=1, source_target_pairs={{0,28},{4,0},{8,4},{12,8},{16,12},{20,16},{24,20},{28,24},{1,29},{... | collective-permute-start | bytes 589832 | tf_op jit(solution)/shard_map/ppermute | solution.py:27
  13.2 1.5 %collective-permute-done.before_ref = bf16[384,128]{1,0:T(8,128)(2,1)S(1)} collective-permute-done((bf16[384,128]{1,0:T(8,128)(2,1)S(1)}, bf16[384,128]{1,0:T(8,128)(2,1)S(1)}, u32[]{:S(2)}, u32[]{:S(2)}) %collective-permute-start) | collective-permute-done | bytes 98336 | tf_op jit(solution)/shard_map/ppermute | solution.py:27
  14.7 0.0 copy-done
  14.7 1.2 %lags.1 = (f32[32,1,256]{2,1,0:T(1,128)}, bf16[768,128]{1,0:T(8,128)(2,1)S(1)}) custom-call(f32[2,8,128]{2,1,0:T(8,128)S(1)} %get-tuple-element.18.masks_ref, bf16[384,128]{1,0:T(8,128)(2,1)S(1)} %bitcast.15, bf16[384,128]{1,0:T(8,128)(2,1)S(1)} %collective-permute-done.before_ref, bf16[128,384]{1,0:T(8,128)(2,1)S(1)} %get-tuple-element.19.turned_ref, ...), custom_call_target="tpu_custom_call" | custom-call | flops 10000000000 | bytes 1048576 | tf_op jit(solution)/shard_map/lags/pallas_call | solution.py:227
  15.9 2.5 %all-to-all-start = ((f32[32,1,256]{2,1,0:T(1,128)}), f32[32,1,256]{2,1,0:T(1,128)S(1)}, u32[]{:S(2)}, u32[]{:S(2)}) async-start(f32[32,1,256]{2,1,0:T(1,128)} %get-tuple-element.27), calls=%async_computation | async-start | bytes 65536 | tf_op jit(solution)/shard_map/all_to_all | solution.py:239
  18.4 0.8 %ahead.1 = (bf16[128,1536]{1,0:T(8,128)(2,1)S(1)}, bf16[128,1536]{1,0:T(8,128)(2,1)S(1)}, bf16[1,384,128]{2,1,0:T(8,128)(2,1)S(1)}) custom-call(s32[1,3]{1,0:T(1,128)S(1)} %get-tuple-element.16.lengths_ref, f32[1,1536]{1,0:T(1,128)S(1)} %reshape.28.taps_ref, bf16[768,128]{1,0:T(8,128)(2,1)S(1)} %get-tuple-element.20.sources_ref), custom_call_target="tpu_custom_call" | custom-call | tf_op jit(solution)/shard_map/ahead/pallas_call | solution.py:243
  19.2 3.6 %collective-permute-start.3 = (bf16[384,128]{1,0:T(8,128)(2,1)S(1)}, bf16[384,128]{1,0:T(8,128)(2,1)S(1)}, u32[]{:S(2)}, u32[]{:S(2)}) collective-permute-start(bf16[384,128]{1,0:T(8,128)(2,1)S(1)} %bitcast.18), channel_id=1, source_target_pairs={{0,8},{4,12},{8,16},{12,20},{16,24},{20,28},{1,9},{5,13},{9,17},{1... | collective-permute-start | bytes 294920 | tf_op jit(solution)/shard_map/ppermute | solution.py:22
  22.8 0.0 collective-permute-done.2
  22.9 1.3 %near.1 = (f32[384,128]{1,0:T(8,128)S(1)}, bf16[384,128]{1,0:T(8,128)(2,1)}, bf16[384,128]{1,0:T(8,128)(2,1)}) custom-call(s32[1,3]{1,0:T(1,128)S(1)} %get-tuple-element.16.lengths_ref, bf16[384,128]{1,0:T(8,128)(2,1)S(1)} %copy-done.2, bf16[384,128]{1,0:T(8,128)(2,1)S(1)} %copy-done.3, f32[1,128]{1,0:T(1,128)S(1)} %get-tuple-element.17.skip_ref, ...), custom_call_target="tpu_custom_call" | custom-call | flops 10000000000 | bytes 1048576 | tf_op jit(solution)/shard_map/near/pallas_call | solution.py:253
  24.2 0.9 %collective-permute-done.3 = bf16[384,128]{1,0:T(8,128)(2,1)S(1)} collective-permute-done((bf16[384,128]{1,0:T(8,128)(2,1)S(1)}, bf16[384,128]{1,0:T(8,128)(2,1)S(1)}, u32[]{:S(2)}, u32[]{:S(2)}) %collective-permute-start.3) | collective-permute-done | bytes 98336 | tf_op jit(solution)/shard_map/ppermute | solution.py:22
  25.2 0.0 copy-start.1
  25.2 0.4 %all-to-all-done.gathered_ref = f32[32,1,256]{2,1,0:T(1,128)S(1)} async-done(((f32[32,1,256]{2,1,0:T(1,128)}), f32[32,1,256]{2,1,0:T(1,128)S(1)}, u32[]{:S(2)}, u32[]{:S(2)}) %all-to-all-start) | async-done | bytes 32800 | tf_op jit(solution)/shard_map/all_to_all | solution.py:239
  25.6 0.6 %sum.1 = f32[1,192]{1,0:T(1,128)} custom-call(f32[32,1,256]{2,1,0:T(1,128)S(1)} %all-to-all-done.gathered_ref, bf16[384,128]{1,0:T(8,128)(2,1)S(1)} %fusion.1.layer_out_ref), custom_call_target="tpu_custom_call" | custom-call | tf_op jit(solution)/shard_map/sum/pallas_call | solution.py:264
  26.2 0.0 copy-done.1
  (6 shorter events, 0.2 us)
Async XLA Ops:
  0.6 2.3 %copy-start.3 = (bf16[384,128]{1,0:T(8,128)(2,1)S(1)}, bf16[384,128]{1,0:T(8,128)(2,1)}, u32[]{:S(2)}) copy-start(bf16[384,128]{1,0:T(8,128)(2,1)} %gate_in_ref.1) | copy-start | bytes 294916
  0.6 2.3 %copy-start.2 = (bf16[384,128]{1,0:T(8,128)(2,1)S(1)}, bf16[384,128]{1,0:T(8,128)(2,1)}, u32[]{:S(2)}) copy-start(bf16[384,128]{1,0:T(8,128)(2,1)} %value_ref.1) | copy-start | bytes 294916
  1.7 7.7 %collective-permute-start.1 = (bf16[1,384,128]{2,1,0:T(8,128)(2,1)S(1)}, bf16[1,384,128]{2,1,0:T(8,128)(2,1)S(1)}, u32[]{:S(2)}, u32[]{:S(2)}) collective-permute-start(bf16[1,384,128]{2,1,0:T(8,128)(2,1)S(1)} %bitcast.11), channel_id=1, source_target_pairs={{8,0},{12,4},{16,8},{20,12},{24,16},{28,20},{9,1},{13,5},{17,9},{2... | collective-permute-start | bytes 294920 | tf_op jit(solution)/shard_map/ppermute | solution.py:22
  3.0 3.1 %copy-start.6 = (f32[1536]{0:T(1024)S(1)}, f32[1536]{0:T(1024)}, u32[]{:S(2)}) copy-start(f32[1536]{0:T(1024)} %param.11) | copy-start | bytes 18436
  3.2 11.5 %collective-permute-start = (bf16[384,128]{1,0:T(8,128)(2,1)S(1)}, bf16[384,128]{1,0:T(8,128)(2,1)S(1)}, u32[]{:S(2)}, u32[]{:S(2)}) collective-permute-start(bf16[384,128]{1,0:T(8,128)(2,1)S(1)} %bitcast.14), channel_id=1, source_target_pairs={{0,4},{4,8},{8,12},{12,16},{16,20},{20,24},{24,28},{28,0},{1,5},{5... | collective-permute-start | bytes 294920 | tf_op jit(solution)/shard_map/ppermute | solution.py:27
  6.2 0.7 %copy-start.4 = (s32[3]{0:T(128)S(1)}, s32[3]{0:T(128)}, u32[]{:S(2)}) copy-start(s32[3]{0:T(128)} %param.12) | copy-start | bytes 40
  6.2 0.7 %copy-start.5 = (f32[128]{0:T(128)S(1)}, f32[128]{0:T(128)}, u32[]{:S(2)}) copy-start(f32[128]{0:T(128)} %param.10) | copy-start | bytes 1540
  7.0 7.7 %copy-start = (bf16[384,128]{1,0:T(8,128)(2,1)S(1)}, bf16[384,128]{1,0:T(8,128)(2,1)}, u32[]{:S(2)}) copy-start(bf16[384,128]{1,0:T(8,128)(2,1)} %gate_out_ref.1) | copy-start | bytes 294916
  9.4 13.4 %collective-permute-start.2 = (bf16[2,384,128]{2,1,0:T(8,128)(2,1)S(1)}, bf16[2,384,128]{2,1,0:T(8,128)(2,1)S(1)}, u32[]{:S(2)}, u32[]{:S(2)}) collective-permute-start(bf16[2,384,128]{2,1,0:T(8,128)(2,1)S(1)} %get-tuple-element.29.cots_ref), channel_id=1, source_target_pairs={{0,28},{4,0},{8,4},{12,8},{16,12},{20,16},{24,20},{28,24},{1,29},{... | collective-permute-start | bytes 589832 | tf_op jit(solution)/shard_map/ppermute | solution.py:27
  15.9 9.7 %all-to-all-start = ((f32[32,1,256]{2,1,0:T(1,128)}), f32[32,1,256]{2,1,0:T(1,128)S(1)}, u32[]{:S(2)}, u32[]{:S(2)}) async-start(f32[32,1,256]{2,1,0:T(1,128)} %get-tuple-element.27), calls=%async_computation | async-start | bytes 65536 | tf_op jit(solution)/shard_map/all_to_all | solution.py:239
  19.2 6.0 %collective-permute-start.3 = (bf16[384,128]{1,0:T(8,128)(2,1)S(1)}, bf16[384,128]{1,0:T(8,128)(2,1)S(1)}, u32[]{:S(2)}, u32[]{:S(2)}) collective-permute-start(bf16[384,128]{1,0:T(8,128)(2,1)S(1)} %bitcast.18), channel_id=1, source_target_pairs={{0,8},{4,12},{8,16},{12,20},{16,24},{20,28},{1,9},{5,13},{9,17},{1... | collective-permute-start | bytes 294920 | tf_op jit(solution)/shard_map/ppermute | solution.py:22
  25.2 1.0 %copy-start.1 = (bf16[384,128]{1,0:T(8,128)(2,1)}, bf16[384,128]{1,0:T(8,128)(2,1)S(1)}, u32[]{:S(2)}) copy-start(bf16[384,128]{1,0:T(8,128)(2,1)S(1)} %fusion.1.layer_out_ref) | copy-start | bytes 294916

commit v7 on v6

--- a/solution.py
+++ b/solution.py
@@ -48,19 +48,35 @@
     return (row + col == TILE - 1).astype(F32).astype(BF16)
 
 
-def stage_kernel(lengths_ref, skip_ref, cots_ref, lengths_out_ref, skip_out_ref, turned_ref, masks_ref):
+def stage_kernel(
+    lengths_ref, skip_ref, cots_ref, flipped_ref, lengths_out_ref, skip_out_ref, turned_ref, masks_ref, own_ref, picks_ref,
+    *, owned, starts,
+):
     lengths_out_ref[...] = lengths_ref[...]
     skip_out_ref[...] = skip_ref[...]
     rows, chans = cots_ref.shape
     for at in range(0, rows, TILE):
         turned_ref[:, at : at + TILE] = cots_ref[at : at + TILE, :].astype(F32).T.astype(BF16)
+    skipped = lax.axis_index("seq") * owned % TILE
+    for n, start in enumerate(starts):
+        picks_ref[n] = jnp.full(picks_ref.shape[1:], (skipped == start).astype(F32))
+    own = [None] * (rows // TILE)
+    for sb in range(len(own)):
+        product = jnp.dot(
+            flipped_ref[sb * TILE : (sb + 1) * TILE, :], turned_ref[:, sb * TILE :], preferred_element_type=F32
+        )
+        for d in range(len(own) - sb):
+            piece = product[:, d * TILE : (d + 1) * TILE]
+            own[d] = piece if own[d] is None else own[d] + piece
+    for d, piece in enumerate(own):
+        own_ref[:, d * TILE : (d + 1) * TILE] = piece
     evens = masks_ref.shape[0]
     for n, mask in enumerate(doc_masks(lengths_ref, [-1] + [2 * e for e in range(1, evens)], chans)):
         masks_ref[n] = jnp.broadcast_to(mask.astype(F32), masks_ref.shape[1:])
 
 
 def lag_kernel(
-    masks_ref, flipped_ref, before_ref, turned_ref, cots_ref, gate_out_ref, parts_ref, sources_ref,
+    masks_ref, flipped_ref, before_ref, turned_ref, own_ref, cots_ref, gate_out_ref, parts_ref, sources_ref,
     *, owned, copies, scale, shards,
 ):
     del gate_out_ref
@@ -72,28 +88,25 @@
     zero = jnp.zeros((chans, TILE), BF16)
 
     def write_parts(used, tiles_before):
-        placed = sources[blocks - tiles_before :]
-        placed = placed + [jnp.zeros_like(placed[0])] * (len(placed) % 2)
-        wide = []
+        sums = [own_ref[:, d * TILE : (d + 1) * TILE] if d < blocks else None for d in range(2 * used * blocks)]
         for e in range(used):
+            placed = sources[blocks - tiles_before :]
             if e == 0:
+                placed = placed[:tiles_before]
                 tiles = [turned_ref[:, at : at + TILE] for at in range(0, rows, TILE)]
             else:
                 cots = cots_ref[e] * masks[e]
                 tiles = [cots[at : at + TILE].astype(F32).T.astype(BF16) for at in range(0, rows, TILE)]
+            placed = placed + [jnp.zeros((TILE, chans), BF16)] * (len(placed) % 2)
             tiles = [zero] + tiles + [zero]
-            wide += [jnp.concatenate(tiles[n : n + 2], axis=0) for n in range(blocks + 1)]
-        wide = jnp.concatenate(wide, axis=1)
-        sums = [None] * (2 * used * blocks)
-        for x in range(0, len(placed), 2):
-            source = jnp.concatenate(placed[x : x + 2], axis=1)
-            product = jnp.dot(source, wide, preferred_element_type=F32)
-            for e in range(used):
+            wide = jnp.concatenate([jnp.concatenate(tiles[n : n + 2], axis=0) for n in range(blocks + 1)], axis=1)
+            for x in range(0, len(placed), 2):
+                source = jnp.concatenate(placed[x : x + 2], axis=1)
+                product = jnp.dot(source, wide, preferred_element_type=F32)
                 for n in range(blocks + 1):
                     d = 2 * blocks * e + n - 1 + tiles_before - x
                     if d >= 0:
-                        at = (e * (blocks + 1) + n) * TILE
-                        piece = product[:, at : at + TILE]
+                        piece = product[:, n * TILE : (n + 1) * TILE]
                         sums[d] = piece if sums[d] is None else sums[d] + piece
         row = lax.broadcasted_iota(jnp.int32, (TILE, TILE), 0)
         col = lax.broadcasted_iota(jnp.int32, (TILE, TILE), 1)
@@ -102,13 +115,16 @@
         width = len(sums) * TILE
         skewed = pltpu.roll(jnp.concatenate(sums, axis=1), width - TILE + 1, 1, stride=1, stride_axis=0)
         lags = jnp.sum(skewed, axis=0, keepdims=True) * scale
+        window = parts_ref.shape[2]
         for p in range(parts_ref.shape[0] // copies):
-            some = min(max(width - p * owned, 0), owned)
-            pieces = [lags[:, p * owned : p * owned + some]] if some > 0 else []
-            pieces += [jnp.zeros((1, owned - some), F32)] if some < owned else []
-            piece = pieces[0] if len(pieces) == 1 else jnp.concatenate(pieces, axis=1)
+            first = p * owned // TILE * TILE
+            last = min(first + window, width)
             for q in range(copies):
-                parts_ref[q * shards + p, :, :owned] = piece
+                if first < last:
+                    parts_ref[q * shards + p, :, : last - first] = lags[:, first:last]
+                if last < first + window:
+                    rest = max(last - first, 0)
+                    parts_ref[q * shards + p, :, rest:] = jnp.zeros((1, window - rest), F32)
 
     if evens == 1:
         write_parts(1, blocks)
@@ -177,10 +193,15 @@
         near_ref[here, :] = convolved + skip * (gate_in * value).astype(BF16).astype(F32)
 
 
-def sum_kernel(gathered_ref, layer_out_ref, total_ref):
+def sum_kernel(gathered_ref, picks_ref, layer_out_ref, total_ref, *, starts):
     del layer_out_ref
     owned = total_ref.shape[1]
-    total_ref[...] = jnp.sum(gathered_ref[:, 0, :], axis=0, keepdims=True)[:, :owned]
+    total = jnp.sum(gathered_ref[:, 0, :], axis=0, keepdims=True)
+    owner = total[:, : owned]
+    for n, start in enumerate(starts):
+        if start > 0:
+            owner = jnp.where(picks_ref[n, 0:1, :owned] > 0.0, total[:, start : start + owned], owner)
+    total_ref[...] = owner
 
 
 PARAMS = pltpu.CompilerParams(vmem_limit_bytes=LIMIT)
@@ -209,33 +230,37 @@
     odds = rotated(evens, "seq", -1)
     future = jnp.stack([evens, odds], axis=1).reshape(longest, rows, chans)
 
-    lengths, skip, turned, masks = pl.pallas_call(
-        stage_kernel,
+    owned = maxlag // shards
+    starts = tuple(sorted({p * owned % TILE for p in range(shards)}))
+    window = -(-(starts[-1] + owned) // TILE) * TILE
+    lengths, skip, turned, masks, own, picks = pl.pallas_call(
+        functools.partial(stage_kernel, owned=owned, starts=starts),
         out_shape=(
             jax.ShapeDtypeStruct((1, doc_lengths.shape[0]), jnp.int32),
             jax.ShapeDtypeStruct((1, chans), F32),
             jax.ShapeDtypeStruct((chans, rows), BF16),
             jax.ShapeDtypeStruct((evens.shape[0], 8, chans), F32),
+            jax.ShapeDtypeStruct((TILE, rows), F32),
+            jax.ShapeDtypeStruct((len(starts), 8, window), F32),
         ),
-        in_specs=[VMEM] * 3,
-        out_specs=(VMEM,) * 4,
+        in_specs=[VMEM] * 4,
+        out_specs=(VMEM,) * 6,
         compiler_params=PARAMS,
         name="stage",
-    )(doc_lengths.reshape(1, -1), skip_gain.reshape(1, chans), cot_gated)
-    owned = maxlag // shards
+    )(doc_lengths.reshape(1, -1), skip_gain.reshape(1, chans), cot_gated, flipped)
     grad_scale = 1.0 / math.sqrt(shards * rows * chans * groups)
     parts, sources = pl.pallas_call(
         functools.partial(lag_kernel, owned=owned, copies=groups, scale=grad_scale, shards=shards),
         out_shape=(
-            jax.ShapeDtypeStruct((shards * groups, 1, -(-owned // TILE) * TILE), F32),
+            jax.ShapeDtypeStruct((shards * groups, 1, window), F32),
             jax.ShapeDtypeStruct((2 * rows, chans), BF16),
         ),
-        in_specs=[VMEM] * 6,
+        in_specs=[VMEM] * 7,
         out_specs=(VMEM,) * 2,
         compiler_params=PARAMS,
         cost_estimate=pl.CostEstimate(flops=LAGF, bytes_accessed=2**20, transcendentals=0),
         name="lags",
-    )(masks, flipped, before, turned, evens, gate_out)
+    )(masks, flipped, before, turned, own, evens, gate_out)
     gathered = lax.all_to_all(parts, ("ch", "seq"), 0, 0, tiled=True)
 
     band = jax.ShapeDtypeStruct((TILE, maxlag), BF16)
@@ -262,13 +287,13 @@
     )(lengths, value_proj, gate_in, skip, later, earlier, sources, future)
     layer_out = (gate_out.astype(F32) * (near + far)).astype(BF16)
     filter_grad = pl.pallas_call(
-        sum_kernel,
+        functools.partial(sum_kernel, starts=starts),
         out_shape=jax.ShapeDtypeStruct((1, owned), F32),
-        in_specs=[VMEM, pl.BlockSpec(memory_space=pl.ANY)],
+        in_specs=[VMEM, VMEM, pl.BlockSpec(memory_space=pl.ANY)],
         out_specs=VMEM,
         compiler_params=PARAMS,
         name="sum",
-    )(gathered, layer_out)[0]
+    )(gathered, picks, layer_out)[0]
     return (layer_out, grad_value, grad_gate, filter_grad)
 
 

time: 26.5 us -> 26.4 us (level)
  no operation moved by 1% of the time
where the time goes in v7:
time: 26.4 us; the launch traced here: 26.2 us
  starting transfers between devices  14.2 us (54%)
  waiting for transfers between devices  5.05 us (19%)
  Pallas kernels  4.13 us (16%)
  other arithmetic  1.15 us (4%)
  local copies, waits for them, and re-layouts  0.84 us (3%)
  between operations  0.8 us (3%)
    ppermute x2, starting transfers between devices, rotated(): lax.ppermute(value, axis, [(i, (i + by) % length) for i in range(length)])  6.75 us
    ppermute x2, starting transfers between devices, shifted(): return lax.ppermute(value, axis, pairs)  4.89 us
    ppermute x2, waiting for transfers between devices, shifted(): return lax.ppermute(value, axis, pairs)  3.16 us
    all_to_all x1, starting transfers between devices, body(): gathered = lax.all_to_all(parts, ('ch', 'seq'), 0, 0, tiled=True)  2.55 us
    ppermute x2, waiting for transfers between devices, rotated(): lax.ppermute(value, axis, [(i, (i + by) % length) for i in range(length)])  1.48 us
    pallas_call x1, Pallas kernels, body(): pl.pallas_call(near_kernel, out_shape=(jax.ShapeDtypeStruct((rows, chans)...  1.31 us
    pallas_call x1, Pallas kernels, body(): pl.pallas_call(functools.partial(lag_kernel, owned=owned, copies=groups,...  1.1 us
    convert_element_type x1, other arithmetic, body(): cot_gated = (cotangent.astype(F32) * gate_out.astype(F32)).astype(BF16)  1.01 us
  transfers between devices with their start and end apart: 5, of which 4 were waited for; matrix products, arithmetic and copies ran while one was open for 1% of the time, Pallas kernels for 13%

profile of v7, /device:TPU:0, one launch (start us, length us, event | category | flops | bytes accessed | tf_op | source)
XLA Modules:
  0.0 26.2 jit_solution(9842551633029777295)
XLA Ops:
  0.6 0.0 copy-start.3
  0.6 0.0 copy-start.2
  0.7 1.0 %fusion.cots_ref = bf16[384,128]{1,0:T(8,128)(2,1)S(1)} fusion(bf16[384,128]{1,0:T(8,128)(2,1)} %gate_out_ref.1, bf16[384,128]{1,0:T(8,128)(2,1)} %param.13), kind=kLoop, calls=%fused_computation.3 | loop fusion | flops 196608 | bytes 294912 | tf_op jit(solution)/shard_map/convert_element_type | solution.py:217
  1.7 1.3 %collective-permute-start.1 = (bf16[1,384,128]{2,1,0:T(8,128)(2,1)S(1)}, bf16[1,384,128]{2,1,0:T(8,128)(2,1)S(1)}, u32[]{:S(2)}, u32[]{:S(2)}) collective-permute-start(bf16[1,384,128]{2,1,0:T(8,128)(2,1)S(1)} %bitcast.11), channel_id=1, source_target_pairs={{8,0},{12,4},{16,8},{20,12},{24,16},{28,20},{9,1},{13,5},{17,9},{2... | collective-permute-start | bytes 294920 | tf_op jit(solution)/shard_map/ppermute | solution.py:22
  3.0 0.0 copy-done.3
  3.0 0.0 copy-done.2
  3.0 0.0 copy-start.6
  3.0 0.1 rev.3
  3.2 3.0 %collective-permute-start = (bf16[384,128]{1,0:T(8,128)(2,1)S(1)}, bf16[384,128]{1,0:T(8,128)(2,1)S(1)}, u32[]{:S(2)}, u32[]{:S(2)}) collective-permute-start(bf16[384,128]{1,0:T(8,128)(2,1)S(1)} %bitcast.14), channel_id=1, source_target_pairs={{0,4},{4,8},{8,12},{12,16},{16,20},{20,24},{24,28},{28,0},{1,5},{5... | collective-permute-start | bytes 294920 | tf_op jit(solution)/shard_map/ppermute | solution.py:27
  6.2 0.0 copy-done.6
  6.2 0.0 copy-start.4
  6.2 0.0 copy-start.5
  6.2 0.6 %copy-done.4 = s32[3]{0:T(128)S(1)} copy-done((s32[3]{0:T(128)S(1)}, s32[3]{0:T(128)}, u32[]{:S(2)}) %copy-start.4) | copy-done | bytes 36
  6.8 0.0 copy-done.5
  6.8 0.3 %stage.1 = (s32[1,3]{1,0:T(1,128)S(1)}, f32[1,128]{1,0:T(1,128)S(1)}, bf16[128,384]{1,0:T(8,128)(2,1)S(1)}, f32[2,8,128]{2,1,0:T(8,128)S(1)}, f32[128,384]{1,0:T(8,128)S(1)}, /*index=5*/f32[2,8,256]{2,1,0:T(8,128)S(1)}) custom-call(s32[1,3]{1,0:T(1,128)S(1)} %bitcast.17, f32[1,128]{1,0:T(1,128)S(1)} %bitcast.18, bf16[384,128]{1,0:T(8,128)(2,1)S(1)} %fusion.cots_ref, ...), custom_call_target="tpu_custom_call" | custom-call | tf_op jit(solution)/shard_map/stage/pallas_call | solution.py:236
  7.2 0.0 copy-start.1
  7.2 2.2 %collective-permute-done.1 = bf16[1,384,128]{2,1,0:T(8,128)(2,1)S(1)} collective-permute-done((bf16[1,384,128]{2,1,0:T(8,128)(2,1)S(1)}, bf16[1,384,128]{2,1,0:T(8,128)(2,1)S(1)}, u32[]{:S(2)}, u32[]{:S(2)}) %collective-permute-start.1) | collective-permute-done | bytes 98336 | tf_op jit(solution)/shard_map/ppermute | solution.py:22
  9.4 3.8 %collective-permute-start.2 = (bf16[2,384,128]{2,1,0:T(8,128)(2,1)S(1)}, bf16[2,384,128]{2,1,0:T(8,128)(2,1)S(1)}, u32[]{:S(2)}, u32[]{:S(2)}) collective-permute-start(bf16[2,384,128]{2,1,0:T(8,128)(2,1)S(1)} %get-tuple-element.33.cots_ref), channel_id=1, source_target_pairs={{0,28},{4,0},{8,4},{12,8},{16,12},{20,16},{24,20},{28,24},{1,29},{... | collective-permute-start | bytes 589832 | tf_op jit(solution)/shard_map/ppermute | solution.py:27
  13.2 1.5 %collective-permute-done.before_ref = bf16[384,128]{1,0:T(8,128)(2,1)S(1)} collective-permute-done((bf16[384,128]{1,0:T(8,128)(2,1)S(1)}, bf16[384,128]{1,0:T(8,128)(2,1)S(1)}, u32[]{:S(2)}, u32[]{:S(2)}) %collective-permute-start) | collective-permute-done | bytes 98336 | tf_op jit(solution)/shard_map/ppermute | solution.py:27
  14.7 0.0 copy-done.1
  14.7 1.1 %lags.1 = (f32[32,1,256]{2,1,0:T(1,128)}, bf16[768,128]{1,0:T(8,128)(2,1)S(1)}) custom-call(f32[2,8,128]{2,1,0:T(8,128)S(1)} %get-tuple-element.20.masks_ref, bf16[384,128]{1,0:T(8,128)(2,1)S(1)} %bitcast.16, bf16[384,128]{1,0:T(8,128)(2,1)S(1)} %collective-permute-done.before_ref, bf16[128,384]{1,0:T(8,128)(2,1)S(1)} %get-tuple-element.21.turned_ref, ...), custom_call_target="tpu_custom_call" | custom-call | flops 10000000000 | bytes 1048576 | tf_op jit(solution)/shard_map/lags/pallas_call | solution.py:252
  15.8 2.5 %all-to-all-start = ((f32[32,1,256]{2,1,0:T(1,128)}), f32[32,1,256]{2,1,0:T(1,128)S(1)}, u32[]{:S(2)}, u32[]{:S(2)}) async-start(f32[32,1,256]{2,1,0:T(1,128)} %get-tuple-element.30), calls=%async_computation | async-start | bytes 65536 | tf_op jit(solution)/shard_map/all_to_all | solution.py:264
  18.3 0.8 %ahead.1 = (bf16[128,1536]{1,0:T(8,128)(2,1)S(1)}, bf16[128,1536]{1,0:T(8,128)(2,1)S(1)}, bf16[1,384,128]{2,1,0:T(8,128)(2,1)S(1)}) custom-call(s32[1,3]{1,0:T(1,128)S(1)} %get-tuple-element.18.lengths_ref, f32[1,1536]{1,0:T(1,128)S(1)} %reshape.30.taps_ref, bf16[768,128]{1,0:T(8,128)(2,1)S(1)} %get-tuple-element.23.sources_ref), custom_call_target="tpu_custom_call" | custom-call | tf_op jit(solution)/shard_map/ahead/pallas_call | solution.py:268
  19.1 3.6 %collective-permute-start.3 = (bf16[384,128]{1,0:T(8,128)(2,1)S(1)}, bf16[384,128]{1,0:T(8,128)(2,1)S(1)}, u32[]{:S(2)}, u32[]{:S(2)}) collective-permute-start(bf16[384,128]{1,0:T(8,128)(2,1)S(1)} %bitcast.19), channel_id=1, source_target_pairs={{0,8},{4,12},{8,16},{12,20},{16,24},{20,28},{1,9},{5,13},{9,17},{1... | collective-permute-start | bytes 294920 | tf_op jit(solution)/shard_map/ppermute | solution.py:22
  22.7 0.0 collective-permute-done.2
  22.8 1.3 %near.1 = (f32[384,128]{1,0:T(8,128)S(1)}, bf16[384,128]{1,0:T(8,128)(2,1)}, bf16[384,128]{1,0:T(8,128)(2,1)}) custom-call(s32[1,3]{1,0:T(1,128)S(1)} %get-tuple-element.18.lengths_ref, bf16[384,128]{1,0:T(8,128)(2,1)S(1)} %copy-done.2, bf16[384,128]{1,0:T(8,128)(2,1)S(1)} %copy-done.3, f32[1,128]{1,0:T(1,128)S(1)} %get-tuple-element.19.skip_ref, ...), custom_call_target="tpu_custom_call" | custom-call | flops 10000000000 | bytes 1048576 | tf_op jit(solution)/shard_map/near/pallas_call | solution.py:278
  24.1 0.9 %collective-permute-done.3 = bf16[384,128]{1,0:T(8,128)(2,1)S(1)} collective-permute-done((bf16[384,128]{1,0:T(8,128)(2,1)S(1)}, bf16[384,128]{1,0:T(8,128)(2,1)S(1)}, u32[]{:S(2)}, u32[]{:S(2)}) %collective-permute-start.3) | collective-permute-done | bytes 98336 | tf_op jit(solution)/shard_map/ppermute | solution.py:22
  25.1 0.0 copy-start
  25.1 0.4 %all-to-all-done.gathered_ref = f32[32,1,256]{2,1,0:T(1,128)S(1)} async-done(((f32[32,1,256]{2,1,0:T(1,128)}), f32[32,1,256]{2,1,0:T(1,128)S(1)}, u32[]{:S(2)}, u32[]{:S(2)}) %all-to-all-start) | async-done | bytes 32800 | tf_op jit(solution)/shard_map/all_to_all | solution.py:264
  25.5 0.7 %sum.1 = f32[1,192]{1,0:T(1,128)} custom-call(f32[32,1,256]{2,1,0:T(1,128)S(1)} %all-to-all-done.gathered_ref, f32[2,8,256]{2,1,0:T(8,128)S(1)} %get-tuple-element.31.picks_ref, bf16[384,128]{1,0:T(8,128)(2,1)S(1)} %fusion.1.layer_out_ref), custom_call_target="tpu_custom_call" | custom-call | tf_op jit(solution)/shard_map/sum/pallas_call | solution.py:289
  26.2 0.0 copy-done
  (6 shorter events, 0.2 us)
Async XLA Ops:
  0.6 2.3 %copy-start.3 = (bf16[384,128]{1,0:T(8,128)(2,1)S(1)}, bf16[384,128]{1,0:T(8,128)(2,1)}, u32[]{:S(2)}) copy-start(bf16[384,128]{1,0:T(8,128)(2,1)} %gate_in_ref.1) | copy-start | bytes 294916
  0.6 2.3 %copy-start.2 = (bf16[384,128]{1,0:T(8,128)(2,1)S(1)}, bf16[384,128]{1,0:T(8,128)(2,1)}, u32[]{:S(2)}) copy-start(bf16[384,128]{1,0:T(8,128)(2,1)} %value_ref.1) | copy-start | bytes 294916
  1.7 7.7 %collective-permute-start.1 = (bf16[1,384,128]{2,1,0:T(8,128)(2,1)S(1)}, bf16[1,384,128]{2,1,0:T(8,128)(2,1)S(1)}, u32[]{:S(2)}, u32[]{:S(2)}) collective-permute-start(bf16[1,384,128]{2,1,0:T(8,128)(2,1)S(1)} %bitcast.11), channel_id=1, source_target_pairs={{8,0},{12,4},{16,8},{20,12},{24,16},{28,20},{9,1},{13,5},{17,9},{2... | collective-permute-start | bytes 294920 | tf_op jit(solution)/shard_map/ppermute | solution.py:22
  3.0 3.1 %copy-start.6 = (f32[1536]{0:T(1024)S(1)}, f32[1536]{0:T(1024)}, u32[]{:S(2)}) copy-start(f32[1536]{0:T(1024)} %param.11) | copy-start | bytes 18436
  3.2 11.5 %collective-permute-start = (bf16[384,128]{1,0:T(8,128)(2,1)S(1)}, bf16[384,128]{1,0:T(8,128)(2,1)S(1)}, u32[]{:S(2)}, u32[]{:S(2)}) collective-permute-start(bf16[384,128]{1,0:T(8,128)(2,1)S(1)} %bitcast.14), channel_id=1, source_target_pairs={{0,4},{4,8},{8,12},{12,16},{16,20},{20,24},{24,28},{28,0},{1,5},{5... | collective-permute-start | bytes 294920 | tf_op jit(solution)/shard_map/ppermute | solution.py:27
  6.2 0.7 %copy-start.4 = (s32[3]{0:T(128)S(1)}, s32[3]{0:T(128)}, u32[]{:S(2)}) copy-start(s32[3]{0:T(128)} %param.12) | copy-start | bytes 40
  6.2 0.7 %copy-start.5 = (f32[128]{0:T(128)S(1)}, f32[128]{0:T(128)}, u32[]{:S(2)}) copy-start(f32[128]{0:T(128)} %param.10) | copy-start | bytes 1540
  7.2 7.5 %copy-start.1 = (bf16[384,128]{1,0:T(8,128)(2,1)S(1)}, bf16[384,128]{1,0:T(8,128)(2,1)}, u32[]{:S(2)}) copy-start(bf16[384,128]{1,0:T(8,128)(2,1)} %gate_out_ref.1) | copy-start | bytes 294916
  9.4 13.3 %collective-permute-start.2 = (bf16[2,384,128]{2,1,0:T(8,128)(2,1)S(1)}, bf16[2,384,128]{2,1,0:T(8,128)(2,1)S(1)}, u32[]{:S(2)}, u32[]{:S(2)}) collective-permute-start(bf16[2,384,128]{2,1,0:T(8,128)(2,1)S(1)} %get-tuple-element.33.cots_ref), channel_id=1, source_target_pairs={{0,28},{4,0},{8,4},{12,8},{16,12},{20,16},{24,20},{28,24},{1,29},{... | collective-permute-start | bytes 589832 | tf_op jit(solution)/shard_map/ppermute | solution.py:27
  15.8 9.7 %all-to-all-start = ((f32[32,1,256]{2,1,0:T(1,128)}), f32[32,1,256]{2,1,0:T(1,128)S(1)}, u32[]{:S(2)}, u32[]{:S(2)}) async-start(f32[32,1,256]{2,1,0:T(1,128)} %get-tuple-element.30), calls=%async_computation | async-start | bytes 65536 | tf_op jit(solution)/shard_map/all_to_all | solution.py:264
  19.1 5.9 %collective-permute-start.3 = (bf16[384,128]{1,0:T(8,128)(2,1)S(1)}, bf16[384,128]{1,0:T(8,128)(2,1)S(1)}, u32[]{:S(2)}, u32[]{:S(2)}) collective-permute-start(bf16[384,128]{1,0:T(8,128)(2,1)S(1)} %bitcast.19), channel_id=1, source_target_pairs={{0,8},{4,12},{8,16},{12,20},{16,24},{20,28},{1,9},{5,13},{9,17},{1... | collective-permute-start | bytes 294920 | tf_op jit(solution)/shard_map/ppermute | solution.py:22
  25.1 1.1 %copy-start = (bf16[384,128]{1,0:T(8,128)(2,1)}, bf16[384,128]{1,0:T(8,128)(2,1)S(1)}, u32[]{:S(2)}) copy-start(bf16[384,128]{1,0:T(8,128)(2,1)S(1)} %fusion.1.layer_out_ref) | copy-start | bytes 294916

commit v8 on v7

--- a/solution.py
+++ b/solution.py
@@ -76,7 +76,7 @@
 
 
 def lag_kernel(
-    masks_ref, flipped_ref, before_ref, turned_ref, own_ref, cots_ref, gate_out_ref, parts_ref, sources_ref,
+    masks_ref, flipped_ref, before_ref, turned_ref, own_ref, cots_ref, gate_out_ref, parts_ref,
     *, owned, copies, scale, shards,
 ):
     del gate_out_ref
@@ -134,11 +134,18 @@
         pl.when(jnp.logical_and(later, position > 0))(functools.partial(write_parts, evens, blocks))
         pl.when(jnp.logical_and(later, position == 0))(functools.partial(write_parts, evens, 0))
         pl.when(jnp.logical_not(later))(functools.partial(write_parts, 1, blocks))
-    for n, tile in enumerate(sources[::-1]):
-        sources_ref[n * TILE : (n + 1) * TILE, :] = tile
-
-
-def ahead_kernel(lengths_ref, taps_ref, sources_ref, later_ref, earlier_ref, ahead_ref):
+
+
+def ahead_kernel(
+    lengths_ref, taps_ref, masks_ref, flipped_ref, before_ref, parts_ref,
+    later_ref, earlier_ref, ahead_ref, sources_ref,
+):
+    del parts_ref
+    tiles = sources_ref.shape[0] // TILE // 2
+    before = before_ref[...] * masks_ref[0, 0:1, :].astype(BF16)
+    for b in range(tiles):
+        sources_ref[(tiles - 1 - b) * TILE : (tiles - b) * TILE, :] = flipped_ref[b * TILE : (b + 1) * TILE, :]
+        sources_ref[(2 * tiles - 1 - b) * TILE : (2 * tiles - b) * TILE, :] = before[b * TILE : (b + 1) * TILE]
     width = taps_ref.shape[1]
     count = sources_ref.shape[0] // TILE
     further, _, chans = ahead_ref.shape
@@ -249,14 +256,11 @@
         name="stage",
     )(doc_lengths.reshape(1, -1), skip_gain.reshape(1, chans), cot_gated, flipped)
     grad_scale = 1.0 / math.sqrt(shards * rows * chans * groups)
-    parts, sources = pl.pallas_call(
+    parts = pl.pallas_call(
         functools.partial(lag_kernel, owned=owned, copies=groups, scale=grad_scale, shards=shards),
-        out_shape=(
-            jax.ShapeDtypeStruct((shards * groups, 1, window), F32),
-            jax.ShapeDtypeStruct((2 * rows, chans), BF16),
-        ),
+        out_shape=jax.ShapeDtypeStruct((shards * groups, 1, window), F32),
         in_specs=[VMEM] * 7,
-        out_specs=(VMEM,) * 2,
+        out_specs=VMEM,
         compiler_params=PARAMS,
         cost_estimate=pl.CostEstimate(flops=LAGF, bytes_accessed=2**20, transcendentals=0),
         name="lags",
@@ -265,14 +269,16 @@
 
     band = jax.ShapeDtypeStruct((TILE, maxlag), BF16)
     further = longest // 2 - 1
-    later, earlier, ahead = pl.pallas_call(
+    later, earlier, ahead, sources = pl.pallas_call(
         ahead_kernel,
-        out_shape=(band, band, jax.ShapeDtypeStruct((further, rows, chans), BF16)),
-        in_specs=[VMEM] * 3,
-        out_specs=(VMEM,) * 3,
+        out_shape=(
+            band, band, jax.ShapeDtypeStruct((further, rows, chans), BF16), jax.ShapeDtypeStruct((2 * rows, chans), BF16)
+        ),
+        in_specs=[VMEM] * 5 + [pl.BlockSpec(memory_space=pl.ANY)],
+        out_specs=(VMEM,) * 4,
         compiler_params=PARAMS,
         name="ahead",
-    )(lengths, filter_taps.reshape(1, maxlag), sources)
+    )(lengths, filter_taps.reshape(1, maxlag), masks, flipped, before, parts)
     far = sum(shifted(ahead[m], "seq", 2 * m + 2).astype(F32) for m in range(further))
 
     near, grad_value, grad_gate = pl.pallas_call(

time: 26.4 us -> 26.4 us (level)
  no operation moved by 1% of the time
where the time goes in v8:
time: 26.4 us; the launch traced here: 26.2 us
  starting transfers between devices  14.2 us (54%)
  waiting for transfers between devices  5.07 us (19%)
  Pallas kernels  4.11 us (16%)
  other arithmetic  1.15 us (4%)
  local copies, waits for them, and re-layouts  0.84 us (3%)
  between operations  0.8 us (3%)
    ppermute x2, starting transfers between devices, rotated(): lax.ppermute(value, axis, [(i, (i + by) % length) for i in range(length)])  6.75 us
    ppermute x2, starting transfers between devices, shifted(): return lax.ppermute(value, axis, pairs)  4.89 us
    ppermute x2, waiting for transfers between devices, shifted(): return lax.ppermute(value, axis, pairs)  3.17 us
    all_to_all x1, starting transfers between devices, body(): gathered = lax.all_to_all(parts, ('ch', 'seq'), 0, 0, tiled=True)  2.56 us
    ppermute x2, waiting for transfers between devices, rotated(): lax.ppermute(value, axis, [(i, (i + by) % length) for i in range(length)])  1.48 us
    pallas_call x1, Pallas kernels, body(): pl.pallas_call(near_kernel, out_shape=(jax.ShapeDtypeStruct((rows, chans)...  1.3 us
    pallas_call x1, Pallas kernels, body(): pl.pallas_call(functools.partial(lag_kernel, owned=owned, copies=groups,...  1.09 us
    convert_element_type x1, other arithmetic, body(): cot_gated = (cotangent.astype(F32) * gate_out.astype(F32)).astype(BF16)  1.01 us
  transfers between devices with their start and end apart: 5, of which 4 were waited for; matrix products, arithmetic and copies ran while one was open for 1% of the time, Pallas kernels for 13%

profile of v8, /device:TPU:0, one launch (start us, length us, event | category | flops | bytes accessed | tf_op | source)
XLA Modules:
  0.0 26.2 jit_solution(16675431642548953374)
XLA Ops:
  0.6 0.0 copy-start.3
  0.6 0.0 copy-start.2
  0.7 1.0 %fusion.cots_ref = bf16[384,128]{1,0:T(8,128)(2,1)S(1)} fusion(bf16[384,128]{1,0:T(8,128)(2,1)} %gate_out_ref.1, bf16[384,128]{1,0:T(8,128)(2,1)} %param.13), kind=kLoop, calls=%fused_computation.3 | loop fusion | flops 196608 | bytes 294912 | tf_op jit(solution)/shard_map/convert_element_type | solution.py:224
  1.7 1.3 %collective-permute-start.1 = (bf16[1,384,128]{2,1,0:T(8,128)(2,1)S(1)}, bf16[1,384,128]{2,1,0:T(8,128)(2,1)S(1)}, u32[]{:S(2)}, u32[]{:S(2)}) collective-permute-start(bf16[1,384,128]{2,1,0:T(8,128)(2,1)S(1)} %bitcast.15), channel_id=1, source_target_pairs={{8,0},{12,4},{16,8},{20,12},{24,16},{28,20},{9,1},{13,5},{17,9},{2... | collective-permute-start | bytes 294920 | tf_op jit(solution)/shard_map/ppermute | solution.py:22
  3.0 0.0 copy-done.3
  3.0 0.0 copy-done.2
  3.0 0.0 copy-start.6
  3.0 0.1 rev.3
  3.2 3.0 %collective-permute-start = (bf16[384,128]{1,0:T(8,128)(2,1)S(1)}, bf16[384,128]{1,0:T(8,128)(2,1)S(1)}, u32[]{:S(2)}, u32[]{:S(2)}) collective-permute-start(bf16[384,128]{1,0:T(8,128)(2,1)S(1)} %bitcast.11), channel_id=1, source_target_pairs={{0,4},{4,8},{8,12},{12,16},{16,20},{20,24},{24,28},{28,0},{1,5},{5... | collective-permute-start | bytes 294920 | tf_op jit(solution)/shard_map/ppermute | solution.py:27
  6.2 0.0 copy-done.6
  6.2 0.0 copy-start.4
  6.2 0.0 copy-start.5
  6.2 0.6 %copy-done.4 = s32[3]{0:T(128)S(1)} copy-done((s32[3]{0:T(128)S(1)}, s32[3]{0:T(128)}, u32[]{:S(2)}) %copy-start.4) | copy-done | bytes 36
  6.8 0.0 copy-done.5
  6.8 0.3 %stage.1 = (s32[1,3]{1,0:T(1,128)S(1)}, f32[1,128]{1,0:T(1,128)S(1)}, bf16[128,384]{1,0:T(8,128)(2,1)S(1)}, f32[2,8,128]{2,1,0:T(8,128)S(1)}, f32[128,384]{1,0:T(8,128)S(1)}, /*index=5*/f32[2,8,256]{2,1,0:T(8,128)S(1)}) custom-call(s32[1,3]{1,0:T(1,128)S(1)} %bitcast.18, f32[1,128]{1,0:T(1,128)S(1)} %bitcast.19, bf16[384,128]{1,0:T(8,128)(2,1)S(1)} %fusion.cots_ref, ...), custom_call_target="tpu_custom_call" | custom-call | tf_op jit(solution)/shard_map/stage/pallas_call | solution.py:243
  7.2 0.0 copy-start.1
  7.2 2.2 %collective-permute-done.1 = bf16[1,384,128]{2,1,0:T(8,128)(2,1)S(1)} collective-permute-done((bf16[1,384,128]{2,1,0:T(8,128)(2,1)S(1)}, bf16[1,384,128]{2,1,0:T(8,128)(2,1)S(1)}, u32[]{:S(2)}, u32[]{:S(2)}) %collective-permute-start.1) | collective-permute-done | bytes 98336 | tf_op jit(solution)/shard_map/ppermute | solution.py:22
  9.4 3.8 %collective-permute-start.2 = (bf16[2,384,128]{2,1,0:T(8,128)(2,1)S(1)}, bf16[2,384,128]{2,1,0:T(8,128)(2,1)S(1)}, u32[]{:S(2)}, u32[]{:S(2)}) collective-permute-start(bf16[2,384,128]{2,1,0:T(8,128)(2,1)S(1)} %get-tuple-element.31.cots_ref), channel_id=1, source_target_pairs={{0,28},{4,0},{8,4},{12,8},{16,12},{20,16},{24,20},{28,24},{1,29},{... | collective-permute-start | bytes 589832 | tf_op jit(solution)/shard_map/ppermute | solution.py:27
  13.2 1.5 %collective-permute-done.before_ref = bf16[384,128]{1,0:T(8,128)(2,1)S(1)} collective-permute-done((bf16[384,128]{1,0:T(8,128)(2,1)S(1)}, bf16[384,128]{1,0:T(8,128)(2,1)S(1)}, u32[]{:S(2)}, u32[]{:S(2)}) %collective-permute-start) | collective-permute-done | bytes 98336 | tf_op jit(solution)/shard_map/ppermute | solution.py:27
  14.7 0.0 copy-done.1
  14.7 1.1 %lags.1.parts_ref = f32[32,1,256]{2,1,0:T(1,128)} custom-call(f32[2,8,128]{2,1,0:T(8,128)S(1)} %get-tuple-element.19.masks_ref, bf16[384,128]{1,0:T(8,128)(2,1)S(1)} %bitcast.13, bf16[384,128]{1,0:T(8,128)(2,1)S(1)} %collective-permute-done.before_ref, bf16[128,384]{1,0:T(8,128)(2,1)S(1)} %get-tuple-element.20.turned_ref, ...), custom_call_target="tpu_custom_call" | custom-call | flops 10000000000 | bytes 1048576 | tf_op jit(solution)/shard_map/lags/pallas_call | solution.py:259
  15.7 2.6 %all-to-all-start = ((f32[32,1,256]{2,1,0:T(1,128)}), f32[32,1,256]{2,1,0:T(1,128)S(1)}, u32[]{:S(2)}, u32[]{:S(2)}) async-start(f32[32,1,256]{2,1,0:T(1,128)} %lags.1.parts_ref), calls=%async_computation | async-start | bytes 65536 | tf_op jit(solution)/shard_map/all_to_all | solution.py:268
  18.3 0.8 %ahead.1 = (bf16[128,1536]{1,0:T(8,128)(2,1)S(1)}, bf16[128,1536]{1,0:T(8,128)(2,1)S(1)}, bf16[1,384,128]{2,1,0:T(8,128)(2,1)S(1)}, bf16[768,128]{1,0:T(8,128)(2,1)S(1)}) custom-call(s32[1,3]{1,0:T(1,128)S(1)} %get-tuple-element.17.lengths_ref, f32[1,1536]{1,0:T(1,128)S(1)} %reshape.30.taps_ref, f32[2,8,128]{2,1,0:T(8,128)S(1)} %get-tuple-element.19.masks_ref, ...), custom_call_target="tpu_custom_call" | custom-call | tf_op jit(solution)/shard_map/ahead/pallas_call | solution.py:272
  19.1 3.6 %collective-permute-start.3 = (bf16[384,128]{1,0:T(8,128)(2,1)S(1)}, bf16[384,128]{1,0:T(8,128)(2,1)S(1)}, u32[]{:S(2)}, u32[]{:S(2)}) collective-permute-start(bf16[384,128]{1,0:T(8,128)(2,1)S(1)} %bitcast.20), channel_id=1, source_target_pairs={{0,8},{4,12},{8,16},{12,20},{16,24},{20,28},{1,9},{5,13},{9,17},{1... | collective-permute-start | bytes 294920 | tf_op jit(solution)/shard_map/ppermute | solution.py:22
  22.7 0.0 collective-permute-done.2
  22.8 1.3 %near.1 = (f32[384,128]{1,0:T(8,128)S(1)}, bf16[384,128]{1,0:T(8,128)(2,1)}, bf16[384,128]{1,0:T(8,128)(2,1)}) custom-call(s32[1,3]{1,0:T(1,128)S(1)} %get-tuple-element.17.lengths_ref, bf16[384,128]{1,0:T(8,128)(2,1)S(1)} %copy-done.2, bf16[384,128]{1,0:T(8,128)(2,1)S(1)} %copy-done.3, f32[1,128]{1,0:T(1,128)S(1)} %get-tuple-element.18.skip_ref, ...), custom_call_target="tpu_custom_call" | custom-call | flops 10000000000 | bytes 1048576 | tf_op jit(solution)/shard_map/near/pallas_call | solution.py:284
  24.1 1.0 %collective-permute-done.3 = bf16[384,128]{1,0:T(8,128)(2,1)S(1)} collective-permute-done((bf16[384,128]{1,0:T(8,128)(2,1)S(1)}, bf16[384,128]{1,0:T(8,128)(2,1)S(1)}, u32[]{:S(2)}, u32[]{:S(2)}) %collective-permute-start.3) | collective-permute-done | bytes 98336 | tf_op jit(solution)/shard_map/ppermute | solution.py:22
  25.1 0.0 copy-start
  25.1 0.4 %all-to-all-done.gathered_ref = f32[32,1,256]{2,1,0:T(1,128)S(1)} async-done(((f32[32,1,256]{2,1,0:T(1,128)}), f32[32,1,256]{2,1,0:T(1,128)S(1)}, u32[]{:S(2)}, u32[]{:S(2)}) %all-to-all-start) | async-done | bytes 32800 | tf_op jit(solution)/shard_map/all_to_all | solution.py:268
  25.5 0.7 %sum.1 = f32[1,192]{1,0:T(1,128)} custom-call(f32[32,1,256]{2,1,0:T(1,128)S(1)} %all-to-all-done.gathered_ref, f32[2,8,256]{2,1,0:T(8,128)S(1)} %get-tuple-element.29.picks_ref, bf16[384,128]{1,0:T(8,128)(2,1)S(1)} %fusion.1.layer_out_ref), custom_call_target="tpu_custom_call" | custom-call | tf_op jit(solution)/shard_map/sum/pallas_call | solution.py:295
  26.2 0.0 copy-done
  (6 shorter events, 0.2 us)
Async XLA Ops:
  0.6 2.3 %copy-start.3 = (bf16[384,128]{1,0:T(8,128)(2,1)S(1)}, bf16[384,128]{1,0:T(8,128)(2,1)}, u32[]{:S(2)}) copy-start(bf16[384,128]{1,0:T(8,128)(2,1)} %gate_in_ref.1) | copy-start | bytes 294916
  0.6 2.3 %copy-start.2 = (bf16[384,128]{1,0:T(8,128)(2,1)S(1)}, bf16[384,128]{1,0:T(8,128)(2,1)}, u32[]{:S(2)}) copy-start(bf16[384,128]{1,0:T(8,128)(2,1)} %value_ref.1) | copy-start | bytes 294916
  1.7 7.7 %collective-permute-start.1 = (bf16[1,384,128]{2,1,0:T(8,128)(2,1)S(1)}, bf16[1,384,128]{2,1,0:T(8,128)(2,1)S(1)}, u32[]{:S(2)}, u32[]{:S(2)}) collective-permute-start(bf16[1,384,128]{2,1,0:T(8,128)(2,1)S(1)} %bitcast.15), channel_id=1, source_target_pairs={{8,0},{12,4},{16,8},{20,12},{24,16},{28,20},{9,1},{13,5},{17,9},{2... | collective-permute-start | bytes 294920 | tf_op jit(solution)/shard_map/ppermute | solution.py:22
  3.0 3.1 %copy-start.6 = (f32[1536]{0:T(1024)S(1)}, f32[1536]{0:T(1024)}, u32[]{:S(2)}) copy-start(f32[1536]{0:T(1024)} %param.11) | copy-start | bytes 18436
  3.2 11.5 %collective-permute-start = (bf16[384,128]{1,0:T(8,128)(2,1)S(1)}, bf16[384,128]{1,0:T(8,128)(2,1)S(1)}, u32[]{:S(2)}, u32[]{:S(2)}) collective-permute-start(bf16[384,128]{1,0:T(8,128)(2,1)S(1)} %bitcast.11), channel_id=1, source_target_pairs={{0,4},{4,8},{8,12},{12,16},{16,20},{20,24},{24,28},{28,0},{1,5},{5... | collective-permute-start | bytes 294920 | tf_op jit(solution)/shard_map/ppermute | solution.py:27
  6.2 0.7 %copy-start.4 = (s32[3]{0:T(128)S(1)}, s32[3]{0:T(128)}, u32[]{:S(2)}) copy-start(s32[3]{0:T(128)} %param.12) | copy-start | bytes 40
  6.2 0.7 %copy-start.5 = (f32[128]{0:T(128)S(1)}, f32[128]{0:T(128)}, u32[]{:S(2)}) copy-start(f32[128]{0:T(128)} %param.10) | copy-start | bytes 1540
  7.2 7.5 %copy-start.1 = (bf16[384,128]{1,0:T(8,128)(2,1)S(1)}, bf16[384,128]{1,0:T(8,128)(2,1)}, u32[]{:S(2)}) copy-start(bf16[384,128]{1,0:T(8,128)(2,1)} %gate_out_ref.1) | copy-start | bytes 294916
  9.4 13.3 %collective-permute-start.2 = (bf16[2,384,128]{2,1,0:T(8,128)(2,1)S(1)}, bf16[2,384,128]{2,1,0:T(8,128)(2,1)S(1)}, u32[]{:S(2)}, u32[]{:S(2)}) collective-permute-start(bf16[2,384,128]{2,1,0:T(8,128)(2,1)S(1)} %get-tuple-element.31.cots_ref), channel_id=1, source_target_pairs={{0,28},{4,0},{8,4},{12,8},{16,12},{20,16},{24,20},{28,24},{1,29},{... | collective-permute-start | bytes 589832 | tf_op jit(solution)/shard_map/ppermute | solution.py:27
  15.7 9.7 %all-to-all-start = ((f32[32,1,256]{2,1,0:T(1,128)}), f32[32,1,256]{2,1,0:T(1,128)S(1)}, u32[]{:S(2)}, u32[]{:S(2)}) async-start(f32[32,1,256]{2,1,0:T(1,128)} %lags.1.parts_ref), calls=%async_computation | async-start | bytes 65536 | tf_op jit(solution)/shard_map/all_to_all | solution.py:268
  19.1 6.0 %collective-permute-start.3 = (bf16[384,128]{1,0:T(8,128)(2,1)S(1)}, bf16[384,128]{1,0:T(8,128)(2,1)S(1)}, u32[]{:S(2)}, u32[]{:S(2)}) collective-permute-start(bf16[384,128]{1,0:T(8,128)(2,1)S(1)} %bitcast.20), channel_id=1, source_target_pairs={{0,8},{4,12},{8,16},{12,20},{16,24},{20,28},{1,9},{5,13},{9,17},{1... | collective-permute-start | bytes 294920 | tf_op jit(solution)/shard_map/ppermute | solution.py:22
  25.1 1.1 %copy-start = (bf16[384,128]{1,0:T(8,128)(2,1)}, bf16[384,128]{1,0:T(8,128)(2,1)S(1)}, u32[]{:S(2)}) copy-start(bf16[384,128]{1,0:T(8,128)(2,1)S(1)} %fusion.1.layer_out_ref) | copy-start | bytes 294916

commit v9 on v8

--- a/solution.py
+++ b/solution.py
@@ -77,7 +77,7 @@
 
 def lag_kernel(
     masks_ref, flipped_ref, before_ref, turned_ref, own_ref, cots_ref, gate_out_ref, parts_ref,
-    *, owned, copies, scale, shards,
+    *, owned, copies, shards,
 ):
     del gate_out_ref
     evens, rows, chans = cots_ref.shape
@@ -114,7 +114,7 @@
         sums = [jnp.zeros((TILE, TILE), F32) if piece is None else piece for piece in sums]
         width = len(sums) * TILE
         skewed = pltpu.roll(jnp.concatenate(sums, axis=1), width - TILE + 1, 1, stride=1, stride_axis=0)
-        lags = jnp.sum(skewed, axis=0, keepdims=True) * scale
+        lags = jnp.sum(skewed, axis=0, keepdims=True)
         window = parts_ref.shape[2]
         for p in range(parts_ref.shape[0] // copies):
             first = p * owned // TILE * TILE
@@ -200,7 +200,7 @@
         near_ref[here, :] = convolved + skip * (gate_in * value).astype(BF16).astype(F32)
 
 
-def sum_kernel(gathered_ref, picks_ref, layer_out_ref, total_ref, *, starts):
+def sum_kernel(gathered_ref, picks_ref, layer_out_ref, total_ref, *, starts, scale):
     del layer_out_ref
     owned = total_ref.shape[1]
     total = jnp.sum(gathered_ref[:, 0, :], axis=0, keepdims=True)
@@ -208,7 +208,7 @@
     for n, start in enumerate(starts):
         if start > 0:
             owner = jnp.where(picks_ref[n, 0:1, :owned] > 0.0, total[:, start : start + owned], owner)
-    total_ref[...] = owner
+    total_ref[...] = owner * scale
 
 
 PARAMS = pltpu.CompilerParams(vmem_limit_bytes=LIMIT)
@@ -257,7 +257,7 @@
     )(doc_lengths.reshape(1, -1), skip_gain.reshape(1, chans), cot_gated, flipped)
     grad_scale = 1.0 / math.sqrt(shards * rows * chans * groups)
     parts = pl.pallas_call(
-        functools.partial(lag_kernel, owned=owned, copies=groups, scale=grad_scale, shards=shards),
+        functools.partial(lag_kernel, owned=owned, copies=groups, shards=shards),
         out_shape=jax.ShapeDtypeStruct((shards * groups, 1, window), F32),
         in_specs=[VMEM] * 7,
         out_specs=VMEM,
@@ -293,7 +293,7 @@
     )(lengths, value_proj, gate_in, skip, later, earlier, sources, future)
     layer_out = (gate_out.astype(F32) * (near + far)).astype(BF16)
     filter_grad = pl.pallas_call(
-        functools.partial(sum_kernel, starts=starts),
+        functools.partial(sum_kernel, starts=starts, scale=grad_scale),
         out_shape=jax.ShapeDtypeStruct((1, owned), F32),
         in_specs=[VMEM, VMEM, pl.BlockSpec(memory_space=pl.ANY)],
         out_specs=VMEM,

time: 26.4 us -> 26.4 us (level)
  no operation moved by 1% of the time
where the time goes in v9:
time: 26.4 us; the launch traced here: 26.2 us
  starting transfers between devices  14.2 us (54%)
  waiting for transfers between devices  5.07 us (19%)
  Pallas kernels  4.11 us (16%)
  other arithmetic  1.15 us (4%)
  local copies, waits for them, and re-layouts  0.84 us (3%)
  between operations  0.8 us (3%)
    ppermute x2, starting transfers between devices, rotated(): lax.ppermute(value, axis, [(i, (i + by) % length) for i in range(length)])  6.75 us
    ppermute x2, starting transfers between devices, shifted(): return lax.ppermute(value, axis, pairs)  4.89 us
    ppermute x2, waiting for transfers between devices, shifted(): return lax.ppermute(value, axis, pairs)  3.17 us
    all_to_all x1, starting transfers between devices, body(): gathered = lax.all_to_all(parts, ('ch', 'seq'), 0, 0, tiled=True)  2.56 us
    ppermute x2, waiting for transfers between devices, rotated(): lax.ppermute(value, axis, [(i, (i + by) % length) for i in range(length)])  1.48 us
    pallas_call x1, Pallas kernels, body(): pl.pallas_call(near_kernel, out_shape=(jax.ShapeDtypeStruct((rows, chans)...  1.3 us
    pallas_call x1, Pallas kernels, body(): pl.pallas_call(functools.partial(lag_kernel, owned=owned, copies=groups,...  1.09 us
    convert_element_type x1, other arithmetic, body(): cot_gated = (cotangent.astype(F32) * gate_out.astype(F32)).astype(BF16)  1.01 us
  transfers between devices with their start and end apart: 5, of which 4 were waited for; matrix products, arithmetic and copies ran while one was open for 1% of the time, Pallas kernels for 13%

profile of v9, /device:TPU:0, one launch (start us, length us, event | category | flops | bytes accessed | tf_op | source)
XLA Modules:
  0.0 26.2 jit_solution(838566921944890846)
XLA Ops:
  0.6 0.0 copy-start.3
  0.6 0.0 copy-start.2
  0.7 1.0 %fusion.cots_ref = bf16[384,128]{1,0:T(8,128)(2,1)S(1)} fusion(bf16[384,128]{1,0:T(8,128)(2,1)} %gate_out_ref.1, bf16[384,128]{1,0:T(8,128)(2,1)} %param.13), kind=kLoop, calls=%fused_computation.3 | loop fusion | flops 196608 | bytes 294912 | tf_op jit(solution)/shard_map/convert_element_type | solution.py:224
  1.7 1.3 %collective-permute-start.1 = (bf16[1,384,128]{2,1,0:T(8,128)(2,1)S(1)}, bf16[1,384,128]{2,1,0:T(8,128)(2,1)S(1)}, u32[]{:S(2)}, u32[]{:S(2)}) collective-permute-start(bf16[1,384,128]{2,1,0:T(8,128)(2,1)S(1)} %bitcast.15), channel_id=1, source_target_pairs={{8,0},{12,4},{16,8},{20,12},{24,16},{28,20},{9,1},{13,5},{17,9},{2... | collective-permute-start | bytes 294920 | tf_op jit(solution)/shard_map/ppermute | solution.py:22
  3.0 0.0 copy-done.3
  3.0 0.0 copy-done.2
  3.0 0.0 copy-start.6
  3.0 0.1 rev.3
  3.2 3.0 %collective-permute-start = (bf16[384,128]{1,0:T(8,128)(2,1)S(1)}, bf16[384,128]{1,0:T(8,128)(2,1)S(1)}, u32[]{:S(2)}, u32[]{:S(2)}) collective-permute-start(bf16[384,128]{1,0:T(8,128)(2,1)S(1)} %bitcast.11), channel_id=1, source_target_pairs={{0,4},{4,8},{8,12},{12,16},{16,20},{20,24},{24,28},{28,0},{1,5},{5... | collective-permute-start | bytes 294920 | tf_op jit(solution)/shard_map/ppermute | solution.py:27
  6.2 0.0 copy-done.6
  6.2 0.0 copy-start.4
  6.2 0.0 copy-start.5
  6.2 0.6 %copy-done.4 = s32[3]{0:T(128)S(1)} copy-done((s32[3]{0:T(128)S(1)}, s32[3]{0:T(128)}, u32[]{:S(2)}) %copy-start.4) | copy-done | bytes 36
  6.8 0.0 copy-done.5
  6.8 0.3 %stage.1 = (s32[1,3]{1,0:T(1,128)S(1)}, f32[1,128]{1,0:T(1,128)S(1)}, bf16[128,384]{1,0:T(8,128)(2,1)S(1)}, f32[2,8,128]{2,1,0:T(8,128)S(1)}, f32[128,384]{1,0:T(8,128)S(1)}, /*index=5*/f32[2,8,256]{2,1,0:T(8,128)S(1)}) custom-call(s32[1,3]{1,0:T(1,128)S(1)} %bitcast.18, f32[1,128]{1,0:T(1,128)S(1)} %bitcast.19, bf16[384,128]{1,0:T(8,128)(2,1)S(1)} %fusion.cots_ref, ...), custom_call_target="tpu_custom_call" | custom-call | tf_op jit(solution)/shard_map/stage/pallas_call | solution.py:243
  7.2 0.0 copy-start.1
  7.2 2.2 %collective-permute-done.1 = bf16[1,384,128]{2,1,0:T(8,128)(2,1)S(1)} collective-permute-done((bf16[1,384,128]{2,1,0:T(8,128)(2,1)S(1)}, bf16[1,384,128]{2,1,0:T(8,128)(2,1)S(1)}, u32[]{:S(2)}, u32[]{:S(2)}) %collective-permute-start.1) | collective-permute-done | bytes 98336 | tf_op jit(solution)/shard_map/ppermute | solution.py:22
  9.4 3.8 %collective-permute-start.2 = (bf16[2,384,128]{2,1,0:T(8,128)(2,1)S(1)}, bf16[2,384,128]{2,1,0:T(8,128)(2,1)S(1)}, u32[]{:S(2)}, u32[]{:S(2)}) collective-permute-start(bf16[2,384,128]{2,1,0:T(8,128)(2,1)S(1)} %get-tuple-element.31.cots_ref), channel_id=1, source_target_pairs={{0,28},{4,0},{8,4},{12,8},{16,12},{20,16},{24,20},{28,24},{1,29},{... | collective-permute-start | bytes 589832 | tf_op jit(solution)/shard_map/ppermute | solution.py:27
  13.2 1.5 %collective-permute-done.before_ref = bf16[384,128]{1,0:T(8,128)(2,1)S(1)} collective-permute-done((bf16[384,128]{1,0:T(8,128)(2,1)S(1)}, bf16[384,128]{1,0:T(8,128)(2,1)S(1)}, u32[]{:S(2)}, u32[]{:S(2)}) %collective-permute-start) | collective-permute-done | bytes 98336 | tf_op jit(solution)/shard_map/ppermute | solution.py:27
  14.7 0.0 copy-done.1
  14.7 1.1 %lags.1.parts_ref = f32[32,1,256]{2,1,0:T(1,128)} custom-call(f32[2,8,128]{2,1,0:T(8,128)S(1)} %get-tuple-element.19.masks_ref, bf16[384,128]{1,0:T(8,128)(2,1)S(1)} %bitcast.13, bf16[384,128]{1,0:T(8,128)(2,1)S(1)} %collective-permute-done.before_ref, bf16[128,384]{1,0:T(8,128)(2,1)S(1)} %get-tuple-element.20.turned_ref, ...), custom_call_target="tpu_custom_call" | custom-call | flops 10000000000 | bytes 1048576 | tf_op jit(solution)/shard_map/lags/pallas_call | solution.py:259
  15.7 2.6 %all-to-all-start = ((f32[32,1,256]{2,1,0:T(1,128)}), f32[32,1,256]{2,1,0:T(1,128)S(1)}, u32[]{:S(2)}, u32[]{:S(2)}) async-start(f32[32,1,256]{2,1,0:T(1,128)} %lags.1.parts_ref), calls=%async_computation | async-start | bytes 65536 | tf_op jit(solution)/shard_map/all_to_all | solution.py:268
  18.3 0.8 %ahead.1 = (bf16[128,1536]{1,0:T(8,128)(2,1)S(1)}, bf16[128,1536]{1,0:T(8,128)(2,1)S(1)}, bf16[1,384,128]{2,1,0:T(8,128)(2,1)S(1)}, bf16[768,128]{1,0:T(8,128)(2,1)S(1)}) custom-call(s32[1,3]{1,0:T(1,128)S(1)} %get-tuple-element.17.lengths_ref, f32[1,1536]{1,0:T(1,128)S(1)} %reshape.30.taps_ref, f32[2,8,128]{2,1,0:T(8,128)S(1)} %get-tuple-element.19.masks_ref, ...), custom_call_target="tpu_custom_call" | custom-call | tf_op jit(solution)/shard_map/ahead/pallas_call | solution.py:272
  19.1 3.6 %collective-permute-start.3 = (bf16[384,128]{1,0:T(8,128)(2,1)S(1)}, bf16[384,128]{1,0:T(8,128)(2,1)S(1)}, u32[]{:S(2)}, u32[]{:S(2)}) collective-permute-start(bf16[384,128]{1,0:T(8,128)(2,1)S(1)} %bitcast.20), channel_id=1, source_target_pairs={{0,8},{4,12},{8,16},{12,20},{16,24},{20,28},{1,9},{5,13},{9,17},{1... | collective-permute-start | bytes 294920 | tf_op jit(solution)/shard_map/ppermute | solution.py:22
  22.7 0.0 collective-permute-done.2
  22.8 1.3 %near.1 = (f32[384,128]{1,0:T(8,128)S(1)}, bf16[384,128]{1,0:T(8,128)(2,1)}, bf16[384,128]{1,0:T(8,128)(2,1)}) custom-call(s32[1,3]{1,0:T(1,128)S(1)} %get-tuple-element.17.lengths_ref, bf16[384,128]{1,0:T(8,128)(2,1)S(1)} %copy-done.2, bf16[384,128]{1,0:T(8,128)(2,1)S(1)} %copy-done.3, f32[1,128]{1,0:T(1,128)S(1)} %get-tuple-element.18.skip_ref, ...), custom_call_target="tpu_custom_call" | custom-call | flops 10000000000 | bytes 1048576 | tf_op jit(solution)/shard_map/near/pallas_call | solution.py:284
  24.1 1.0 %collective-permute-done.3 = bf16[384,128]{1,0:T(8,128)(2,1)S(1)} collective-permute-done((bf16[384,128]{1,0:T(8,128)(2,1)S(1)}, bf16[384,128]{1,0:T(8,128)(2,1)S(1)}, u32[]{:S(2)}, u32[]{:S(2)}) %collective-permute-start.3) | collective-permute-done | bytes 98336 | tf_op jit(solution)/shard_map/ppermute | solution.py:22
  25.1 0.0 copy-start
  25.1 0.4 %all-to-all-done.gathered_ref = f32[32,1,256]{2,1,0:T(1,128)S(1)} async-done(((f32[32,1,256]{2,1,0:T(1,128)}), f32[32,1,256]{2,1,0:T(1,128)S(1)}, u32[]{:S(2)}, u32[]{:S(2)}) %all-to-all-start) | async-done | bytes 32800 | tf_op jit(solution)/shard_map/all_to_all | solution.py:268
  25.5 0.7 %sum.1 = f32[1,192]{1,0:T(1,128)} custom-call(f32[32,1,256]{2,1,0:T(1,128)S(1)} %all-to-all-done.gathered_ref, f32[2,8,256]{2,1,0:T(8,128)S(1)} %get-tuple-element.29.picks_ref, bf16[384,128]{1,0:T(8,128)(2,1)S(1)} %fusion.1.layer_out_ref), custom_call_target="tpu_custom_call" | custom-call | tf_op jit(solution)/shard_map/sum/pallas_call | solution.py:295
  26.2 0.0 copy-done
  (6 shorter events, 0.2 us)
Async XLA Ops:
  0.6 2.3 %copy-start.3 = (bf16[384,128]{1,0:T(8,128)(2,1)S(1)}, bf16[384,128]{1,0:T(8,128)(2,1)}, u32[]{:S(2)}) copy-start(bf16[384,128]{1,0:T(8,128)(2,1)} %gate_in_ref.1) | copy-start | bytes 294916
  0.6 2.3 %copy-start.2 = (bf16[384,128]{1,0:T(8,128)(2,1)S(1)}, bf16[384,128]{1,0:T(8,128)(2,1)}, u32[]{:S(2)}) copy-start(bf16[384,128]{1,0:T(8,128)(2,1)} %value_ref.1) | copy-start | bytes 294916
  1.7 7.7 %collective-permute-start.1 = (bf16[1,384,128]{2,1,0:T(8,128)(2,1)S(1)}, bf16[1,384,128]{2,1,0:T(8,128)(2,1)S(1)}, u32[]{:S(2)}, u32[]{:S(2)}) collective-permute-start(bf16[1,384,128]{2,1,0:T(8,128)(2,1)S(1)} %bitcast.15), channel_id=1, source_target_pairs={{8,0},{12,4},{16,8},{20,12},{24,16},{28,20},{9,1},{13,5},{17,9},{2... | collective-permute-start | bytes 294920 | tf_op jit(solution)/shard_map/ppermute | solution.py:22
  3.0 3.1 %copy-start.6 = (f32[1536]{0:T(1024)S(1)}, f32[1536]{0:T(1024)}, u32[]{:S(2)}) copy-start(f32[1536]{0:T(1024)} %param.11) | copy-start | bytes 18436
  3.2 11.5 %collective-permute-start = (bf16[384,128]{1,0:T(8,128)(2,1)S(1)}, bf16[384,128]{1,0:T(8,128)(2,1)S(1)}, u32[]{:S(2)}, u32[]{:S(2)}) collective-permute-start(bf16[384,128]{1,0:T(8,128)(2,1)S(1)} %bitcast.11), channel_id=1, source_target_pairs={{0,4},{4,8},{8,12},{12,16},{16,20},{20,24},{24,28},{28,0},{1,5},{5... | collective-permute-start | bytes 294920 | tf_op jit(solution)/shard_map/ppermute | solution.py:27
  6.2 0.7 %copy-start.4 = (s32[3]{0:T(128)S(1)}, s32[3]{0:T(128)}, u32[]{:S(2)}) copy-start(s32[3]{0:T(128)} %param.12) | copy-start | bytes 40
  6.2 0.7 %copy-start.5 = (f32[128]{0:T(128)S(1)}, f32[128]{0:T(128)}, u32[]{:S(2)}) copy-start(f32[128]{0:T(128)} %param.10) | copy-start | bytes 1540
  7.2 7.5 %copy-start.1 = (bf16[384,128]{1,0:T(8,128)(2,1)S(1)}, bf16[384,128]{1,0:T(8,128)(2,1)}, u32[]{:S(2)}) copy-start(bf16[384,128]{1,0:T(8,128)(2,1)} %gate_out_ref.1) | copy-start | bytes 294916
  9.4 13.3 %collective-permute-start.2 = (bf16[2,384,128]{2,1,0:T(8,128)(2,1)S(1)}, bf16[2,384,128]{2,1,0:T(8,128)(2,1)S(1)}, u32[]{:S(2)}, u32[]{:S(2)}) collective-permute-start(bf16[2,384,128]{2,1,0:T(8,128)(2,1)S(1)} %get-tuple-element.31.cots_ref), channel_id=1, source_target_pairs={{0,28},{4,0},{8,4},{12,8},{16,12},{20,16},{24,20},{28,24},{1,29},{... | collective-permute-start | bytes 589832 | tf_op jit(solution)/shard_map/ppermute | solution.py:27
  15.7 9.7 %all-to-all-start = ((f32[32,1,256]{2,1,0:T(1,128)}), f32[32,1,256]{2,1,0:T(1,128)S(1)}, u32[]{:S(2)}, u32[]{:S(2)}) async-start(f32[32,1,256]{2,1,0:T(1,128)} %lags.1.parts_ref), calls=%async_computation | async-start | bytes 65536 | tf_op jit(solution)/shard_map/all_to_all | solution.py:268
  19.1 5.9 %collective-permute-start.3 = (bf16[384,128]{1,0:T(8,128)(2,1)S(1)}, bf16[384,128]{1,0:T(8,128)(2,1)S(1)}, u32[]{:S(2)}, u32[]{:S(2)}) collective-permute-start(bf16[384,128]{1,0:T(8,128)(2,1)S(1)} %bitcast.20), channel_id=1, source_target_pairs={{0,8},{4,12},{8,16},{12,20},{16,24},{20,28},{1,9},{5,13},{9,17},{1... | collective-permute-start | bytes 294920 | tf_op jit(solution)/shard_map/ppermute | solution.py:22
  25.1 1.1 %copy-start = (bf16[384,128]{1,0:T(8,128)(2,1)}, bf16[384,128]{1,0:T(8,128)(2,1)S(1)}, u32[]{:S(2)}) copy-start(bf16[384,128]{1,0:T(8,128)(2,1)S(1)} %fusion.1.layer_out_ref) | copy-start | bytes 294916
